TPU v7x, 128 devices: a whole 4x4x4 slice. The times are simulated.
128 devices in a mesh: req: 16 (over y, z), tp: 8 (over x, core).
Axes of the slice: x: 4, y: 4, z: 4, core: 2. Of those that a mesh axis runs over, the one named last changes fastest.
Arguments:
- hidden: bfloat16 [14336, 8192], P('req'), may hold values from -150 to 150
- norm_gain_vector: float32 [8192], replicated, may hold values from 0.1 to 1.9
- query_weight: bfloat16 [8192, 4096], P(None, 'tp'), may hold values from -0.0625 to 0.0625
- adapter_down_weight: bfloat16 [128, 64, 8192], P(('req', 'tp')), may hold values from -0.0625 to 0.0625
- adapter_up_weight: bfloat16 [128, 64, 4096], P(('req', 'tp')), may hold values from -0.75 to 0.75
- block_adapter_ids: int32 [16, 7], replicated, may hold values from 0 to 127, as said below
- adapter_slot_table: int32 [128], replicated, may hold values from 0 to 127, as said below
Outputs:
- query: bfloat16 [14336, 4096], P('req', 'tp')
Inputs may be any that keep to these rules, and one draw needn't show every extreme that they name: `block_adapter_ids`: in every request group the 7 blocks use different adapters, and no two of them have storage slots s, s2 with s // 8 == s2 // 8. `adapter_slot_table`: each storage slot holds exactly one adapter id.
All inputs are finite; a program needn't handle non-finite values.
Results may differ from a plain program's by a relative error of at most 0.0052.
Values may be sent and summed in bfloat16 or wider, within the bound.
No kernel may reach another device: no remote copies, remote signals or barrier semaphores. Data moves between devices by JAX's collectives and lax.ppermute only.
A program may use at most 192 MiB of HBM per device.

v0:
```python
import jax
import jax.numpy as jnp
from jax import lax
from jax.sharding import PartitionSpec as P

ADAPTER_SCALE = 0.5


def shards(
    hidden,
    norm_gain_vector,
    query_weight,
    adapter_down_weight,
    adapter_up_weight,
    block_adapter_ids,
    adapter_slot_table,
):
    row_count, features = hidden.shape
    rank_total = adapter_down_weight.shape[1]
    tp_count = lax.axis_size("tp")
    req_count = lax.axis_size("req")
    part_width = features // tp_count
    part_cols = query_weight.shape[1]
    tp_index = lax.axis_index("tp")
    req_index = lax.axis_index("req")
    wide = hidden.astype(jnp.float32)
    inverse_rms = lax.rsqrt(jnp.mean(wide * wide, axis=-1, keepdims=True) + 1e-05)
    normed = (wide * inverse_rms * norm_gain_vector).astype(jnp.bfloat16)
    base_output = jnp.dot(normed, query_weight, preferred_element_type=jnp.float32)
    matches = (
        block_adapter_ids[:, :, None]
        == jnp.arange(adapter_slot_table.shape[0], dtype=jnp.int32)[None, None, :]
    )
    slot_table = jnp.sum(jnp.where(matches, adapter_slot_table[None, None, :], 0), axis=2)
    block_count = slot_table.shape[1]
    own_slots = lax.dynamic_index_in_dim(slot_table, req_index, 0, keepdims=False)
    down_local = adapter_down_weight[0]
    up_local = adapter_up_weight[0]
    self_slot = req_index * tp_count + tp_index
    wanted = jnp.any(slot_table == self_slot, axis=1).astype(jnp.bfloat16)
    down_parts = jnp.swapaxes(down_local.reshape(rank_total, tp_count, part_width), 0, 1)
    up_parts = jnp.swapaxes(up_local.reshape(rank_total, tp_count, part_cols), 0, 1)
    send_down = (wanted[:, None, None, None] * down_parts[None]).reshape(
        req_count * tp_count, rank_total, part_width
    )
    send_up = (wanted[:, None, None, None] * up_parts[None]).reshape(
        req_count * tp_count, rank_total, part_cols
    )
    recv_down, recv_up = (
        lax.all_to_all(send_down, ("req", "tp"), split_axis=0, concat_axis=0, tiled=True),
        lax.all_to_all(send_up, ("req", "tp"), split_axis=0, concat_axis=0, tiled=True),
    )
    got_down = jnp.take(recv_down, own_slots, axis=0)
    got_up = jnp.take(recv_up, own_slots, axis=0)
    own_features = lax.dynamic_slice_in_dim(normed, tp_index * part_width, part_width, 1)
    block_rows = own_features.reshape(block_count, row_count // block_count, part_width)
    partial_value = jnp.einsum(
        "jrd,jbd->jrb", got_down, block_rows, preferred_element_type=jnp.float32
    )
    shrink = lax.psum(partial_value, "tp").astype(jnp.bfloat16)
    rank_output = jnp.einsum("jrb,jrc->jbc", shrink, got_up, preferred_element_type=jnp.float32)
    rank_output = rank_output.reshape(row_count, part_cols)
    return (base_output + ADAPTER_SCALE * rank_output).astype(jnp.bfloat16)


def solution(mesh):
    return jax.shard_map(
        shards,
        mesh=mesh,
        in_specs=(
            P("req", None),
            P(),
            P(None, "tp"),
            P(("req", "tp"), None, None),
            P(("req", "tp"), None, None),
            P(),
            P(),
        ),
        out_specs=P("req", "tp"),
        check_vma=False,
    )
```

profile of v0, /device:TPU:24, one launch (start us, length us, event | category | flops | bytes accessed | tf_op | source)
XLA Modules:
  0.0 420.1 jit_solution(12147582205902086123)
XLA Ops:
  0.0 0.0 copy-start.1
  0.0 1.1 select_reduce_fusion
  1.1 0.1 mul.76
  1.2 0.1 mul.77
  1.3 1.2 copy.19
  2.5 0.2 copy.17
  2.7 4.0 bitcast_multiply_fusion.1
  6.7 10.7 %all-to-all-start.1 = ((bf16[128,64,512]{2,1,0:T(8,128)(2,1)}), bf16[128,64,512]{2,1,0:T(8,128)(2,1)}, u32[]{:S(2)}, u32[]{:S(2)}) async-start(bf16[128,64,512]{2,1,0:T(8,128)(2,1)} %bitcast_multiply_fusion.1), calls=%async_computation.1 | async-start | bytes 16777216 | tf_op jit(solution)/shard_map/all_to_all | solution.py:51
  17.4 0.0 copy-done.1
  17.4 0.6 copy.18
  18.0 0.6 copy.16
  18.6 6.0 %bitcast_multiply_fusion = bf16[128,64,1024]{2,1,0:T(8,128)(2,1)} fusion(bf16[8,64,1024]{2,1,0:T(8,128)(2,1)S(1)} %copy.16, bf16[128]{0:T(256)(128)(2,1)S(1)} %mul.77), kind=kLoop, calls=%fused_computation.7 | loop fusion | flops 8388608 | bytes 17826048 | tf_op jit(solution)/shard_map/mul | solution.py:43
  24.6 91.2 %all-to-all-done.1 = bf16[128,64,512]{2,1,0:T(8,128)(2,1)} async-done(((bf16[128,64,512]{2,1,0:T(8,128)(2,1)}), bf16[128,64,512]{2,1,0:T(8,128)(2,1)}, u32[]{:S(2)}, u32[]{:S(2)}) %all-to-all-start.1) | async-done | bytes 8388640 | tf_op jit(solution)/shard_map/all_to_all | solution.py:51
  115.8 15.2 %all-to-all-start = ((bf16[128,64,1024]{2,1,0:T(8,128)(2,1)}), bf16[128,64,1024]{2,1,0:T(8,128)(2,1)}, u32[]{:S(2)}, u32[]{:S(2)}) async-start(bf16[128,64,1024]{2,1,0:T(8,128)(2,1)} %bitcast_multiply_fusion), calls=%async_computation | async-start | bytes 33554432 | tf_op jit(solution)/shard_map/all_to_all | solution.py:50
  131.0 0.0 copy-start.2
  131.1 0.2 dynamic-slice_reduce_fusion
  131.3 8.1 %fusion = f32[896]{0:T(1024)S(1)} fusion(bf16[896,8192]{1,0:T(8,128)(2,1)} %param.7), kind=kLoop, calls=%fused_computation.4 | loop fusion | flops 22019200 | bytes 14683648 | tf_op jit(solution)/shard_map/reduce_sum | solution.py:27
  139.4 0.0 copy-done.2
  139.4 8.8 %fusion.2 = bf16[896,8192]{1,0:T(8,128)(2,1)S(1)} fusion(bf16[896,8192]{1,0:T(8,128)(2,1)} %param.7, f32[8192]{0:T(1024)S(1)} %copy-done.2, f32[896]{0:T(1024)S(1)} %add_rsqrt_fusion), kind=kLoop, calls=%fused_computation.6 | loop fusion | flops 29360128 | bytes 29396480 | tf_op jit(solution)/shard_map/convert_element_type | solution.py:28
  148.2 0.0 copy-start
  148.2 5.2 %copy-done = bf16[896,8192]{1,0:T(8,128)(2,1)} copy-done((bf16[896,8192]{1,0:T(8,128)(2,1)}, bf16[896,8192]{1,0:T(8,128)(2,1)S(1)}, u32[]{:S(2)}) %copy-start) | copy-done | bytes 14680088
  153.4 0.2 constant_dynamic-slice_fusion
  153.6 4.0 gather_fusion.1
  157.6 201.4 %all-to-all-done = bf16[128,64,1024]{2,1,0:T(8,128)(2,1)} async-done(((bf16[128,64,1024]{2,1,0:T(8,128)(2,1)}), bf16[128,64,1024]{2,1,0:T(8,128)(2,1)}, u32[]{:S(2)}, u32[]{:S(2)}) %all-to-all-start) | async-done | bytes 16777248 | tf_op jit(solution)/shard_map/all_to_all | solution.py:50
  359.0 6.4 %gather_fusion = bf16[7,64,1024]{2,1,0:T(8,128)(2,1)S(1)} fusion(bf16[128,64,1024]{2,1,0:T(8,128)(2,1)} %all-to-all-done, s32[1024]{0:T(1024)S(1)} %pad_clamp_fusion), kind=kCustom, calls=%fused_computation | custom fusion | bytes 1835036 | tf_op jit(solution)/shard_map/jit(_take)/gather | solution.py:53
  365.3 0.8 fusion.4
  366.1 39.4 %all-reduce.1 = bf16[7,64,128]{2,1,0:T(8,128)(2,1)S(1)} all-reduce(f32[7,64,128]{2,1,0:T(8,128)S(1)} %fusion.4), channel_id=1, replica_groups=mesh['req'=16,'tp'=8] {'tp'}, use_global_device_ids=true, to_apply=%region_3.4 | all-reduce | flops 57344 | bytes 344064 | tf_op jit(solution)/shard_map/psum | solution.py:60
  405.5 0.5 convolution_multiply_fusion
  406.0 14.2 %fusion.3 = bf16[896,512]{1,0:T(8,128)(2,1)} fusion(f32[7,128,512]{2,1,0:T(8,128)S(1)} %convolution_multiply_fusion, bf16[896,8192]{1,0:T(8,128)(2,1)} %copy-done, bf16[8192,512]{1,0:T(8,128)(2,1)} %param.9), kind=kOutput, calls=%fused_computation.10 | convolution fusion | flops 7517110272 | bytes 25821184 | tf_op jit(solution)/shard_map/dot_general | solution.py:29
  (6 shorter events, 0.1 us)
Async XLA Ops:
  0.0 17.4 %copy-start.1 = (bf16[1,64,8192]{2,1,0:T(8,128)(2,1)S(1)}, bf16[1,64,8192]{2,1,0:T(8,128)(2,1)}, u32[]{:S(2)}) copy-start(bf16[1,64,8192]{2,1,0:T(8,128)(2,1)} %param.10) | copy-start | bytes 3145732
  6.7 109.1 %all-to-all-start.1 = ((bf16[128,64,512]{2,1,0:T(8,128)(2,1)}), bf16[128,64,512]{2,1,0:T(8,128)(2,1)}, u32[]{:S(2)}, u32[]{:S(2)}) async-start(bf16[128,64,512]{2,1,0:T(8,128)(2,1)} %bitcast_multiply_fusion.1), calls=%async_computation.1 | async-start | bytes 16777216 | tf_op jit(solution)/shard_map/all_to_all | solution.py:51
  115.8 243.1 %all-to-all-start = ((bf16[128,64,1024]{2,1,0:T(8,128)(2,1)}), bf16[128,64,1024]{2,1,0:T(8,128)(2,1)}, u32[]{:S(2)}, u32[]{:S(2)}) async-start(bf16[128,64,1024]{2,1,0:T(8,128)(2,1)} %bitcast_multiply_fusion), calls=%async_computation | async-start | bytes 33554432 | tf_op jit(solution)/shard_map/all_to_all | solution.py:50
  131.0 8.3 %copy-start.2 = (f32[8192]{0:T(1024)S(1)}, f32[8192]{0:T(1024)}, u32[]{:S(2)}) copy-start(f32[8192]{0:T(1024)} %param.8) | copy-start | bytes 98308
  148.2 5.2 %copy-start = (bf16[896,8192]{1,0:T(8,128)(2,1)}, bf16[896,8192]{1,0:T(8,128)(2,1)S(1)}, u32[]{:S(2)}) copy-start(bf16[896,8192]{1,0:T(8,128)(2,1)S(1)} %fusion.2) | copy-start | bytes 44040196
where the time goes:
time: 421 us; the launch traced here: 420 us
  waiting for transfers between devices  293 us (70%)
  blocking collectives  39.4 us (9%)
  other arithmetic  28 us (7%)
  starting transfers between devices  25.9 us (6%)
  local copies, waits for them, and re-layouts  18.7 us (4%)
  matrix products  15.4 us (4%)
    all_to_all x1, waiting for transfers between devices, shards(): lax.all_to_all(send_down, ('req', 'tp'), split_axis=0, concat_axis=0, til...  201 us
    all_to_all x1, waiting for transfers between devices, shards(): lax.all_to_all(send_up, ('req', 'tp'), split_axis=0, concat_axis=0, tiled...  91.2 us
    psum x1, blocking collectives, shards(): shrink = lax.psum(partial_value, 'tp').astype(jnp.bfloat16)  39.4 us
    all_to_all x1, starting transfers between devices, shards(): lax.all_to_all(send_down, ('req', 'tp'), split_axis=0, concat_axis=0, til...  15.2 us
    dot_general x1, matrix products, shards(): jnp.dot(normed, query_weight, preferred_element_type=jnp.float32)  14.2 us
    all_to_all x1, starting transfers between devices, shards(): lax.all_to_all(send_up, ('req', 'tp'), split_axis=0, concat_axis=0, tiled...  10.7 us
    convert_element_type x1, other arithmetic, shards(): normed = (wide * inverse_rms * norm_gain_vector).astype(jnp.bfloat16)  8.83 us
  transfers between devices with their start and end apart: 2, of which 2 were waited for; matrix products, arithmetic and copies ran while one was open for 7% of the time, Pallas kernels for 0%

commit v1 on v0

v1 whole, which is shorter than its diff:
```python
import functools

import jax
import jax.numpy as jnp
from jax import lax
from jax.experimental import pallas as pl
from jax.experimental.pallas import tpu as pltpu
from jax.sharding import PartitionSpec as P

ADAPTER_SCALE = 0.5
X, CORES = 4, 2
LANES = X * CORES
BOTH = ("req", "tp")


def lane_shift(groups, dx, dc):
    return [
        (g * LANES + x * CORES + c, g * LANES + (x + dx) % X * CORES + (c + dc) % CORES)
        for g in range(groups)
        for x in range(X)
        for c in range(CORES)
    ]


def relative(lane, other):
    dx = (lane // CORES - other // CORES) % X
    dc = (lane % CORES - other % CORES) % CORES
    return dx * CORES + dc


def split_kernel(lane_ref, up_ref, *rest):
    outs, sems = rest[:LANES], rest[LANES]
    lane = lane_ref[0]
    width = outs[0].shape[1]
    copies = []
    for k in range(LANES):
        dx, dc = k // CORES, k % CORES
        to = (lane // CORES + dx) % X * CORES + (lane % CORES + dc) % CORES
        col = pl.multiple_of(to * width, width)
        copies.append(pltpu.make_async_copy(up_ref.at[0, :, pl.ds(col, width)], outs[k], sems.at[k]))
    for copy in copies:
        copy.start()
    for copy in copies:
        copy.wait()


def split_up(lane, up):
    rank, cols = up.shape[1:]
    width = cols // LANES
    any_spec = pl.BlockSpec(memory_space=pl.ANY)
    return pl.pallas_call(
        split_kernel,
        grid_spec=pltpu.PrefetchScalarGridSpec(
            num_scalar_prefetch=1,
            grid=(1,),
            in_specs=[any_spec],
            out_specs=[any_spec] * LANES,
            scratch_shapes=[pltpu.SemaphoreType.DMA((LANES,))],
        ),
        out_shape=[jax.ShapeDtypeStruct((rank, width), up.dtype)] * LANES,
        name="split_up",
    )(lane, up)


def pick_kernel(pick_ref, src_ref, out_ref, sems):
    copies = [
        pltpu.make_async_copy(src_ref.at[pick_ref[g]], out_ref.at[g], sems.at[g])
        for g in range(out_ref.shape[0])
    ]
    for copy in copies:
        copy.start()
    for copy in copies:
        copy.wait()


def pick_down(pick, pieces):
    any_spec = pl.BlockSpec(memory_space=pl.ANY)
    groups = pick.shape[0]
    return pl.pallas_call(
        pick_kernel,
        grid_spec=pltpu.PrefetchScalarGridSpec(
            num_scalar_prefetch=1,
            grid=(1,),
            in_specs=[any_spec],
            out_specs=any_spec,
            scratch_shapes=[pltpu.SemaphoreType.DMA((groups,))],
        ),
        out_shape=jax.ShapeDtypeStruct((groups,) + pieces.shape[1:], pieces.dtype),
        name="pick_down",
    )(pick, pieces)


def pick_many_kernel(pick_ref, *rest):
    srcs, out_ref, sems = rest[:LANES], rest[LANES], rest[LANES + 1]
    groups = out_ref.shape[0]
    for g in range(groups):
        for k in range(LANES):

            @pl.when(pick_ref[g] == k)
            def _():
                pltpu.make_async_copy(srcs[k], out_ref.at[g], sems.at[g]).start()

    for g in range(groups):
        pltpu.make_async_copy(srcs[0], out_ref.at[g], sems.at[g]).wait()


def pick_up(pick, pieces):
    any_spec = pl.BlockSpec(memory_space=pl.ANY)
    groups = pick.shape[0]
    return pl.pallas_call(
        pick_many_kernel,
        grid_spec=pltpu.PrefetchScalarGridSpec(
            num_scalar_prefetch=1,
            grid=(1,),
            in_specs=[any_spec] * LANES,
            out_specs=any_spec,
            scratch_shapes=[pltpu.SemaphoreType.DMA((groups,))],
        ),
        out_shape=jax.ShapeDtypeStruct((groups,) + pieces[0].shape, pieces[0].dtype),
        name="pick_up",
    )(pick, *pieces)


def shrink_kernel(row_ref, down_ref, normed_ref, low_ref):
    low_ref[0] = lax.dot_general(
        down_ref[0], normed_ref[...], (((1,), (1,)), ((), ())), preferred_element_type=jnp.float32
    )


def shrink(owner_rows, down_got, normed, blocks):
    rows, features = normed.shape
    block = rows // blocks
    part = down_got.shape[1]
    return pl.pallas_call(
        shrink_kernel,
        grid_spec=pltpu.PrefetchScalarGridSpec(
            num_scalar_prefetch=1,
            grid=(blocks,),
            in_specs=[
                pl.BlockSpec((1, part, features), lambda j, row: (row[j], 0, 0)),
                pl.BlockSpec((block, features), lambda j, row: (j, 0)),
            ],
            out_specs=pl.BlockSpec((1, part, block), lambda j, row: (j, 0, 0)),
        ),
        out_shape=jax.ShapeDtypeStruct((blocks, part, block), jnp.float32),
        compiler_params=pltpu.CompilerParams(vmem_limit_bytes=32 * 2**20),
        cost_estimate=pl.CostEstimate(
            flops=2 * rows * features * 256, bytes_accessed=2 * rows * features, transcendentals=0
        ),
        name="shrink",
    )(owner_rows, down_got, normed)


def expand_kernel(row_ref, lane_ref, base_ref, low0, low1, low2, low3, up_ref, out_ref, full):
    lows = (low0, low1, low2, low3)
    lane = lane_ref[0]
    part = low0.shape[2]
    for dx in range(X):
        for dc in range(CORES):
            src = (lane // CORES - dx) % X * CORES + (lane % CORES - dc) % CORES
            full[pl.ds(pl.multiple_of(src * part, part), part), :] = lows[dx][dc, 0]
    low = full[...].astype(jnp.bfloat16)
    term = lax.dot_general(low, up_ref[0], (((0,), (0,)), ((), ())), preferred_element_type=jnp.float32)
    out_ref[...] = (base_ref[...] + ADAPTER_SCALE * term).astype(out_ref.dtype)


def expand(owner_rows, lane, base, lows, up_got, blocks):
    rows, cols = base.shape
    block = rows // blocks
    part = lows[0].shape[2]
    rank = up_got.shape[1]
    low_spec = pl.BlockSpec((CORES, 1, part, block), lambda j, row, lane: (0, j, 0, 0))
    return pl.pallas_call(
        expand_kernel,
        grid_spec=pltpu.PrefetchScalarGridSpec(
            num_scalar_prefetch=2,
            grid=(blocks,),
            in_specs=[
                pl.BlockSpec((block, cols), lambda j, row, lane: (j, 0)),
                low_spec,
                low_spec,
                low_spec,
                low_spec,
                pl.BlockSpec((1, rank, cols), lambda j, row, lane: (row[j], 0, 0)),
            ],
            out_specs=pl.BlockSpec((block, cols), lambda j, row, lane: (j, 0)),
            scratch_shapes=[pltpu.VMEM((rank, block), jnp.float32)],
        ),
        out_shape=jax.ShapeDtypeStruct((rows, cols), jnp.bfloat16),
        name="expand",
    )(owner_rows, lane, base, *lows, up_got)


def shards(
    hidden,
    norm_gain_vector,
    query_weight,
    adapter_down_weight,
    adapter_up_weight,
    block_adapter_ids,
    adapter_slot_table,
):
    groups, blocks = block_adapter_ids.shape
    rank, features = adapter_down_weight.shape[1:]
    lane = lax.axis_index("tp")
    group = lax.axis_index("req")
    lane_arr = lane.reshape(1).astype(jnp.int32)

    down_row = lax.all_to_all(
        adapter_down_weight.reshape(LANES, rank // LANES, features), "tp", 0, 0, tiled=True
    )

    matches = block_adapter_ids[:, :, None] == jnp.arange(adapter_slot_table.shape[0], dtype=jnp.int32)
    slots = jnp.sum(jnp.where(matches, adapter_slot_table, 0), axis=2)
    here = slots // LANES == group
    wanted = jnp.sum(jnp.where(here, slots % LANES, 0), axis=1)
    wanted_shift = relative(lane, wanted)
    owner_rows = lax.dynamic_index_in_dim(slots, group, 0, keepdims=False) // LANES

    down_got = lax.all_to_all(pick_down(wanted, down_row), "req", 0, 0, tiled=True)

    up_pieces = split_up(lane_arr, adapter_up_weight)
    up_row = [up_pieces[0]] + [
        lax.ppermute(up_pieces[k], BOTH, lane_shift(groups, k // CORES, k % CORES)) for k in range(1, LANES)
    ]
    up_got = lax.all_to_all(pick_up(wanted_shift, up_row), "req", 0, 0, tiled=True)

    wide = hidden.astype(jnp.float32)
    inverse_rms = lax.rsqrt(jnp.mean(wide * wide, axis=-1, keepdims=True) + 1e-05)
    normed = (wide * inverse_rms * norm_gain_vector).astype(jnp.bfloat16)
    base = jnp.dot(normed, query_weight, preferred_element_type=jnp.float32)

    low = shrink(owner_rows, down_got, normed, blocks)
    other = lax.ppermute(low, BOTH, lane_shift(groups, 0, 1))
    chip = jnp.stack([low, other])
    lows = [chip] + [lax.ppermute(chip, BOTH, lane_shift(groups, dx, 0)) for dx in range(1, X)]
    return expand(owner_rows, lane_arr, base, lows, up_got, blocks)


def solution(mesh):
    return jax.shard_map(
        shards,
        mesh=mesh,
        in_specs=(
            P("req", None),
            P(),
            P(None, "tp"),
            P(("req", "tp"), None, None),
            P(("req", "tp"), None, None),
            P(),
            P(),
        ),
        out_specs=P("req", "tp"),
        check_vma=False,
    )
```

time: 421 us -> 227 us (0.54)
  the two profiles are of different devices: /device:TPU:24 before, /device:TPU:0 now
where the time goes in v1:
time: 227 us; the launch traced here: 225 us
  Pallas kernels  128 us (56%)
  starting transfers between devices  29.8 us (13%)
  other arithmetic  24.8 us (11%)
  waiting for transfers between devices  19 us (8%)
  matrix products  14.3 us (6%)
  local copies, waits for them, and re-layouts  8.61 us (4%)
    pallas_call x1, Pallas kernels, pick_down(): pl.pallas_call(pick_kernel, grid_spec=pltpu.PrefetchScalarGridSpec(num_sc...  65.4 us
    pallas_call x1, Pallas kernels, pick_up(): pl.pallas_call(pick_many_kernel, grid_spec=pltpu.PrefetchScalarGridSpec(n...  33.7 us
    pallas_call x1, Pallas kernels, split_up(): pl.pallas_call(split_kernel, grid_spec=pltpu.PrefetchScalarGridSpec(num_s...  17.1 us
    all_to_all x1, waiting for transfers between devices, shards(): lax.all_to_all(pick_down(wanted, down_row), 'req', 0, 0, tiled=True)  16.2 us
    convert_element_type x1, other arithmetic, shards(): normed = (wide * inverse_rms * norm_gain_vector).astype(jnp.bfloat16)  14.6 us
    dot_general x1, matrix products, shards(): base = jnp.dot(normed, query_weight, preferred_element_type=jnp.float32)  14.3 us
    ppermute x7, starting transfers between devices, shards(): lax.ppermute(up_pieces[k], BOTH, lane_shift(groups, k // CORES, k % CORES))  8.61 us
    unnamed x38, local copies, waits for them, and re-layouts  8.42 us
  transfers between devices with their start and end apart: 14, of which 3 were waited for; matrix products, arithmetic and copies ran while one was open for 18% of the time, Pallas kernels for 54%

profile of v1, /device:TPU:0, one launch (start us, length us, event | category | flops | bytes accessed | tf_op | source)
XLA Modules:
  0.0 224.5 jit_solution(15509078308412089031)
XLA Ops:
  0.0 4.5 %all-to-all-start = ((bf16[8,8,8192]{2,1,0:T(8,128)(2,1)}), bf16[8,8,8192]{2,1,0:T(8,128)(2,1)S(1)}, u32[]{:S(2)}, u32[]{:S(2)}) async-start(bf16[8,8,8192]{2,1,0:T(8,128)(2,1)} %bitcast.7), calls=%async_computation | async-start | bytes 2097152 | tf_op jit(solution)/shard_map/all_to_all | solution.py:209
  4.5 17.1 %split_up.1 = (bf16[64,512]{1,0:T(8,128)(2,1)}, bf16[64,512]{1,0:T(8,128)(2,1)}, bf16[64,512]{1,0:T(8,128)(2,1)}, bf16[64,512]{1,0:T(8,128)(2,1)}, bf16[64,512]{...) custom-call(s32[1]{0:T(128)} %bitcast.lane_ref, ...), custom_call_target="tpu_custom_call" | custom-call | tf_op jit(solution)/shard_map/split_up/pallas_call | solution.py:51
  21.6 0.6 collective-permute-start.4
  22.2 1.7 collective-permute-start.5
  23.8 1.1 collective-permute-start.6
  25.0 1.5 collective-permute-start.7
  26.5 1.8 collective-permute-start.8
  28.3 1.0 select_reduce_fusion
  29.3 0.6 fusion.5.pick_ref
  29.9 0.2 dynamic-slice_reduce_fusion
  30.1 8.1 %fusion = f32[896]{0:T(1024)S(1)} fusion(bf16[896,8192]{1,0:T(8,128)(2,1)} %param.7), kind=kLoop, calls=%fused_computation.2 | loop fusion | flops 22019200 | bytes 14683648 | tf_op jit(solution)/shard_map/reduce_sum | solution.py:229
  38.2 0.0 all-to-all-done.src_ref
  38.2 1.0 copy-done.3
  39.2 65.4 %pick_down.1 = bf16[16,8,8192]{2,1,0:T(8,128)(2,1)} custom-call(s32[16]{0:T(128)} %fusion.5.pick_ref, bf16[8,8,8192]{2,1,0:T(8,128)(2,1)} %copy-done.3), custom_call_target="tpu_custom_call" | custom-call | tf_op jit(solution)/shard_map/pick_down/pallas_call | solution.py:79
  104.7 8.1 %all-to-all-start.1 = ((bf16[16,8,8192]{2,1,0:T(8,128)(2,1)}), bf16[16,8,8192]{2,1,0:T(8,128)(2,1)S(1)}, u32[]{:S(2)}, u32[]{:S(2)}) async-start(bf16[16,8,8192]{2,1,0:T(8,128)(2,1)} %pick_down.1), calls=%async_computation.1 | async-start | bytes 4194304 | tf_op jit(solution)/shard_map/all_to_all | solution.py:220
  112.7 14.6 %fusion.2.normed_ref = bf16[896,8192]{1,0:T(8,128)(2,1)} fusion(bf16[896,8192]{1,0:T(8,128)(2,1)} %param.7, f32[8192]{0:T(1024)S(1)} %copy-done.15, f32[896]{0:T(1024)S(1)} %add_rsqrt_fusion), kind=kLoop, calls=%fused_computation.4 | loop fusion | flops 29360128 | bytes 29396480 | tf_op jit(solution)/shard_map/convert_element_type | solution.py:230
  127.3 16.2 %all-to-all-done.1.down_ref = bf16[16,8,8192]{2,1,0:T(8,128)(2,1)S(1)} async-done(((bf16[16,8,8192]{2,1,0:T(8,128)(2,1)}), bf16[16,8,8192]{2,1,0:T(8,128)(2,1)S(1)}, u32[]{:S(2)}, u32[]{:S(2)}) %all-to-all-start.1) | async-done | bytes 2097184 | tf_op jit(solution)/shard_map/all_to_all | solution.py:220
  143.5 5.2 %copy-done = bf16[896,8192]{1,0:T(8,128)(2,1)S(1)} copy-done((bf16[896,8192]{1,0:T(8,128)(2,1)S(1)}, bf16[896,8192]{1,0:T(8,128)(2,1)}, u32[]{:S(2)}) %copy-start) | copy-done | bytes 14680088
  148.7 5.1 %shrink.1 = f32[7,8,128]{2,1,0:T(8,128)S(1)} custom-call(s32[7]{0:T(128)S(1)} %and_select_fusion.4.row_ref, bf16[16,8,8192]{2,1,0:T(8,128)(2,1)S(1)} %all-to-all-done.1.down_ref, bf16[896,8192]{1,0:T(8,128)(2,1)S(1)} %copy-done), custom_call_target="tpu_custom_call" | custom-call | flops 3758096384 | bytes 14680064 | tf_op jit(solution)/shard_map/shrink/pallas_call | solution.py:134
  153.8 0.0 collective-permute-done.4.rest_1_
  153.8 0.0 copy-done.18
  153.8 1.8 collective-permute-start.9
  155.7 0.0 collective-permute-done.5.rest_2_
  155.7 0.1 collective-permute-start.10
  155.8 0.0 collective-permute-done.6.rest_3_
  155.8 0.4 collective-permute-start
  156.2 0.5 fusion.8.pick_ref
  156.8 0.0 collective-permute-done.7.rest_4_
  156.8 0.0 collective-permute-done.8.rest_5_
  156.8 1.4 collective-permute-done.9.rest_6_
  158.2 1.4 collective-permute-done.10.rest_7_
  159.6 0.6 copy-done.11
  160.2 33.7 %pick_up.1 = bf16[16,64,512]{2,1,0:T(8,128)(2,1)} custom-call(s32[16]{0:T(128)} %fusion.8.pick_ref, bf16[64,512]{1,0:T(8,128)(2,1)} %get-tuple-element.13.rest_0_, bf16[64,512]{1,0:T(8,128)(2,1)} %copy-done.5, bf16[64,512]{1,0:T(8,128)(2,1)} %copy-done.6, bf16[64,512]{1,0:T(8,128)(2,1)} %copy-done.7, bf16[64,512]{1,0:T(8,128)(2,1)} %copy-done.8, ...), custom_call_target="tpu_custom_call" | custom-call | tf_op jit(solution)/shard_map/pick_up/pallas_call | solution.py:110
  193.9 5.0 %all-to-all-start.2 = ((bf16[16,64,512]{2,1,0:T(8,128)(2,1)}), bf16[16,64,512]{2,1,0:T(8,128)(2,1)S(1)}, u32[]{:S(2)}, u32[]{:S(2)}) async-start(bf16[16,64,512]{2,1,0:T(8,128)(2,1)} %pick_up.1), calls=%async_computation.2 | async-start | bytes 2097152 | tf_op jit(solution)/shard_map/all_to_all | solution.py:226
  198.9 0.0 collective-permute-done
  198.9 2.2 collective-permute-start.3
  201.1 0.7 collective-permute-start.2
  201.8 0.3 collective-permute-start.1
  202.1 14.3 %fusion.13.base_ref = f32[896,512]{1,0:T(8,128)} fusion(bf16[896,8192]{1,0:T(8,128)(2,1)} %fusion.2.normed_ref, bf16[8192,512]{1,0:T(8,128)(2,1)} %param.9), kind=kOutput, calls=%fused_computation.41 | convolution fusion | flops 7516192768 | bytes 24903680 | tf_op jit(solution)/shard_map/dot_general | solution.py:231
  216.4 0.0 all-to-all-done.2.up_ref
  216.4 0.0 collective-permute-done.3.low3
  216.4 0.0 collective-permute-done.2.low2
  216.4 0.0 collective-permute-done.1.low1
  216.4 0.9 copy-done.2
  217.4 0.0 copy-done.12
  217.4 0.0 copy-done.13
  217.4 0.6 copy-done.14
  218.0 6.5 %expand.1 = bf16[896,512]{1,0:T(8,128)(2,1)} custom-call(s32[7]{0:T(128)} %copy-done.1, s32[1]{0:T(128)} %bitcast.lane_ref, f32[896,512]{1,0:T(8,128)} %fusion.13.base_ref, f32[2,7,8,128]{3,2,1,0:T(8,128)} %copy-done.4, f32[2,7,8,128]{3,2,1,0:T(8,128)} %copy-done.14, f32[2,7,8,128]{3,2,1,0:T(8,128)} %copy-done.13, f32[2,7,8,128]{3,2,1,0:T(8,128)} %copy-done.12, ...), custom_call_target="tpu_custom_call" | custom-call | tf_op jit(solution)/shard_map/expand/pallas_call | solution.py:173
  (33 shorter events, 0.1 us)
Async XLA Ops:
  0.0 112.7 %copy-start.15 = (f32[8192]{0:T(1024)S(1)}, f32[8192]{0:T(1024)}, u32[]{:S(2)}) copy-start(f32[8192]{0:T(1024)} %param.8) | copy-start | bytes 98308
  0.0 38.2 %all-to-all-start = ((bf16[8,8,8192]{2,1,0:T(8,128)(2,1)}), bf16[8,8,8192]{2,1,0:T(8,128)(2,1)S(1)}, u32[]{:S(2)}, u32[]{:S(2)}) async-start(bf16[8,8,8192]{2,1,0:T(8,128)(2,1)} %bitcast.7), calls=%async_computation | async-start | bytes 2097152 | tf_op jit(solution)/shard_map/all_to_all | solution.py:209
  21.6 132.2 %collective-permute-start.4 = (bf16[64,512]{1,0:T(8,128)(2,1)}, bf16[64,512]{1,0:T(8,128)(2,1)S(1)}, u32[]{:S(2)}, u32[]{:S(2)}) collective-permute-start(bf16[64,512]{1,0:T(8,128)(2,1)} %get-tuple-element.14), channel_id=1, source_target_pairs={{0,1},{1,0},{2,3},{3,2},{4,5},{5,4},{6,7},{7,6},{8,9},{9,8},{10,11... | collective-permute-start | bytes 196616 | tf_op jit(solution)/shard_map/ppermute | solution.py:224
  22.2 133.5 %collective-permute-start.5 = (bf16[64,512]{1,0:T(8,128)(2,1)}, bf16[64,512]{1,0:T(8,128)(2,1)S(1)}, u32[]{:S(2)}, u32[]{:S(2)}) collective-permute-start(bf16[64,512]{1,0:T(8,128)(2,1)} %get-tuple-element.15), channel_id=1, source_target_pairs={{0,2},{1,3},{2,4},{3,5},{4,6},{5,7},{6,0},{7,1},{8,10},{9,11},{10,... | collective-permute-start | bytes 196616 | tf_op jit(solution)/shard_map/ppermute | solution.py:224
  23.8 131.9 %collective-permute-start.6 = (bf16[64,512]{1,0:T(8,128)(2,1)}, bf16[64,512]{1,0:T(8,128)(2,1)S(1)}, u32[]{:S(2)}, u32[]{:S(2)}) collective-permute-start(bf16[64,512]{1,0:T(8,128)(2,1)} %get-tuple-element.16), channel_id=1, source_target_pairs={{0,3},{1,2},{2,5},{3,4},{4,7},{5,6},{6,1},{7,0},{8,11},{9,10},{10,... | collective-permute-start | bytes 196616 | tf_op jit(solution)/shard_map/ppermute | solution.py:224
  25.0 131.8 %collective-permute-start.7 = (bf16[64,512]{1,0:T(8,128)(2,1)}, bf16[64,512]{1,0:T(8,128)(2,1)S(1)}, u32[]{:S(2)}, u32[]{:S(2)}) collective-permute-start(bf16[64,512]{1,0:T(8,128)(2,1)} %get-tuple-element.17), channel_id=1, source_target_pairs={{0,4},{1,5},{2,6},{3,7},{4,0},{5,1},{6,2},{7,3},{8,12},{9,13},{10,... | collective-permute-start | bytes 196616 | tf_op jit(solution)/shard_map/ppermute | solution.py:224
  26.5 130.2 %collective-permute-start.8 = (bf16[64,512]{1,0:T(8,128)(2,1)}, bf16[64,512]{1,0:T(8,128)(2,1)S(1)}, u32[]{:S(2)}, u32[]{:S(2)}) collective-permute-start(bf16[64,512]{1,0:T(8,128)(2,1)} %get-tuple-element.18), channel_id=1, source_target_pairs={{0,5},{1,4},{2,7},{3,6},{4,1},{5,0},{6,3},{7,2},{8,13},{9,12},{10,... | collective-permute-start | bytes 196616 | tf_op jit(solution)/shard_map/ppermute | solution.py:224
  30.1 113.4 %copy-start.1 = (s32[7]{0:T(128)}, s32[7]{0:T(128)S(1)}, u32[]{:S(2)}) copy-start(s32[7]{0:T(128)S(1)} %and_select_fusion.4.row_ref) | copy-start | bytes 88
  38.2 1.0 copy-start.3
  104.7 38.8 %all-to-all-start.1 = ((bf16[16,8,8192]{2,1,0:T(8,128)(2,1)}), bf16[16,8,8192]{2,1,0:T(8,128)(2,1)S(1)}, u32[]{:S(2)}, u32[]{:S(2)}) async-start(bf16[16,8,8192]{2,1,0:T(8,128)(2,1)} %pick_down.1), calls=%async_computation.1 | async-start | bytes 4194304 | tf_op jit(solution)/shard_map/all_to_all | solution.py:220
  143.5 5.2 %copy-start = (bf16[896,8192]{1,0:T(8,128)(2,1)S(1)}, bf16[896,8192]{1,0:T(8,128)(2,1)}, u32[]{:S(2)}) copy-start(bf16[896,8192]{1,0:T(8,128)(2,1)} %fusion.2.normed_ref) | copy-start | bytes 44040196
  148.7 5.2 %copy-start.18 = (bf16[64,512]{1,0:T(8,128)(2,1)S(1)}, bf16[64,512]{1,0:T(8,128)(2,1)}, u32[]{:S(2)}) copy-start(bf16[64,512]{1,0:T(8,128)(2,1)} %get-tuple-element.19) | copy-start | bytes 196612
  148.7 7.0 %copy-start.17 = (bf16[64,512]{1,0:T(8,128)(2,1)S(1)}, bf16[64,512]{1,0:T(8,128)(2,1)}, u32[]{:S(2)}) copy-start(bf16[64,512]{1,0:T(8,128)(2,1)} %get-tuple-element.20) | copy-start | bytes 196612
  148.7 7.6 %copy-start.16 = (s32[16]{0:T(128)S(1)}, s32[16]{0:T(128)}, u32[]{:S(2)}) copy-start(s32[16]{0:T(128)} %fusion.5.pick_ref) | copy-start | bytes 196
  153.8 5.8 %copy-start.5 = (bf16[64,512]{1,0:T(8,128)(2,1)}, bf16[64,512]{1,0:T(8,128)(2,1)S(1)}, u32[]{:S(2)}) copy-start(bf16[64,512]{1,0:T(8,128)(2,1)S(1)} %collective-permute-done.4.rest_1_) | copy-start | bytes 196612
  153.8 4.3 %collective-permute-start.9 = (bf16[64,512]{1,0:T(8,128)(2,1)S(1)}, bf16[64,512]{1,0:T(8,128)(2,1)S(1)}, u32[]{:S(2)}, u32[]{:S(2)}) collective-permute-start(bf16[64,512]{1,0:T(8,128)(2,1)S(1)} %copy-done.18), channel_id=1, source_target_pairs={{0,6},{1,7},{2,0},{3,1},{4,2},{5,3},{6,4},{7,5},{8,14},{9,15},{10,... | collective-permute-start | bytes 196616 | tf_op jit(solution)/shard_map/ppermute | solution.py:224
  155.7 3.9 %copy-start.6 = (bf16[64,512]{1,0:T(8,128)(2,1)}, bf16[64,512]{1,0:T(8,128)(2,1)S(1)}, u32[]{:S(2)}) copy-start(bf16[64,512]{1,0:T(8,128)(2,1)S(1)} %collective-permute-done.5.rest_2_) | copy-start | bytes 196612
  155.7 3.9 %collective-permute-start.10 = (bf16[64,512]{1,0:T(8,128)(2,1)S(1)}, bf16[64,512]{1,0:T(8,128)(2,1)S(1)}, u32[]{:S(2)}, u32[]{:S(2)}) collective-permute-start(bf16[64,512]{1,0:T(8,128)(2,1)S(1)} %copy-done.17), channel_id=1, source_target_pairs={{0,7},{1,6},{2,1},{3,0},{4,3},{5,2},{6,5},{7,4},{8,15},{9,14},{10,... | collective-permute-start | bytes 196616 | tf_op jit(solution)/shard_map/ppermute | solution.py:224
  155.8 3.8 %copy-start.7 = (bf16[64,512]{1,0:T(8,128)(2,1)}, bf16[64,512]{1,0:T(8,128)(2,1)S(1)}, u32[]{:S(2)}) copy-start(bf16[64,512]{1,0:T(8,128)(2,1)S(1)} %collective-permute-done.6.rest_3_) | copy-start | bytes 196612
  155.8 43.1 %collective-permute-start = (f32[7,8,128]{2,1,0:T(8,128)S(1)}, f32[7,8,128]{2,1,0:T(8,128)S(1)}, u32[]{:S(2)}, u32[]{:S(2)}) collective-permute-start(f32[7,8,128]{2,1,0:T(8,128)S(1)} %shrink.1), channel_id=1, source_target_pairs={{0,1},{1,0},{2,3},{3,2},{4,5},{5,4},{6,7},{7,6},{8,9},{9,8},{10,11... | collective-permute-start | bytes 86024 | tf_op jit(solution)/shard_map/ppermute | solution.py:234
  156.8 2.8 %copy-start.8 = (bf16[64,512]{1,0:T(8,128)(2,1)}, bf16[64,512]{1,0:T(8,128)(2,1)S(1)}, u32[]{:S(2)}) copy-start(bf16[64,512]{1,0:T(8,128)(2,1)S(1)} %collective-permute-done.7.rest_4_) | copy-start | bytes 196612
  156.8 2.8 %copy-start.9 = (bf16[64,512]{1,0:T(8,128)(2,1)}, bf16[64,512]{1,0:T(8,128)(2,1)S(1)}, u32[]{:S(2)}) copy-start(bf16[64,512]{1,0:T(8,128)(2,1)S(1)} %collective-permute-done.8.rest_5_) | copy-start | bytes 196612
  158.2 1.4 copy-start.10
  159.6 0.6 copy-start.11
  193.9 22.5 %all-to-all-start.2 = ((bf16[16,64,512]{2,1,0:T(8,128)(2,1)}), bf16[16,64,512]{2,1,0:T(8,128)(2,1)S(1)}, u32[]{:S(2)}, u32[]{:S(2)}) async-start(bf16[16,64,512]{2,1,0:T(8,128)(2,1)} %pick_up.1), calls=%async_computation.2 | async-start | bytes 2097152 | tf_op jit(solution)/shard_map/all_to_all | solution.py:226
  198.9 17.5 %copy-start.4 = (f32[2,7,8,128]{3,2,1,0:T(8,128)}, f32[2,7,8,128]{3,2,1,0:T(8,128)S(1)}, u32[]{:S(2)}) copy-start(f32[2,7,8,128]{3,2,1,0:T(8,128)S(1)} %pad_maximum_fusion.low0) | copy-start | bytes 172036
  198.9 17.5 %collective-permute-start.3 = (f32[2,7,8,128]{3,2,1,0:T(8,128)S(1)}, f32[2,7,8,128]{3,2,1,0:T(8,128)S(1)}, u32[]{:S(2)}, u32[]{:S(2)}) collective-permute-start(f32[2,7,8,128]{3,2,1,0:T(8,128)S(1)} %pad_maximum_fusion.low0), channel_id=1, source_target_pairs={{0,6},{1,7},{2,0},{3,1},{4,2},{5,3},{6,4},{7,5},{8,14},{9,15},{10,... | collective-permute-start | bytes 172040 | tf_op jit(solution)/shard_map/ppermute | solution.py:236
  201.1 15.3 %collective-permute-start.2 = (f32[2,7,8,128]{3,2,1,0:T(8,128)S(1)}, f32[2,7,8,128]{3,2,1,0:T(8,128)S(1)}, u32[]{:S(2)}, u32[]{:S(2)}) collective-permute-start(f32[2,7,8,128]{3,2,1,0:T(8,128)S(1)} %pad_maximum_fusion.low0), channel_id=1, source_target_pairs={{0,4},{1,5},{2,6},{3,7},{4,0},{5,1},{6,2},{7,3},{8,12},{9,13},{10,... | collective-permute-start | bytes 172040 | tf_op jit(solution)/shard_map/ppermute | solution.py:236
  201.8 14.6 %collective-permute-start.1 = (f32[2,7,8,128]{3,2,1,0:T(8,128)S(1)}, f32[2,7,8,128]{3,2,1,0:T(8,128)S(1)}, u32[]{:S(2)}, u32[]{:S(2)}) collective-permute-start(f32[2,7,8,128]{3,2,1,0:T(8,128)S(1)} %pad_maximum_fusion.low0), channel_id=1, source_target_pairs={{0,2},{1,3},{2,4},{3,5},{4,6},{5,7},{6,0},{7,1},{8,10},{9,11},{10,... | collective-permute-start | bytes 172040 | tf_op jit(solution)/shard_map/ppermute | solution.py:236
  216.4 1.0 copy-start.2
  216.4 1.0 copy-start.12
  216.4 1.0 copy-start.13
  217.4 0.6 copy-start.14

commit v2 on v1

--- a/solution.py
+++ b/solution.py
@@ -53,7 +53,7 @@
         grid_spec=pltpu.PrefetchScalarGridSpec(
             num_scalar_prefetch=1,
             grid=(1,),
-            in_specs=[any_spec],
+            in_specs=[pl.BlockSpec(up.shape, lambda i, lane: (0, 0, 0))],
             out_specs=[any_spec] * LANES,
             scratch_shapes=[pltpu.SemaphoreType.DMA((LANES,))],
         ),
@@ -62,63 +62,103 @@
     )(lane, up)
 
 
-def pick_kernel(pick_ref, src_ref, out_ref, sems):
-    copies = [
-        pltpu.make_async_copy(src_ref.at[pick_ref[g]], out_ref.at[g], sems.at[g])
-        for g in range(out_ref.shape[0])
-    ]
-    for copy in copies:
-        copy.start()
-    for copy in copies:
-        copy.wait()
+VMEM = pl.BlockSpec(memory_space=pltpu.VMEM)
+SMEM = pl.BlockSpec(memory_space=pltpu.SMEM)
+
+
+def pick_down_kernel(pick_ref, src_ref, out_ref):
+    for g in range(out_ref.shape[0]):
+        out_ref[g] = src_ref[pick_ref[g]]
 
 
 def pick_down(pick, pieces):
-    any_spec = pl.BlockSpec(memory_space=pl.ANY)
     groups = pick.shape[0]
     return pl.pallas_call(
-        pick_kernel,
-        grid_spec=pltpu.PrefetchScalarGridSpec(
-            num_scalar_prefetch=1,
-            grid=(1,),
-            in_specs=[any_spec],
-            out_specs=any_spec,
-            scratch_shapes=[pltpu.SemaphoreType.DMA((groups,))],
-        ),
+        pick_down_kernel,
+        in_specs=[SMEM, VMEM],
+        out_specs=VMEM,
         out_shape=jax.ShapeDtypeStruct((groups,) + pieces.shape[1:], pieces.dtype),
+        compiler_params=pltpu.CompilerParams(vmem_limit_bytes=16 * 2**20),
         name="pick_down",
     )(pick, pieces)
 
 
-def pick_many_kernel(pick_ref, *rest):
-    srcs, out_ref, sems = rest[:LANES], rest[LANES], rest[LANES + 1]
-    groups = out_ref.shape[0]
-    for g in range(groups):
+def pick_up_kernel(pick_ref, *rest):
+    srcs, out_ref = rest[:LANES], rest[LANES]
+    for g in range(out_ref.shape[0]):
         for k in range(LANES):
 
             @pl.when(pick_ref[g] == k)
             def _():
-                pltpu.make_async_copy(srcs[k], out_ref.at[g], sems.at[g]).start()
-
-    for g in range(groups):
-        pltpu.make_async_copy(srcs[0], out_ref.at[g], sems.at[g]).wait()
+                out_ref[g] = srcs[k][...]
 
 
 def pick_up(pick, pieces):
-    any_spec = pl.BlockSpec(memory_space=pl.ANY)
     groups = pick.shape[0]
     return pl.pallas_call(
-        pick_many_kernel,
-        grid_spec=pltpu.PrefetchScalarGridSpec(
-            num_scalar_prefetch=1,
-            grid=(1,),
-            in_specs=[any_spec] * LANES,
-            out_specs=any_spec,
-            scratch_shapes=[pltpu.SemaphoreType.DMA((groups,))],
-        ),
+        pick_up_kernel,
+        in_specs=[SMEM] + [VMEM] * LANES,
+        out_specs=VMEM,
         out_shape=jax.ShapeDtypeStruct((groups,) + pieces[0].shape, pieces[0].dtype),
+        compiler_params=pltpu.CompilerParams(vmem_limit_bytes=16 * 2**20),
         name="pick_up",
     )(pick, *pieces)
+
+
+CHUNK = 1024
+NORM_ROWS = 128
+
+
+def norm_base_kernel(x_ref, gain_ref, weight_ref, *rest):
+    normed_ref, base_ref = rest[-2:]
+    rows, features = x_ref.shape
+    squares = jnp.zeros((rows, 128), jnp.float32)
+    for p in range(features // 128):
+        wide = x_ref[:, p * 128 : (p + 1) * 128].astype(jnp.float32)
+        squares = squares + wide * wide
+    mean = jnp.sum(squares, axis=1, keepdims=True) / features
+    inverse_rms = lax.rsqrt(mean + 1e-05)
+    total = jnp.zeros(base_ref.shape, jnp.float32)
+    for p in range(features // CHUNK):
+        cols = slice(p * CHUNK, (p + 1) * CHUNK)
+        wide = x_ref[:, cols].astype(jnp.float32)
+        normed = (wide * inverse_rms * gain_ref[:, cols]).astype(jnp.bfloat16)
+        normed_ref[:, cols] = normed
+        total += jnp.dot(normed, weight_ref[cols, :], preferred_element_type=jnp.float32)
+    base_ref[...] = total
+
+
+def norm_base(hidden, gain, weight, first, last, done=None):
+    rows, features = hidden.shape
+    cols = weight.shape[1]
+    count = last - first
+    any_spec = pl.BlockSpec(memory_space=pl.ANY)
+    return pl.pallas_call(
+        norm_base_kernel,
+        grid=(count,),
+        in_specs=[
+            pl.BlockSpec((NORM_ROWS, features), lambda i: (i + first, 0)),
+            pl.BlockSpec((1, features), lambda i: (0, 0)),
+            pl.BlockSpec((features, cols), lambda i: (0, 0), pipeline_mode=pl.Buffered(1)),
+        ]
+        + ([] if done is None else [any_spec, any_spec]),
+        out_specs=[
+            pl.BlockSpec((NORM_ROWS, features), lambda i: (i + first, 0)),
+            pl.BlockSpec((NORM_ROWS, cols), lambda i: (i + first, 0)),
+        ],
+        out_shape=[
+            jax.ShapeDtypeStruct((rows, features), jnp.bfloat16),
+            jax.ShapeDtypeStruct((rows, cols), jnp.float32),
+        ],
+        input_output_aliases={} if done is None else {3: 0, 4: 1},
+        compiler_params=pltpu.CompilerParams(vmem_limit_bytes=56 * 2**20),
+        cost_estimate=pl.CostEstimate(
+            flops=4 * NORM_ROWS * count * features * cols,
+            bytes_accessed=4 * NORM_ROWS * count * features + 2 * features * cols,
+            transcendentals=NORM_ROWS * count,
+        ),
+        name="norm_base",
+    )(hidden, gain.reshape(1, features), weight, *(done or ()))
 
 
 def shrink_kernel(row_ref, down_ref, normed_ref, low_ref):
@@ -143,7 +183,7 @@
             out_specs=pl.BlockSpec((1, part, block), lambda j, row: (j, 0, 0)),
         ),
         out_shape=jax.ShapeDtypeStruct((blocks, part, block), jnp.float32),
-        compiler_params=pltpu.CompilerParams(vmem_limit_bytes=32 * 2**20),
+        compiler_params=pltpu.CompilerParams(vmem_limit_bytes=56 * 2**20),
         cost_estimate=pl.CostEstimate(
             flops=2 * rows * features * 256, bytes_accessed=2 * rows * features, transcendentals=0
         ),
@@ -154,39 +194,41 @@
 def expand_kernel(row_ref, lane_ref, base_ref, low0, low1, low2, low3, up_ref, out_ref, full):
     lows = (low0, low1, low2, low3)
     lane = lane_ref[0]
-    part = low0.shape[2]
+    blocks, part, block = low0.shape[1:]
     for dx in range(X):
         for dc in range(CORES):
             src = (lane // CORES - dx) % X * CORES + (lane % CORES - dc) % CORES
-            full[pl.ds(pl.multiple_of(src * part, part), part), :] = lows[dx][dc, 0]
-    low = full[...].astype(jnp.bfloat16)
-    term = lax.dot_general(low, up_ref[0], (((0,), (0,)), ((), ())), preferred_element_type=jnp.float32)
-    out_ref[...] = (base_ref[...] + ADAPTER_SCALE * term).astype(out_ref.dtype)
+            rows = pl.ds(pl.multiple_of(src * part, part), part)
+            for j in range(blocks):
+                full[j, rows, :] = lows[dx][dc, j]
+    for j in range(blocks):
+        low = full[j].astype(jnp.bfloat16)
+        term = lax.dot_general(
+            low, up_ref[row_ref[j]], (((0,), (0,)), ((), ())), preferred_element_type=jnp.float32
+        )
+        rows = slice(j * block, (j + 1) * block)
+        out_ref[rows, :] = (base_ref[rows, :] + ADAPTER_SCALE * term).astype(out_ref.dtype)
 
 
 def expand(owner_rows, lane, base, lows, up_got, blocks):
     rows, cols = base.shape
-    block = rows // blocks
     part = lows[0].shape[2]
     rank = up_got.shape[1]
-    low_spec = pl.BlockSpec((CORES, 1, part, block), lambda j, row, lane: (0, j, 0, 0))
+
+    def whole(shape):
+        return pl.BlockSpec(shape, lambda i, row, lane: (0,) * len(shape))
+
     return pl.pallas_call(
         expand_kernel,
         grid_spec=pltpu.PrefetchScalarGridSpec(
             num_scalar_prefetch=2,
-            grid=(blocks,),
-            in_specs=[
-                pl.BlockSpec((block, cols), lambda j, row, lane: (j, 0)),
-                low_spec,
-                low_spec,
-                low_spec,
-                low_spec,
-                pl.BlockSpec((1, rank, cols), lambda j, row, lane: (row[j], 0, 0)),
-            ],
-            out_specs=pl.BlockSpec((block, cols), lambda j, row, lane: (j, 0)),
-            scratch_shapes=[pltpu.VMEM((rank, block), jnp.float32)],
+            grid=(1,),
+            in_specs=[whole(base.shape)] + [whole(low.shape) for low in lows] + [whole(up_got.shape)],
+            out_specs=whole(base.shape),
+            scratch_shapes=[pltpu.VMEM((blocks, rank, rows // blocks), jnp.float32)],
         ),
         out_shape=jax.ShapeDtypeStruct((rows, cols), jnp.bfloat16),
+        compiler_params=pltpu.CompilerParams(vmem_limit_bytes=24 * 2**20),
         name="expand",
     )(owner_rows, lane, base, *lows, up_got)
 
@@ -217,18 +259,24 @@
     wanted_shift = relative(lane, wanted)
     owner_rows = lax.dynamic_index_in_dim(slots, group, 0, keepdims=False) // LANES
 
-    down_got = lax.all_to_all(pick_down(wanted, down_row), "req", 0, 0, tiled=True)
-
     up_pieces = split_up(lane_arr, adapter_up_weight)
+
+    steps = hidden.shape[0] // NORM_ROWS
+    cut = steps * 4 // 7
+    done = norm_base(hidden, norm_gain_vector, query_weight, 0, cut)
+    down_row, wanted, done, up_pieces = lax.optimization_barrier((down_row, wanted, done, up_pieces))
+
+    down_send, done = lax.optimization_barrier((pick_down(wanted, down_row), done))
+    down_got = lax.all_to_all(down_send, "req", 0, 0, tiled=True)
+
     up_row = [up_pieces[0]] + [
         lax.ppermute(up_pieces[k], BOTH, lane_shift(groups, k // CORES, k % CORES)) for k in range(1, LANES)
     ]
-    up_got = lax.all_to_all(pick_up(wanted_shift, up_row), "req", 0, 0, tiled=True)
-
-    wide = hidden.astype(jnp.float32)
-    inverse_rms = lax.rsqrt(jnp.mean(wide * wide, axis=-1, keepdims=True) + 1e-05)
-    normed = (wide * inverse_rms * norm_gain_vector).astype(jnp.bfloat16)
-    base = jnp.dot(normed, query_weight, preferred_element_type=jnp.float32)
+    normed, base = norm_base(hidden, norm_gain_vector, query_weight, cut, steps, done)
+    down_got, up_send, normed, base = lax.optimization_barrier(
+        (down_got, pick_up(wanted_shift, up_row), normed, base)
+    )
+    up_got = lax.all_to_all(up_send, "req", 0, 0, tiled=True)
 
     low = shrink(owner_rows, down_got, normed, blocks)
     other = lax.ppermute(low, BOTH, lane_shift(groups, 0, 1))

time: 227 us -> 91.7 us (0.40)
  Pallas kernels: 128 us -> 41.2 us
  other arithmetic: 24.8 us -> 2.34 us
  matrix products: 14.3 us -> 0 us
  local copies, waits for them, and re-layouts: 8.61 us -> 1.54 us
  waiting for transfers between devices: 19 us -> 15.3 us
    pallas_call x2 -> x4, Pallas kernels: 99.1 us -> 26.7 us  [the longest x2 22.1 us: norm_base(): pl.pallas_call(norm_base_kernel, grid=(count,), in_specs=[pl.BlockSpec((N...]
    pallas_call x1, Pallas kernels: 17.1 us -> 1.88 us  [split_up(): pl.pallas_call(split_kernel, grid_spec=pltpu.PrefetchScalarGridSpec(num_s...]
    convert_element_type x1 -> x0, other arithmetic: 14.6 us -> none  [shards(): normed = (wide * inverse_rms * norm_gain_vector).astype(jnp.bfloat16)]
    dot_general x1 -> x0, matrix products: 14.3 us -> none  [shards(): base = jnp.dot(normed, query_weight, preferred_element_type=jnp.float32)]
    reduce_sum x1 -> x0, other arithmetic: 8.1 us -> none  [shards(): jnp.mean(wide * wide, axis=-1, keepdims=True) + 1e-05]
    all_to_all x2, waiting for transfers between devices: 16.2 us -> 8.94 us  [the longest x1 8.94 us: shards(): down_got = lax.all_to_all(down_send, 'req', 0, 0, tiled=True)]
    unnamed x38 -> x22, local copies, waits for them, and re-layouts: 8.42 us -> 1.35 us
    pallas_call x1, Pallas kernels: 5.14 us -> 10.7 us  [shrink(): pl.pallas_call(shrink_kernel, grid_spec=pltpu.PrefetchScalarGridSpec(num_...]
  transfers between devices with their start and end apart: 14 -> 14, of which waited for: 3 -> 4; matrix products, arithmetic and copies ran while one was open for 18% -> 3% of each run, Pallas kernels for 54% -> 41%
where the time goes in v2:
time: 91.7 us; the launch traced here: 90.9 us
  Pallas kernels  41.2 us (45%)
  starting transfers between devices  30.2 us (33%)
  waiting for transfers between devices  15.3 us (17%)
  other arithmetic  2.34 us (3%)
  local copies, waits for them, and re-layouts  1.54 us (2%)
    pallas_call x2, Pallas kernels, norm_base(): pl.pallas_call(norm_base_kernel, grid=(count,), in_specs=[pl.BlockSpec((N...  22.1 us
    pallas_call x1, Pallas kernels, shrink(): pl.pallas_call(shrink_kernel, grid_spec=pltpu.PrefetchScalarGridSpec(num_...  10.7 us
    all_to_all x1, waiting for transfers between devices, shards(): down_got = lax.all_to_all(down_send, 'req', 0, 0, tiled=True)  8.94 us
    ppermute x7, starting transfers between devices, shards(): lax.ppermute(up_pieces[k], BOTH, lane_shift(groups, k // CORES, k % CORES))  8.22 us
    all_to_all x1, starting transfers between devices, shards(): down_got = lax.all_to_all(down_send, 'req', 0, 0, tiled=True)  8.05 us
    ppermute x3, starting transfers between devices, shards(): lax.ppermute(chip, BOTH, lane_shift(groups, dx, 0))  5.75 us
    all_to_all x1, starting transfers between devices, shards(): lax.all_to_all(adapter_down_weight.reshape(LANES, rank // LANES, features...  4.38 us
    ppermute x3, waiting for transfers between devices, shards(): lax.ppermute(chip, BOTH, lane_shift(groups, dx, 0))  4 us
  transfers between devices with their start and end apart: 14, of which 4 were waited for; matrix products, arithmetic and copies ran while one was open for 3% of the time, Pallas kernels for 41%

profile of v2, /device:TPU:0, one launch (start us, length us, event | category | flops | bytes accessed | tf_op | source)
XLA Modules:
  0.0 90.9 jit_solution(4926674796327664216)
XLA Ops:
  0.0 4.4 %all-to-all-start = ((bf16[8,8,8192]{2,1,0:T(8,128)(2,1)}), bf16[8,8,8192]{2,1,0:T(8,128)(2,1)S(1)}, u32[]{:S(2)}, u32[]{:S(2)}) async-start(bf16[8,8,8192]{2,1,0:T(8,128)(2,1)} %bitcast.5), calls=%async_computation | async-start | bytes 2097152 | tf_op jit(solution)/shard_map/all_to_all | solution.py:251
  4.4 1.9 %split_up.1 = (bf16[64,512]{1,0:T(8,128)(2,1)}, bf16[64,512]{1,0:T(8,128)(2,1)}, bf16[64,512]{1,0:T(8,128)(2,1)}, bf16[64,512]{1,0:T(8,128)(2,1)}, bf16[64,512]{...) custom-call(s32[1]{0:T(128)} %bitcast.lane_ref, ...), custom_call_target="tpu_custom_call" | custom-call | tf_op jit(solution)/shard_map/split_up/pallas_call | solution.py:51
  6.3 1.0 %select_reduce_fusion = s32[16,7]{0,1:T(8,128)S(1)} fusion(s32[128]{0:T(128)} %param.13, s32[16,7]{0,1:T(8,128)} %param.12), kind=kLoop, calls=%fused_computation.1 | loop fusion | flops 42896 | bytes 1408 | tf_op jit(solution)/shard_map/reduce_sum | solution.py:256
  7.3 0.0 copy-start.9
  7.3 0.0 copy-start.8
  7.3 0.0 copy-start.7
  7.3 0.0 copy-start.6
  7.3 0.0 copy-start.5
  7.3 0.0 copy-start.4
  7.4 12.0 %norm_base.2 = (bf16[896,8192]{1,0:T(8,128)(2,1)}, f32[896,512]{1,0:T(8,128)}) custom-call(bf16[896,8192]{1,0:T(8,128)(2,1)} %x_ref.3, f32[1,8192]{1,0:T(1,128)} %bitcast.7, bf16[8192,512]{1,0:T(8,128)(2,1)} %weight_ref.3), custom_call_target="tpu_custom_call" | custom-call | flops 8589934592 | bytes 25165824 | tf_op jit(solution)/shard_map/norm_base/pallas_call | solution.py:136
  19.4 1.0 %all-to-all-done.src_ref = bf16[8,8,8192]{2,1,0:T(8,128)(2,1)S(1)} async-done(((bf16[8,8,8192]{2,1,0:T(8,128)(2,1)}), bf16[8,8,8192]{2,1,0:T(8,128)(2,1)S(1)}, u32[]{:S(2)}, u32[]{:S(2)}) %all-to-all-start) | async-done | bytes 1048608 | tf_op jit(solution)/shard_map/all_to_all | solution.py:251
  20.4 2.0 %pick_down.1 = bf16[16,8,8192]{2,1,0:T(8,128)(2,1)} custom-call(s32[16]{0:T(128)S(1)} %fusion.2.pick_ref, bf16[8,8,8192]{2,1,0:T(8,128)(2,1)S(1)} %all-to-all-done.src_ref), custom_call_target="tpu_custom_call" | custom-call | tf_op jit(solution)/shard_map/pick_down/pallas_call | solution.py:76
  22.3 8.0 %all-to-all-start.1 = ((bf16[16,8,8192]{2,1,0:T(8,128)(2,1)}), bf16[16,8,8192]{2,1,0:T(8,128)(2,1)S(1)}, u32[]{:S(2)}, u32[]{:S(2)}) async-start(bf16[16,8,8192]{2,1,0:T(8,128)(2,1)} %pick_down.1), calls=%async_computation.1 | async-start | bytes 4194304 | tf_op jit(solution)/shard_map/all_to_all | solution.py:270
  30.4 0.0 copy-done.10
  30.4 0.1 collective-permute-start
  30.5 1.1 %collective-permute-start.1 = (bf16[64,512]{1,0:T(8,128)(2,1)S(1)}, bf16[64,512]{1,0:T(8,128)(2,1)S(1)}, u32[]{:S(2)}, u32[]{:S(2)}) collective-permute-start(bf16[64,512]{1,0:T(8,128)(2,1)S(1)} %copy-done.9), channel_id=1, source_target_pairs={{0,2},{1,3},{2,4},{3,5},{4,6},{5,7},{6,0},{7,1},{8,10},{9,11},{10,... | collective-permute-start | bytes 196616 | tf_op jit(solution)/shard_map/ppermute | solution.py:273
  31.7 0.0 copy-start.1
  31.7 1.3 %collective-permute-start.2 = (bf16[64,512]{1,0:T(8,128)(2,1)S(1)}, bf16[64,512]{1,0:T(8,128)(2,1)S(1)}, u32[]{:S(2)}, u32[]{:S(2)}) collective-permute-start(bf16[64,512]{1,0:T(8,128)(2,1)S(1)} %copy-done.8), channel_id=1, source_target_pairs={{0,3},{1,2},{2,5},{3,4},{4,7},{5,6},{6,1},{7,0},{8,11},{9,10},{10,... | collective-permute-start | bytes 196616 | tf_op jit(solution)/shard_map/ppermute | solution.py:273
  33.0 2.2 %collective-permute-start.3 = (bf16[64,512]{1,0:T(8,128)(2,1)S(1)}, bf16[64,512]{1,0:T(8,128)(2,1)S(1)}, u32[]{:S(2)}, u32[]{:S(2)}) collective-permute-start(bf16[64,512]{1,0:T(8,128)(2,1)S(1)} %copy-done.7), channel_id=1, source_target_pairs={{0,4},{1,5},{2,6},{3,7},{4,0},{5,1},{6,2},{7,3},{8,12},{9,13},{10,... | collective-permute-start | bytes 196616 | tf_op jit(solution)/shard_map/ppermute | solution.py:273
  35.2 1.0 %collective-permute-start.4 = (bf16[64,512]{1,0:T(8,128)(2,1)S(1)}, bf16[64,512]{1,0:T(8,128)(2,1)S(1)}, u32[]{:S(2)}, u32[]{:S(2)}) collective-permute-start(bf16[64,512]{1,0:T(8,128)(2,1)S(1)} %copy-done.6), channel_id=1, source_target_pairs={{0,5},{1,4},{2,7},{3,6},{4,1},{5,0},{6,3},{7,2},{8,13},{9,12},{10,... | collective-permute-start | bytes 196616 | tf_op jit(solution)/shard_map/ppermute | solution.py:273
  36.2 0.0 collective-permute-done.rest_1_
  36.2 1.8 %collective-permute-start.5 = (bf16[64,512]{1,0:T(8,128)(2,1)S(1)}, bf16[64,512]{1,0:T(8,128)(2,1)S(1)}, u32[]{:S(2)}, u32[]{:S(2)}) collective-permute-start(bf16[64,512]{1,0:T(8,128)(2,1)S(1)} %copy-done.5), channel_id=1, source_target_pairs={{0,6},{1,7},{2,0},{3,1},{4,2},{5,3},{6,4},{7,5},{8,14},{9,15},{10,... | collective-permute-start | bytes 196616 | tf_op jit(solution)/shard_map/ppermute | solution.py:273
  38.0 0.0 collective-permute-done.1.rest_2_
  38.0 0.7 collective-permute-start.6
  38.7 10.1 %norm_base.3 = (bf16[896,8192]{1,0:T(8,128)(2,1)}, f32[896,512]{1,0:T(8,128)}) custom-call(bf16[896,8192]{1,0:T(8,128)(2,1)} %x_ref.3, f32[1,8192]{1,0:T(1,128)} %bitcast.8, bf16[8192,512]{1,0:T(8,128)(2,1)} %weight_ref.3, bf16[896,8192]{1,0:T(8,128)(2,1)} %get-tuple-element.59.rest_0_, ...), custom_call_target="tpu_custom_call", output_to_operand_aliasing={{0}: (3, {}), {1}: (4, {})} | custom-call | flops 6442450944 | bytes 20971520 | tf_op jit(solution)/shard_map/norm_base/pallas_call | solution.py:136
  48.8 0.0 collective-permute-done.2.rest_3_
  48.8 0.0 collective-permute-done.3.rest_4_
  48.8 0.0 collective-permute-done.4.rest_5_
  48.8 0.0 collective-permute-done.5.rest_6_
  48.8 0.0 collective-permute-done.6.rest_7_
  48.9 2.6 %pick_up.1 = bf16[16,64,512]{2,1,0:T(8,128)(2,1)} custom-call(s32[16]{0:T(128)S(1)} %fusion.5.pick_ref, bf16[64,512]{1,0:T(8,128)(2,1)S(1)} %copy-done.1, bf16[64,512]{1,0:T(8,128)(2,1)S(1)} %collective-permute-done.rest_1_, bf16[64,512]{1,0:T(8,128)(2,1)S(1)} %collective-permute-done.1.rest_2_, bf16[64,512]{1,0:T(8,128)(2,1)S(1)} %collective-permute-done.2.rest_3_, ...), custom_call_target="tpu_custom_call" | custom-call | tf_op jit(solution)/shard_map/pick_up/pallas_call | solution.py:98
  51.4 8.9 %all-to-all-done.1.down_ref = bf16[16,8,8192]{2,1,0:T(8,128)(2,1)S(1)} async-done(((bf16[16,8,8192]{2,1,0:T(8,128)(2,1)}), bf16[16,8,8192]{2,1,0:T(8,128)(2,1)S(1)}, u32[]{:S(2)}, u32[]{:S(2)}) %all-to-all-start.1) | async-done | bytes 2097184 | tf_op jit(solution)/shard_map/all_to_all | solution.py:270
  60.4 1.3 %copy-done.3 = bf16[16,8,8192]{2,1,0:T(8,128)(2,1)} copy-done((bf16[16,8,8192]{2,1,0:T(8,128)(2,1)}, bf16[16,8,8192]{2,1,0:T(8,128)(2,1)S(1)}, u32[]{:S(2)}) %copy-start.3) | copy-done | bytes 2097176
  61.7 3.8 %all-to-all-start.2 = ((bf16[16,64,512]{2,1,0:T(8,128)(2,1)}), bf16[16,64,512]{2,1,0:T(8,128)(2,1)S(1)}, u32[]{:S(2)}, u32[]{:S(2)}) async-start(bf16[16,64,512]{2,1,0:T(8,128)(2,1)} %pick_up.1), calls=%async_computation.2 | async-start | bytes 2097152 | tf_op jit(solution)/shard_map/all_to_all | solution.py:279
  65.5 0.2 dynamic-slice_reduce_fusion
  65.7 0.6 and_select_fusion.4.row_ref
  66.3 10.7 %shrink.1 = f32[7,8,128]{2,1,0:T(8,128)} custom-call(s32[7]{0:T(128)} %and_select_fusion.4.row_ref, bf16[16,8,8192]{2,1,0:T(8,128)(2,1)} %copy-done.3, bf16[896,8192]{1,0:T(8,128)(2,1)} %get-tuple-element.65.normed_ref), custom_call_target="tpu_custom_call" | custom-call | flops 3758096384 | bytes 14680064 | tf_op jit(solution)/shard_map/shrink/pallas_call | solution.py:174
  77.0 0.0 collective-permute-start.7
  77.0 1.4 %collective-permute-done.7 = f32[7,8,128]{2,1,0:T(8,128)S(1)} collective-permute-done((f32[7,8,128]{2,1,0:T(8,128)}, f32[7,8,128]{2,1,0:T(8,128)S(1)}, u32[]{:S(2)}, u32[]{:S(2)}) %collective-permute-start.7) | collective-permute-done | bytes 28704 | tf_op jit(solution)/shard_map/ppermute | solution.py:282
  78.4 0.8 pad_maximum_fusion.low0
  79.2 3.5 %collective-permute-start.10 = (f32[2,7,8,128]{3,2,1,0:T(8,128)S(1)}, f32[2,7,8,128]{3,2,1,0:T(8,128)S(1)}, u32[]{:S(2)}, u32[]{:S(2)}) collective-permute-start(f32[2,7,8,128]{3,2,1,0:T(8,128)S(1)} %pad_maximum_fusion.low0), channel_id=1, source_target_pairs={{0,6},{1,7},{2,0},{3,1},{4,2},{5,3},{6,4},{7,5},{8,14},{9,15},{10,... | collective-permute-start | bytes 172040 | tf_op jit(solution)/shard_map/ppermute | solution.py:284
  82.7 0.0 collective-permute-start.8
  82.7 2.2 %collective-permute-start.9 = (f32[2,7,8,128]{3,2,1,0:T(8,128)S(1)}, f32[2,7,8,128]{3,2,1,0:T(8,128)S(1)}, u32[]{:S(2)}, u32[]{:S(2)}) collective-permute-start(f32[2,7,8,128]{3,2,1,0:T(8,128)S(1)} %pad_maximum_fusion.low0), channel_id=1, source_target_pairs={{0,4},{1,5},{2,6},{3,7},{4,0},{5,1},{6,2},{7,3},{8,12},{9,13},{10,... | collective-permute-start | bytes 172040 | tf_op jit(solution)/shard_map/ppermute | solution.py:284
  84.9 0.0 collective-permute-done.10.low3
  84.9 4.0 %collective-permute-done.8.low1 = f32[2,7,8,128]{3,2,1,0:T(8,128)S(1)} collective-permute-done((f32[2,7,8,128]{3,2,1,0:T(8,128)S(1)}, f32[2,7,8,128]{3,2,1,0:T(8,128)S(1)}, u32[]{:S(2)}, u32[]{:S(2)}) %collective-permute-start.8) | collective-permute-done | bytes 57376 | tf_op jit(solution)/shard_map/ppermute | solution.py:284
  88.9 0.0 collective-permute-done.9.low2
  88.9 0.0 all-to-all-done.2.up_ref
  88.9 1.9 %expand.1 = bf16[896,512]{1,0:T(8,128)(2,1)} custom-call(s32[7]{0:T(128)S(1)} %copy-done.2, s32[1]{0:T(128)} %bitcast.lane_ref, f32[896,512]{1,0:T(8,128)S(1)} %copy-done, f32[2,7,8,128]{3,2,1,0:T(8,128)S(1)} %pad_maximum_fusion.low0, f32[2,7,8,128]{3,2,1,0:T(8,128)S(1)} %collective-permute-done.8.low1, f32[2,7,8,128]{3,2,1,0:T(8,128)S(1)} %collective-permute-done.9.low2, ...), custom_call_target="tpu_custom_call" | custom-call | tf_op jit(solution)/shard_map/expand/pallas_call | solution.py:221
  (15 shorter events, 0.1 us)
Async XLA Ops:
  0.0 20.4 %all-to-all-start = ((bf16[8,8,8192]{2,1,0:T(8,128)(2,1)}), bf16[8,8,8192]{2,1,0:T(8,128)(2,1)S(1)}, u32[]{:S(2)}, u32[]{:S(2)}) async-start(bf16[8,8,8192]{2,1,0:T(8,128)(2,1)} %bitcast.5), calls=%async_computation | async-start | bytes 2097152 | tf_op jit(solution)/shard_map/all_to_all | solution.py:251
  7.3 23.1 %copy-start.10 = (bf16[64,512]{1,0:T(8,128)(2,1)S(1)}, bf16[64,512]{1,0:T(8,128)(2,1)}, u32[]{:S(2)}) copy-start(bf16[64,512]{1,0:T(8,128)(2,1)} %get-tuple-element.52) | copy-start | bytes 196612
  7.3 23.2 %copy-start.9 = (bf16[64,512]{1,0:T(8,128)(2,1)S(1)}, bf16[64,512]{1,0:T(8,128)(2,1)}, u32[]{:S(2)}) copy-start(bf16[64,512]{1,0:T(8,128)(2,1)} %get-tuple-element.53) | copy-start | bytes 196612
  7.3 24.4 %copy-start.8 = (bf16[64,512]{1,0:T(8,128)(2,1)S(1)}, bf16[64,512]{1,0:T(8,128)(2,1)}, u32[]{:S(2)}) copy-start(bf16[64,512]{1,0:T(8,128)(2,1)} %get-tuple-element.54) | copy-start | bytes 196612
  7.3 25.7 %copy-start.7 = (bf16[64,512]{1,0:T(8,128)(2,1)S(1)}, bf16[64,512]{1,0:T(8,128)(2,1)}, u32[]{:S(2)}) copy-start(bf16[64,512]{1,0:T(8,128)(2,1)} %get-tuple-element.55) | copy-start | bytes 196612
  7.3 27.8 %copy-start.6 = (bf16[64,512]{1,0:T(8,128)(2,1)S(1)}, bf16[64,512]{1,0:T(8,128)(2,1)}, u32[]{:S(2)}) copy-start(bf16[64,512]{1,0:T(8,128)(2,1)} %get-tuple-element.56) | copy-start | bytes 196612
  7.3 28.9 %copy-start.5 = (bf16[64,512]{1,0:T(8,128)(2,1)S(1)}, bf16[64,512]{1,0:T(8,128)(2,1)}, u32[]{:S(2)}) copy-start(bf16[64,512]{1,0:T(8,128)(2,1)} %get-tuple-element.57) | copy-start | bytes 196612
  7.3 30.6 %copy-start.4 = (bf16[64,512]{1,0:T(8,128)(2,1)S(1)}, bf16[64,512]{1,0:T(8,128)(2,1)}, u32[]{:S(2)}) copy-start(bf16[64,512]{1,0:T(8,128)(2,1)} %get-tuple-element.58) | copy-start | bytes 196612
  22.3 38.0 %all-to-all-start.1 = ((bf16[16,8,8192]{2,1,0:T(8,128)(2,1)}), bf16[16,8,8192]{2,1,0:T(8,128)(2,1)S(1)}, u32[]{:S(2)}, u32[]{:S(2)}) async-start(bf16[16,8,8192]{2,1,0:T(8,128)(2,1)} %pick_down.1), calls=%async_computation.1 | async-start | bytes 4194304 | tf_op jit(solution)/shard_map/all_to_all | solution.py:270
  30.4 5.8 %collective-permute-start = (bf16[64,512]{1,0:T(8,128)(2,1)S(1)}, bf16[64,512]{1,0:T(8,128)(2,1)S(1)}, u32[]{:S(2)}, u32[]{:S(2)}) collective-permute-start(bf16[64,512]{1,0:T(8,128)(2,1)S(1)} %copy-done.10), channel_id=1, source_target_pairs={{0,1},{1,0},{2,3},{3,2},{4,5},{5,4},{6,7},{7,6},{8,9},{9,8},{10,11... | collective-permute-start | bytes 196616 | tf_op jit(solution)/shard_map/ppermute | solution.py:273
  30.5 7.4 %collective-permute-start.1 = (bf16[64,512]{1,0:T(8,128)(2,1)S(1)}, bf16[64,512]{1,0:T(8,128)(2,1)S(1)}, u32[]{:S(2)}, u32[]{:S(2)}) collective-permute-start(bf16[64,512]{1,0:T(8,128)(2,1)S(1)} %copy-done.9), channel_id=1, source_target_pairs={{0,2},{1,3},{2,4},{3,5},{4,6},{5,7},{6,0},{7,1},{8,10},{9,11},{10,... | collective-permute-start | bytes 196616 | tf_op jit(solution)/shard_map/ppermute | solution.py:273
  31.7 17.2 %copy-start.1 = (bf16[64,512]{1,0:T(8,128)(2,1)S(1)}, bf16[64,512]{1,0:T(8,128)(2,1)}, u32[]{:S(2)}) copy-start(bf16[64,512]{1,0:T(8,128)(2,1)} %get-tuple-element.51.rest_0_) | copy-start | bytes 196612
  31.7 17.1 %collective-permute-start.2 = (bf16[64,512]{1,0:T(8,128)(2,1)S(1)}, bf16[64,512]{1,0:T(8,128)(2,1)S(1)}, u32[]{:S(2)}, u32[]{:S(2)}) collective-permute-start(bf16[64,512]{1,0:T(8,128)(2,1)S(1)} %copy-done.8), channel_id=1, source_target_pairs={{0,3},{1,2},{2,5},{3,4},{4,7},{5,6},{6,1},{7,0},{8,11},{9,10},{10,... | collective-permute-start | bytes 196616 | tf_op jit(solution)/shard_map/ppermute | solution.py:273
  33.0 15.8 %collective-permute-start.3 = (bf16[64,512]{1,0:T(8,128)(2,1)S(1)}, bf16[64,512]{1,0:T(8,128)(2,1)S(1)}, u32[]{:S(2)}, u32[]{:S(2)}) collective-permute-start(bf16[64,512]{1,0:T(8,128)(2,1)S(1)} %copy-done.7), channel_id=1, source_target_pairs={{0,4},{1,5},{2,6},{3,7},{4,0},{5,1},{6,2},{7,3},{8,12},{9,13},{10,... | collective-permute-start | bytes 196616 | tf_op jit(solution)/shard_map/ppermute | solution.py:273
  35.2 13.7 %collective-permute-start.4 = (bf16[64,512]{1,0:T(8,128)(2,1)S(1)}, bf16[64,512]{1,0:T(8,128)(2,1)S(1)}, u32[]{:S(2)}, u32[]{:S(2)}) collective-permute-start(bf16[64,512]{1,0:T(8,128)(2,1)S(1)} %copy-done.6), channel_id=1, source_target_pairs={{0,5},{1,4},{2,7},{3,6},{4,1},{5,0},{6,3},{7,2},{8,13},{9,12},{10,... | collective-permute-start | bytes 196616 | tf_op jit(solution)/shard_map/ppermute | solution.py:273
  36.2 12.6 %collective-permute-start.5 = (bf16[64,512]{1,0:T(8,128)(2,1)S(1)}, bf16[64,512]{1,0:T(8,128)(2,1)S(1)}, u32[]{:S(2)}, u32[]{:S(2)}) collective-permute-start(bf16[64,512]{1,0:T(8,128)(2,1)S(1)} %copy-done.5), channel_id=1, source_target_pairs={{0,6},{1,7},{2,0},{3,1},{4,2},{5,3},{6,4},{7,5},{8,14},{9,15},{10,... | collective-permute-start | bytes 196616 | tf_op jit(solution)/shard_map/ppermute | solution.py:273
  38.0 10.9 %collective-permute-start.6 = (bf16[64,512]{1,0:T(8,128)(2,1)S(1)}, bf16[64,512]{1,0:T(8,128)(2,1)S(1)}, u32[]{:S(2)}, u32[]{:S(2)}) collective-permute-start(bf16[64,512]{1,0:T(8,128)(2,1)S(1)} %copy-done.4), channel_id=1, source_target_pairs={{0,7},{1,6},{2,1},{3,0},{4,3},{5,2},{6,5},{7,4},{8,15},{9,14},{10,... | collective-permute-start | bytes 196616 | tf_op jit(solution)/shard_map/ppermute | solution.py:273
  60.4 1.3 %copy-start.3 = (bf16[16,8,8192]{2,1,0:T(8,128)(2,1)}, bf16[16,8,8192]{2,1,0:T(8,128)(2,1)S(1)}, u32[]{:S(2)}) copy-start(bf16[16,8,8192]{2,1,0:T(8,128)(2,1)S(1)} %all-to-all-done.1.down_ref) | copy-start | bytes 6291460
  61.7 27.2 %all-to-all-start.2 = ((bf16[16,64,512]{2,1,0:T(8,128)(2,1)}), bf16[16,64,512]{2,1,0:T(8,128)(2,1)S(1)}, u32[]{:S(2)}, u32[]{:S(2)}) async-start(bf16[16,64,512]{2,1,0:T(8,128)(2,1)} %pick_up.1), calls=%async_computation.2 | async-start | bytes 2097152 | tf_op jit(solution)/shard_map/all_to_all | solution.py:279
  66.3 22.7 %copy-start = (f32[896,512]{1,0:T(8,128)S(1)}, f32[896,512]{1,0:T(8,128)}, u32[]{:S(2)}) copy-start(f32[896,512]{1,0:T(8,128)} %get-tuple-element.63.base_ref) | copy-start | bytes 5505028
  66.3 22.7 %copy-start.2 = (s32[7]{0:T(128)S(1)}, s32[7]{0:T(128)}, u32[]{:S(2)}) copy-start(s32[7]{0:T(128)} %and_select_fusion.4.row_ref) | copy-start | bytes 88
  77.0 1.4 %collective-permute-start.7 = (f32[7,8,128]{2,1,0:T(8,128)}, f32[7,8,128]{2,1,0:T(8,128)S(1)}, u32[]{:S(2)}, u32[]{:S(2)}) collective-permute-start(f32[7,8,128]{2,1,0:T(8,128)} %shrink.1), channel_id=1, source_target_pairs={{0,1},{1,0},{2,3},{3,2},{4,5},{5,4},{6,7},{7,6},{8,9},{9,8},{10,11... | collective-permute-start | bytes 86024 | tf_op jit(solution)/shard_map/ppermute | solution.py:282
  79.2 5.8 %collective-permute-start.10 = (f32[2,7,8,128]{3,2,1,0:T(8,128)S(1)}, f32[2,7,8,128]{3,2,1,0:T(8,128)S(1)}, u32[]{:S(2)}, u32[]{:S(2)}) collective-permute-start(f32[2,7,8,128]{3,2,1,0:T(8,128)S(1)} %pad_maximum_fusion.low0), channel_id=1, source_target_pairs={{0,6},{1,7},{2,0},{3,1},{4,2},{5,3},{6,4},{7,5},{8,14},{9,15},{10,... | collective-permute-start | bytes 172040 | tf_op jit(solution)/shard_map/ppermute | solution.py:284
  82.7 6.2 %collective-permute-start.8 = (f32[2,7,8,128]{3,2,1,0:T(8,128)S(1)}, f32[2,7,8,128]{3,2,1,0:T(8,128)S(1)}, u32[]{:S(2)}, u32[]{:S(2)}) collective-permute-start(f32[2,7,8,128]{3,2,1,0:T(8,128)S(1)} %pad_maximum_fusion.low0), channel_id=1, source_target_pairs={{0,2},{1,3},{2,4},{3,5},{4,6},{5,7},{6,0},{7,1},{8,10},{9,11},{10,... | collective-permute-start | bytes 172040 | tf_op jit(solution)/shard_map/ppermute | solution.py:284
  82.7 6.2 %collective-permute-start.9 = (f32[2,7,8,128]{3,2,1,0:T(8,128)S(1)}, f32[2,7,8,128]{3,2,1,0:T(8,128)S(1)}, u32[]{:S(2)}, u32[]{:S(2)}) collective-permute-start(f32[2,7,8,128]{3,2,1,0:T(8,128)S(1)} %pad_maximum_fusion.low0), channel_id=1, source_target_pairs={{0,4},{1,5},{2,6},{3,7},{4,0},{5,1},{6,2},{7,3},{8,12},{9,13},{10,... | collective-permute-start | bytes 172040 | tf_op jit(solution)/shard_map/ppermute | solution.py:284

commit v3 on v2

v3 whole, which is shorter than its diff:
```python
import functools

import jax
import jax.numpy as jnp
from jax import lax
from jax.experimental import pallas as pl
from jax.experimental.pallas import tpu as pltpu
from jax.sharding import PartitionSpec as P

ADAPTER_SCALE = 0.5
X, CORES = 4, 2
LANES = X * CORES
ORDER = (2, 6, 3, 7, 4, 5, 1)
BOTH = ("req", "tp")


def lane_shift(groups, dx, dc):
    return [
        (g * LANES + x * CORES + c, g * LANES + (x + dx) % X * CORES + (c + dc) % CORES)
        for g in range(groups)
        for x in range(X)
        for c in range(CORES)
    ]


def relative(lane, other):
    dx = (lane // CORES - other // CORES) % X
    dc = (lane % CORES - other % CORES) % CORES
    return dx * CORES + dc


VMEM = pl.BlockSpec(memory_space=pltpu.VMEM)
SMEM = pl.BlockSpec(memory_space=pltpu.SMEM)
ANY = pl.BlockSpec(memory_space=pl.ANY)


def reached(lane, k):
    return (lane // CORES + k // CORES) % X * CORES + (lane % CORES + k % CORES) % CORES


def split_down_kernel(lane_ref, down_ref, *outs):
    for k in range(LANES):
        outs[k][...] = down_ref[reached(lane_ref[0], k)]


def split_up_kernel(lane_ref, up_ref, *outs):
    width = outs[0].shape[1]
    for k in range(LANES):
        col = pl.multiple_of(reached(lane_ref[0], k) * width, width)
        outs[k][...] = up_ref[0, :, pl.ds(col, width)]


def split(kernel, lane, whole, piece, name):
    return pl.pallas_call(
        kernel,
        in_specs=[SMEM, VMEM],
        out_specs=[VMEM] * LANES,
        out_shape=[jax.ShapeDtypeStruct(piece, whole.dtype)] * LANES,
        compiler_params=pltpu.CompilerParams(vmem_limit_bytes=16 * 2**20),
        name=name,
    )(lane, whole)


def spread(pieces, groups):
    return [
        lax.ppermute(pieces[k], BOTH, lane_shift(groups, k // CORES, k % CORES)) for k in ORDER
    ] + [pieces[0]]


def pick_kernel(pick_ref, *rest):
    srcs, out_ref, staged = rest[:LANES], rest[LANES], rest[LANES + 1]
    for src, k in zip(srcs, ORDER + (0,)):
        staged[k] = src[...]
    for g in range(out_ref.shape[0]):
        out_ref[g] = staged[pick_ref[g]]


def pick(shifts, pieces, name):
    groups = shifts.shape[0]
    shape, dtype = pieces[0].shape, pieces[0].dtype
    return pl.pallas_call(
        pick_kernel,
        in_specs=[SMEM] + [VMEM] * LANES,
        out_specs=VMEM,
        out_shape=jax.ShapeDtypeStruct((groups,) + shape, dtype),
        scratch_shapes=[pltpu.VMEM((LANES,) + shape, dtype)],
        compiler_params=pltpu.CompilerParams(vmem_limit_bytes=16 * 2**20),
        name=name,
    )(shifts, *pieces)


CHUNK = 1024
NORM_ROWS = 128


def norm_base_kernel(x_ref, gain_ref, weight_ref, normed_ref, base_ref):
    rows, features = x_ref.shape
    squares = jnp.zeros((rows, 128), jnp.float32)
    for p in range(features // 128):
        wide = x_ref[:, p * 128 : (p + 1) * 128].astype(jnp.float32)
        squares = squares + wide * wide
    mean = jnp.sum(squares, axis=1, keepdims=True) / features
    inverse_rms = lax.rsqrt(mean + 1e-05)
    total = jnp.zeros(base_ref.shape, jnp.float32)
    for p in range(features // CHUNK):
        cols = slice(p * CHUNK, (p + 1) * CHUNK)
        wide = x_ref[:, cols].astype(jnp.float32)
        normed = (wide * inverse_rms * gain_ref[:, cols]).astype(jnp.bfloat16)
        normed_ref[:, cols] = normed
        total += jnp.dot(normed, weight_ref[cols, :], preferred_element_type=jnp.float32)
    base_ref[...] = total


def norm_base(hidden, gain, weight):
    rows, features = hidden.shape
    cols = weight.shape[1]
    return pl.pallas_call(
        norm_base_kernel,
        grid=(rows // NORM_ROWS,),
        in_specs=[
            pl.BlockSpec((NORM_ROWS, features), lambda i: (i, 0)),
            pl.BlockSpec((1, features), lambda i: (0, 0)),
            pl.BlockSpec((features, cols), lambda i: (0, 0), pipeline_mode=pl.Buffered(1)),
        ],
        out_specs=[
            pl.BlockSpec((NORM_ROWS, features), lambda i: (i, 0)),
            pl.BlockSpec((NORM_ROWS, cols), lambda i: (i, 0)),
        ],
        out_shape=[
            jax.ShapeDtypeStruct((rows, features), jnp.bfloat16),
            jax.ShapeDtypeStruct((rows, cols), jnp.float32),
        ],
        compiler_params=pltpu.CompilerParams(vmem_limit_bytes=56 * 2**20),
        cost_estimate=pl.CostEstimate(
            flops=4 * rows * features * cols,
            bytes_accessed=4 * rows * features + 2 * features * cols,
            transcendentals=rows,
        ),
        name="norm_base",
    )(hidden, gain.reshape(1, features), weight)


def shrink_kernel(row_ref, down_ref, normed_hbm, low_ref, normed_ref, sems):
    blocks, block = low_ref.shape[0], low_ref.shape[2]

    def rows_of(j):
        return pl.ds(pl.multiple_of(j * block, block), block)

    def copy(j):
        return pltpu.make_async_copy(normed_hbm.at[rows_of(j)], normed_ref.at[rows_of(j)], sems.at[j])

    for j in range(blocks):
        copy(j).start()

    @pl.loop(0, blocks)
    def _(j):
        copy(j).wait()
        low_ref[j] = lax.dot_general(
            down_ref[row_ref[j]],
            normed_ref[rows_of(j), :],
            (((1,), (1,)), ((), ())),
            preferred_element_type=jnp.float32,
        )


def shrink(owner_rows, down_got, normed):
    blocks = owner_rows.shape[0]
    rows, features = normed.shape
    piece = down_got.shape[1]
    return pl.pallas_call(
        shrink_kernel,
        in_specs=[SMEM, VMEM, ANY],
        out_specs=VMEM,
        out_shape=jax.ShapeDtypeStruct((blocks, piece, rows // blocks), jnp.float32),
        scratch_shapes=[pltpu.VMEM((rows, features), jnp.bfloat16), pltpu.SemaphoreType.DMA((blocks,))],
        compiler_params=pltpu.CompilerParams(vmem_limit_bytes=48 * 2**20),
        cost_estimate=pl.CostEstimate(
            flops=2 * rows * features * 256, bytes_accessed=2 * rows * features, transcendentals=0
        ),
        name="shrink",
    )(owner_rows, down_got, normed)


def expand_kernel(row_ref, lane_ref, low0, low1, low2, low3, up_ref, base_ref, out_ref, full):
    lows = (low0, low1, low2, low3)
    lane = lane_ref[0]
    blocks, part, block = low0.shape[1:]
    for dx in range(X):
        for dc in range(CORES):
            src = (lane // CORES - dx) % X * CORES + (lane % CORES - dc) % CORES
            rows = pl.ds(pl.multiple_of(src * part, part), part)
            for j in range(blocks):
                full[j, rows, :] = lows[dx][dc, j]

    for j in range(blocks):
        low = full[j].astype(jnp.bfloat16)
        term = lax.dot_general(
            low, up_ref[row_ref[j]], (((0,), (0,)), ((), ())), preferred_element_type=jnp.float32
        )
        rows = slice(j * block, (j + 1) * block)
        out_ref[rows, :] = (base_ref[rows, :] + ADAPTER_SCALE * term).astype(out_ref.dtype)


def expand(owner_rows, lane, lows, up_got, base):
    blocks, part, block = lows[0].shape[1:]
    return pl.pallas_call(
        expand_kernel,
        in_specs=[SMEM, SMEM] + [VMEM] * (len(lows) + 2),
        out_specs=VMEM,
        out_shape=jax.ShapeDtypeStruct(base.shape, jnp.bfloat16),
        scratch_shapes=[pltpu.VMEM((blocks, part * LANES, block), jnp.float32)],
        compiler_params=pltpu.CompilerParams(vmem_limit_bytes=16 * 2**20),
        name="expand",
    )(owner_rows, lane, *lows, up_got, base)


def shards(
    hidden,
    norm_gain_vector,
    query_weight,
    adapter_down_weight,
    adapter_up_weight,
    block_adapter_ids,
    adapter_slot_table,
):
    groups, blocks = block_adapter_ids.shape
    rank, features = adapter_down_weight.shape[1:]
    lane = lax.axis_index("tp")
    group = lax.axis_index("req")
    lane_arr = lane.reshape(1).astype(jnp.int32)

    piece = (rank // LANES, features)
    down_whole = adapter_down_weight.reshape((LANES,) + piece)
    down_row = spread(split(split_down_kernel, lane_arr, down_whole, piece, "split_down"), groups)

    matches = block_adapter_ids[:, :, None] == jnp.arange(adapter_slot_table.shape[0], dtype=jnp.int32)
    slots = jnp.sum(jnp.where(matches, adapter_slot_table, 0), axis=2)
    here = slots // LANES == group
    wanted = relative(lane, jnp.sum(jnp.where(here, slots % LANES, 0), axis=1))
    owner_rows = lax.dynamic_index_in_dim(slots, group, 0, keepdims=False) // LANES

    down_send, hidden, adapter_up_weight = lax.optimization_barrier(
        (pick(wanted, down_row, "pick_down"), hidden, adapter_up_weight)
    )
    down_got = lax.all_to_all(down_send, "req", 0, 0, tiled=True)
    piece = (rank, adapter_up_weight.shape[2] // LANES)
    up_row = spread(split(split_up_kernel, lane_arr, adapter_up_weight, piece, "split_up"), groups)
    normed, base = norm_base(hidden, norm_gain_vector, query_weight)
    up_row, base = lax.optimization_barrier((up_row, base))
    up_got = lax.all_to_all(pick(wanted, up_row, "pick_up"), "req", 0, 0, tiled=True)

    low = shrink(owner_rows, down_got, normed)
    other = lax.ppermute(low, BOTH, lane_shift(groups, 0, 1))
    chip = jnp.stack([low, other])
    lows = [chip] + [lax.ppermute(chip, BOTH, lane_shift(groups, dx, 0)) for dx in range(1, X)]
    return expand(owner_rows, lane_arr, lows, up_got, base)


def solution(mesh):
    return jax.shard_map(
        shards,
        mesh=mesh,
        in_specs=(
            P("req", None),
            P(),
            P(None, "tp"),
            P(("req", "tp"), None, None),
            P(("req", "tp"), None, None),
            P(),
            P(),
        ),
        out_specs=P("req", "tp"),
        check_vma=False,
    )
```

time: 91.7 us -> 84.8 us (0.925)
  Pallas kernels: 41.2 us -> 27.5 us
  starting transfers between devices: 30.2 us -> 36.9 us
  local copies, waits for them, and re-layouts: 1.54 us -> 5.2 us
  waiting for transfers between devices: 15.3 us -> 13.6 us
  other arithmetic: 2.34 us -> 1.05 us
    pallas_call x7, Pallas kernels: 41.2 us -> 27.5 us  [the longest x1 17.2 us: norm_base(): pl.pallas_call(norm_base_kernel, grid=(rows // NORM_ROWS,), in_specs=[pl....]
    ppermute x7 -> x14, starting transfers between devices: 8.22 us -> 19.9 us  [spread(): lax.ppermute(pieces[k], BOTH, lane_shift(groups, k // CORES, k % CORES))]
    all_to_all x1, waiting for transfers between devices: 8.94 us -> 1.72 us  [shards(): down_got = lax.all_to_all(down_send, 'req', 0, 0, tiled=True)]
    all_to_all x2 -> x1, waiting for transfers between devices: 0.96 us -> 6.31 us  [shards(): lax.all_to_all(pick(wanted, up_row, 'pick_up'), 'req', 0, 0, tiled=True)]
    ppermute x7 -> x14, waiting for transfers between devices: 0.02 us -> 4.37 us  [spread(): lax.ppermute(pieces[k], BOTH, lane_shift(groups, k // CORES, k % CORES))]
    ppermute x3, waiting for transfers between devices: 4 us -> 0.01 us  [shards(): lax.ppermute(chip, BOTH, lane_shift(groups, dx, 0))]
    unnamed x22 -> x10, local copies, waits for them, and re-layouts: 1.35 us -> 5.01 us
    all_to_all x2 -> x1, starting transfers between devices: 8.2 us -> 5.49 us  [shards(): lax.all_to_all(pick(wanted, up_row, 'pick_up'), 'req', 0, 0, tiled=True)]
  transfers between devices with their start and end apart: 14 -> 20, of which waited for: 4 -> 5; matrix products, arithmetic and copies ran while one was open for 3% -> 1% of each run, Pallas kernels for 41% -> 29%
where the time goes in v3:
time: 84.8 us; the launch traced here: 84.4 us
  starting transfers between devices  36.9 us (44%)
  Pallas kernels  27.5 us (32%)
  waiting for transfers between devices  13.6 us (16%)
  local copies, waits for them, and re-layouts  5.2 us (6%)
  other arithmetic  1.05 us (1%)
    ppermute x14, starting transfers between devices, spread(): lax.ppermute(pieces[k], BOTH, lane_shift(groups, k // CORES, k % CORES))  19.9 us
    pallas_call x1, Pallas kernels, norm_base(): pl.pallas_call(norm_base_kernel, grid=(rows // NORM_ROWS,), in_specs=[pl....  17.2 us
    all_to_all x1, starting transfers between devices, shards(): down_got = lax.all_to_all(down_send, 'req', 0, 0, tiled=True)  8.04 us
    pallas_call x1, Pallas kernels, shrink(): pl.pallas_call(shrink_kernel, in_specs=[SMEM, VMEM, ANY], out_specs=VMEM,...  6.8 us
    all_to_all x1, waiting for transfers between devices, shards(): lax.all_to_all(pick(wanted, up_row, 'pick_up'), 'req', 0, 0, tiled=True)  6.31 us
    all_to_all x1, starting transfers between devices, shards(): lax.all_to_all(pick(wanted, up_row, 'pick_up'), 'req', 0, 0, tiled=True)  5.49 us
    unnamed x10, local copies, waits for them, and re-layouts  5.01 us
    ppermute x14, waiting for transfers between devices, spread(): lax.ppermute(pieces[k], BOTH, lane_shift(groups, k // CORES, k % CORES))  4.37 us
  transfers between devices with their start and end apart: 20, of which 5 were waited for; matrix products, arithmetic and copies ran while one was open for 1% of the time, Pallas kernels for 29%

profile of v3, /device:TPU:0, one launch (start us, length us, event | category | flops | bytes accessed | tf_op | source)
XLA Modules:
  0.0 84.4 jit_solution(13442421080773329386)
XLA Ops:
  0.0 1.2 %copy-done.3 = bf16[1,64,8192]{2,1,0:T(8,128)(2,1)S(1)} copy-done((bf16[1,64,8192]{2,1,0:T(8,128)(2,1)S(1)}, bf16[1,64,8192]{2,1,0:T(8,128)(2,1)}, u32[]{:S(2)}) %copy-start.3) | copy-done | bytes 1048600
  1.2 0.1 split_down.1
  1.3 1.6 %collective-permute-start = (bf16[8,8192]{1,0:T(8,128)(2,1)S(1)}, bf16[8,8192]{1,0:T(8,128)(2,1)S(1)}, u32[]{:S(2)}, u32[]{:S(2)}) collective-permute-start(bf16[8,8192]{1,0:T(8,128)(2,1)S(1)} %get-tuple-element.35), channel_id=1, source_target_pairs={{0,2},{1,3},{2,4},{3,5},{4,6},{5,7},{6,0},{7,1},{8,10},{9,11},{10,... | collective-permute-start | bytes 393224 | tf_op jit(solution)/shard_map/ppermute | solution.py:66
  2.9 1.7 %collective-permute-start.1 = (bf16[8,8192]{1,0:T(8,128)(2,1)S(1)}, bf16[8,8192]{1,0:T(8,128)(2,1)S(1)}, u32[]{:S(2)}, u32[]{:S(2)}) collective-permute-start(bf16[8,8192]{1,0:T(8,128)(2,1)S(1)} %get-tuple-element.36), channel_id=1, source_target_pairs={{0,6},{1,7},{2,0},{3,1},{4,2},{5,3},{6,4},{7,5},{8,14},{9,15},{10,... | collective-permute-start | bytes 393224 | tf_op jit(solution)/shard_map/ppermute | solution.py:66
  4.6 0.0 collective-permute-start.2
  4.6 3.0 %collective-permute-start.3 = (bf16[8,8192]{1,0:T(8,128)(2,1)S(1)}, bf16[8,8192]{1,0:T(8,128)(2,1)S(1)}, u32[]{:S(2)}, u32[]{:S(2)}) collective-permute-start(bf16[8,8192]{1,0:T(8,128)(2,1)S(1)} %get-tuple-element.38), channel_id=1, source_target_pairs={{0,7},{1,6},{2,1},{3,0},{4,3},{5,2},{6,5},{7,4},{8,15},{9,14},{10,... | collective-permute-start | bytes 393224 | tf_op jit(solution)/shard_map/ppermute | solution.py:66
  7.6 0.7 collective-permute-start.4
  8.2 1.0 %select_reduce_fusion = s32[16,7]{0,1:T(8,128)S(1)} fusion(s32[128]{0:T(128)} %param.13, s32[16,7]{0,1:T(8,128)} %param.12), kind=kLoop, calls=%fused_computation.1 | loop fusion | flops 42896 | bytes 1408 | tf_op jit(solution)/shard_map/reduce_sum | solution.py:237
  9.3 0.0 collective-permute-done.rest_0_
  9.3 1.5 %collective-permute-start.5 = (bf16[8,8192]{1,0:T(8,128)(2,1)S(1)}, bf16[8,8192]{1,0:T(8,128)(2,1)S(1)}, u32[]{:S(2)}, u32[]{:S(2)}) collective-permute-start(bf16[8,8192]{1,0:T(8,128)(2,1)S(1)} %get-tuple-element.40), channel_id=1, source_target_pairs={{0,5},{1,4},{2,7},{3,6},{4,1},{5,0},{6,3},{7,2},{8,13},{9,12},{10,... | collective-permute-start | bytes 393224 | tf_op jit(solution)/shard_map/ppermute | solution.py:66
  10.8 0.0 collective-permute-done.1.rest_1_
  10.8 1.5 %collective-permute-start.6 = (bf16[8,8192]{1,0:T(8,128)(2,1)S(1)}, bf16[8,8192]{1,0:T(8,128)(2,1)S(1)}, u32[]{:S(2)}, u32[]{:S(2)}) collective-permute-start(bf16[8,8192]{1,0:T(8,128)(2,1)S(1)} %get-tuple-element.41), channel_id=1, source_target_pairs={{0,1},{1,0},{2,3},{3,2},{4,5},{5,4},{6,7},{7,6},{8,9},{9,8},{10,11... | collective-permute-start | bytes 393224 | tf_op jit(solution)/shard_map/ppermute | solution.py:66
  12.4 0.0 collective-permute-done.2.rest_2_
  12.4 3.3 %collective-permute-done.3.rest_3_ = bf16[8,8192]{1,0:T(8,128)(2,1)S(1)} collective-permute-done((bf16[8,8192]{1,0:T(8,128)(2,1)S(1)}, bf16[8,8192]{1,0:T(8,128)(2,1)S(1)}, u32[]{:S(2)}, u32[]{:S(2)}) %collective-permute-start.3) | collective-permute-done | bytes 131104 | tf_op jit(solution)/shard_map/ppermute | solution.py:66
  15.7 0.0 collective-permute-done.4.rest_4_
  15.7 1.0 %collective-permute-done.5.rest_5_ = bf16[8,8192]{1,0:T(8,128)(2,1)S(1)} collective-permute-done((bf16[8,8192]{1,0:T(8,128)(2,1)S(1)}, bf16[8,8192]{1,0:T(8,128)(2,1)S(1)}, u32[]{:S(2)}, u32[]{:S(2)}) %collective-permute-start.5) | collective-permute-done | bytes 131104 | tf_op jit(solution)/shard_map/ppermute | solution.py:66
  16.7 0.0 collective-permute-done.6.rest_6_
  16.7 0.7 pick_down.1
  17.5 1.3 %copy-done = bf16[16,8,8192]{2,1,0:T(8,128)(2,1)} copy-done((bf16[16,8,8192]{2,1,0:T(8,128)(2,1)}, bf16[16,8,8192]{2,1,0:T(8,128)(2,1)S(1)}, u32[]{:S(2)}) %copy-start) | copy-done | bytes 2097176
  18.8 8.0 %all-to-all-start = ((bf16[16,8,8192]{2,1,0:T(8,128)(2,1)}), bf16[16,8,8192]{2,1,0:T(8,128)(2,1)S(1)}, u32[]{:S(2)}, u32[]{:S(2)}) async-start(bf16[16,8,8192]{2,1,0:T(8,128)(2,1)} %copy-done), calls=%async_computation | async-start | bytes 4194304 | tf_op jit(solution)/shard_map/all_to_all | solution.py:245
  26.8 0.1 split_up.1
  26.9 1.5 %collective-permute-start.11 = (bf16[64,512]{1,0:T(8,128)(2,1)S(1)}, bf16[64,512]{1,0:T(8,128)(2,1)S(1)}, u32[]{:S(2)}, u32[]{:S(2)}) collective-permute-start(bf16[64,512]{1,0:T(8,128)(2,1)S(1)} %get-tuple-element.47), channel_id=1, source_target_pairs={{0,2},{1,3},{2,4},{3,5},{4,6},{5,7},{6,0},{7,1},{8,10},{9,11},{10,... | collective-permute-start | bytes 196616 | tf_op jit(solution)/shard_map/ppermute | solution.py:66
  28.4 1.8 %collective-permute-start.12 = (bf16[64,512]{1,0:T(8,128)(2,1)S(1)}, bf16[64,512]{1,0:T(8,128)(2,1)S(1)}, u32[]{:S(2)}, u32[]{:S(2)}) collective-permute-start(bf16[64,512]{1,0:T(8,128)(2,1)S(1)} %get-tuple-element.48), channel_id=1, source_target_pairs={{0,6},{1,7},{2,0},{3,1},{4,2},{5,3},{6,4},{7,5},{8,14},{9,15},{10,... | collective-permute-start | bytes 196616 | tf_op jit(solution)/shard_map/ppermute | solution.py:66
  30.2 0.0 collective-permute-start.13
  30.2 3.0 %collective-permute-start.14 = (bf16[64,512]{1,0:T(8,128)(2,1)S(1)}, bf16[64,512]{1,0:T(8,128)(2,1)S(1)}, u32[]{:S(2)}, u32[]{:S(2)}) collective-permute-start(bf16[64,512]{1,0:T(8,128)(2,1)S(1)} %get-tuple-element.50), channel_id=1, source_target_pairs={{0,7},{1,6},{2,1},{3,0},{4,3},{5,2},{6,5},{7,4},{8,15},{9,14},{10,... | collective-permute-start | bytes 196616 | tf_op jit(solution)/shard_map/ppermute | solution.py:66
  33.2 0.0 collective-permute-start.15
  33.2 0.0 collective-permute-done.11.rest_0_
  33.2 2.5 %collective-permute-start.16 = (bf16[64,512]{1,0:T(8,128)(2,1)S(1)}, bf16[64,512]{1,0:T(8,128)(2,1)S(1)}, u32[]{:S(2)}, u32[]{:S(2)}) collective-permute-start(bf16[64,512]{1,0:T(8,128)(2,1)S(1)} %get-tuple-element.52), channel_id=1, source_target_pairs={{0,5},{1,4},{2,7},{3,6},{4,1},{5,0},{6,3},{7,2},{8,13},{9,12},{10,... | collective-permute-start | bytes 196616 | tf_op jit(solution)/shard_map/ppermute | solution.py:66
  35.6 1.2 %collective-permute-start.17 = (bf16[64,512]{1,0:T(8,128)(2,1)S(1)}, bf16[64,512]{1,0:T(8,128)(2,1)S(1)}, u32[]{:S(2)}, u32[]{:S(2)}) collective-permute-start(bf16[64,512]{1,0:T(8,128)(2,1)S(1)} %get-tuple-element.53), channel_id=1, source_target_pairs={{0,1},{1,0},{2,3},{3,2},{4,5},{5,4},{6,7},{7,6},{8,9},{9,8},{10,11... | collective-permute-start | bytes 196616 | tf_op jit(solution)/shard_map/ppermute | solution.py:66
  36.8 17.2 %norm_base.1 = (bf16[896,8192]{1,0:T(8,128)(2,1)}, f32[896,512]{1,0:T(8,128)}) custom-call(bf16[896,8192]{1,0:T(8,128)(2,1)} %x_ref, f32[1,8192]{1,0:T(1,128)} %bitcast.8, bf16[8192,512]{1,0:T(8,128)(2,1)} %weight_ref.1), custom_call_target="tpu_custom_call" | custom-call | flops 15032385536 | bytes 37748736 | tf_op jit(solution)/shard_map/norm_base/pallas_call | solution.py:117
  54.1 0.0 collective-permute-done.13.rest_2_
  54.1 0.0 collective-permute-done.14.rest_3_
  54.1 0.0 collective-permute-done.17.rest_6_
  54.1 0.6 pick_up.1
  54.8 1.0 %copy-done.1 = bf16[16,64,512]{2,1,0:T(8,128)(2,1)} copy-done((bf16[16,64,512]{2,1,0:T(8,128)(2,1)}, bf16[16,64,512]{2,1,0:T(8,128)(2,1)S(1)}, u32[]{:S(2)}) %copy-start.1) | copy-done | bytes 1048600
  55.7 1.7 %all-to-all-done.down_ref = bf16[16,8,8192]{2,1,0:T(8,128)(2,1)S(1)} async-done(((bf16[16,8,8192]{2,1,0:T(8,128)(2,1)}), bf16[16,8,8192]{2,1,0:T(8,128)(2,1)S(1)}, u32[]{:S(2)}, u32[]{:S(2)}) %all-to-all-start) | async-done | bytes 2097184 | tf_op jit(solution)/shard_map/all_to_all | solution.py:245
  57.5 5.5 %all-to-all-start.1 = ((bf16[16,64,512]{2,1,0:T(8,128)(2,1)}), bf16[16,64,512]{2,1,0:T(8,128)(2,1)S(1)}, u32[]{:S(2)}, u32[]{:S(2)}) async-start(bf16[16,64,512]{2,1,0:T(8,128)(2,1)} %copy-done.1), calls=%async_computation.1 | async-start | bytes 2097152 | tf_op jit(solution)/shard_map/all_to_all | solution.py:250
  63.0 0.2 dynamic-slice_reduce_fusion
  63.2 6.8 %shrink.1 = f32[7,8,128]{2,1,0:T(8,128)S(1)} custom-call(s32[7]{0:T(128)S(1)} %and_select_fusion.4.row_ref, bf16[16,8,8192]{2,1,0:T(8,128)(2,1)S(1)} %all-to-all-done.down_ref, bf16[896,8192]{1,0:T(8,128)(2,1)} %get-tuple-element.45.normed_hbm), custom_call_target="tpu_custom_call" | custom-call | flops 3758096384 | bytes 14680064 | tf_op jit(solution)/shard_map/shrink/pallas_call | solution.py:170
  70.0 0.1 collective-permute-start.7
  70.1 1.2 %collective-permute-done.7 = f32[7,8,128]{2,1,0:T(8,128)S(1)} collective-permute-done((f32[7,8,128]{2,1,0:T(8,128)S(1)}, f32[7,8,128]{2,1,0:T(8,128)S(1)}, u32[]{:S(2)}, u32[]{:S(2)}) %collective-permute-start.7) | collective-permute-done | bytes 28704 | tf_op jit(solution)/shard_map/ppermute | solution.py:253
  71.2 0.4 collective-permute-start.8
  71.6 3.0 %collective-permute-start.9 = (f32[2,7,8,128]{3,2,1,0:T(8,128)S(1)}, f32[2,7,8,128]{3,2,1,0:T(8,128)S(1)}, u32[]{:S(2)}, u32[]{:S(2)}) collective-permute-start(f32[2,7,8,128]{3,2,1,0:T(8,128)S(1)} %pad_maximum_fusion.low0), channel_id=1, source_target_pairs={{0,4},{1,5},{2,6},{3,7},{4,0},{5,1},{6,2},{7,3},{8,12},{9,13},{10,... | collective-permute-start | bytes 172040 | tf_op jit(solution)/shard_map/ppermute | solution.py:255
  74.6 6.3 %all-to-all-done.1.up_ref = bf16[16,64,512]{2,1,0:T(8,128)(2,1)S(1)} async-done(((bf16[16,64,512]{2,1,0:T(8,128)(2,1)}), bf16[16,64,512]{2,1,0:T(8,128)(2,1)S(1)}, u32[]{:S(2)}, u32[]{:S(2)}) %all-to-all-start.1) | async-done | bytes 1048608 | tf_op jit(solution)/shard_map/all_to_all | solution.py:250
  81.0 0.0 collective-permute-done.8.low1
  81.0 0.0 collective-permute-done.9.low2
  81.0 1.5 %copy-done.2 = f32[896,512]{1,0:T(8,128)S(1)} copy-done((f32[896,512]{1,0:T(8,128)S(1)}, f32[896,512]{1,0:T(8,128)}, u32[]{:S(2)}) %copy-start.2) | copy-done | bytes 1835032
  82.5 1.9 %expand.1 = bf16[896,512]{1,0:T(8,128)(2,1)} custom-call(s32[7]{0:T(128)S(1)} %and_select_fusion.4.row_ref, s32[1]{0:T(128)} %bitcast.lane_ref, f32[2,7,8,128]{3,2,1,0:T(8,128)S(1)} %pad_maximum_fusion.low0, f32[2,7,8,128]{3,2,1,0:T(8,128)S(1)} %collective-permute-done.8.low1, f32[2,7,8,128]{3,2,1,0:T(8,128)S(1)} %collective-permute-done.9.low2, ...), custom_call_target="tpu_custom_call" | custom-call | tf_op jit(solution)/shard_map/expand/pallas_call | solution.py:206
  (15 shorter events, 0.1 us)
Async XLA Ops:
  0.0 1.2 %copy-start.3 = (bf16[1,64,8192]{2,1,0:T(8,128)(2,1)S(1)}, bf16[1,64,8192]{2,1,0:T(8,128)(2,1)}, u32[]{:S(2)}) copy-start(bf16[1,64,8192]{2,1,0:T(8,128)(2,1)} %param.10) | copy-start | bytes 3145732
  1.2 25.6 %copy-start.4 = (bf16[1,64,4096]{2,1,0:T(8,128)(2,1)S(1)}, bf16[1,64,4096]{2,1,0:T(8,128)(2,1)}, u32[]{:S(2)}) copy-start(bf16[1,64,4096]{2,1,0:T(8,128)(2,1)} %up_ref) | copy-start | bytes 1572868
  1.3 8.0 %collective-permute-start = (bf16[8,8192]{1,0:T(8,128)(2,1)S(1)}, bf16[8,8192]{1,0:T(8,128)(2,1)S(1)}, u32[]{:S(2)}, u32[]{:S(2)}) collective-permute-start(bf16[8,8192]{1,0:T(8,128)(2,1)S(1)} %get-tuple-element.35), channel_id=1, source_target_pairs={{0,2},{1,3},{2,4},{3,5},{4,6},{5,7},{6,0},{7,1},{8,10},{9,11},{10,... | collective-permute-start | bytes 393224 | tf_op jit(solution)/shard_map/ppermute | solution.py:66
  2.9 7.8 %collective-permute-start.1 = (bf16[8,8192]{1,0:T(8,128)(2,1)S(1)}, bf16[8,8192]{1,0:T(8,128)(2,1)S(1)}, u32[]{:S(2)}, u32[]{:S(2)}) collective-permute-start(bf16[8,8192]{1,0:T(8,128)(2,1)S(1)} %get-tuple-element.36), channel_id=1, source_target_pairs={{0,6},{1,7},{2,0},{3,1},{4,2},{5,3},{6,4},{7,5},{8,14},{9,15},{10,... | collective-permute-start | bytes 393224 | tf_op jit(solution)/shard_map/ppermute | solution.py:66
  4.6 7.8 %collective-permute-start.2 = (bf16[8,8192]{1,0:T(8,128)(2,1)S(1)}, bf16[8,8192]{1,0:T(8,128)(2,1)S(1)}, u32[]{:S(2)}, u32[]{:S(2)}) collective-permute-start(bf16[8,8192]{1,0:T(8,128)(2,1)S(1)} %get-tuple-element.37), channel_id=1, source_target_pairs={{0,3},{1,2},{2,5},{3,4},{4,7},{5,6},{6,1},{7,0},{8,11},{9,10},{10,... | collective-permute-start | bytes 393224 | tf_op jit(solution)/shard_map/ppermute | solution.py:66
  4.6 11.1 %collective-permute-start.3 = (bf16[8,8192]{1,0:T(8,128)(2,1)S(1)}, bf16[8,8192]{1,0:T(8,128)(2,1)S(1)}, u32[]{:S(2)}, u32[]{:S(2)}) collective-permute-start(bf16[8,8192]{1,0:T(8,128)(2,1)S(1)} %get-tuple-element.38), channel_id=1, source_target_pairs={{0,7},{1,6},{2,1},{3,0},{4,3},{5,2},{6,5},{7,4},{8,15},{9,14},{10,... | collective-permute-start | bytes 393224 | tf_op jit(solution)/shard_map/ppermute | solution.py:66
  7.6 8.1 %collective-permute-start.4 = (bf16[8,8192]{1,0:T(8,128)(2,1)S(1)}, bf16[8,8192]{1,0:T(8,128)(2,1)S(1)}, u32[]{:S(2)}, u32[]{:S(2)}) collective-permute-start(bf16[8,8192]{1,0:T(8,128)(2,1)S(1)} %get-tuple-element.39), channel_id=1, source_target_pairs={{0,4},{1,5},{2,6},{3,7},{4,0},{5,1},{6,2},{7,3},{8,12},{9,13},{10,... | collective-permute-start | bytes 393224 | tf_op jit(solution)/shard_map/ppermute | solution.py:66
  9.3 7.4 %collective-permute-start.5 = (bf16[8,8192]{1,0:T(8,128)(2,1)S(1)}, bf16[8,8192]{1,0:T(8,128)(2,1)S(1)}, u32[]{:S(2)}, u32[]{:S(2)}) collective-permute-start(bf16[8,8192]{1,0:T(8,128)(2,1)S(1)} %get-tuple-element.40), channel_id=1, source_target_pairs={{0,5},{1,4},{2,7},{3,6},{4,1},{5,0},{6,3},{7,2},{8,13},{9,12},{10,... | collective-permute-start | bytes 393224 | tf_op jit(solution)/shard_map/ppermute | solution.py:66
  10.8 5.9 %collective-permute-start.6 = (bf16[8,8192]{1,0:T(8,128)(2,1)S(1)}, bf16[8,8192]{1,0:T(8,128)(2,1)S(1)}, u32[]{:S(2)}, u32[]{:S(2)}) collective-permute-start(bf16[8,8192]{1,0:T(8,128)(2,1)S(1)} %get-tuple-element.41), channel_id=1, source_target_pairs={{0,1},{1,0},{2,3},{3,2},{4,5},{5,4},{6,7},{7,6},{8,9},{9,8},{10,11... | collective-permute-start | bytes 393224 | tf_op jit(solution)/shard_map/ppermute | solution.py:66
  17.5 1.3 %copy-start = (bf16[16,8,8192]{2,1,0:T(8,128)(2,1)}, bf16[16,8,8192]{2,1,0:T(8,128)(2,1)S(1)}, u32[]{:S(2)}) copy-start(bf16[16,8,8192]{2,1,0:T(8,128)(2,1)S(1)} %pick_down.1) | copy-start | bytes 6291460
  18.8 38.7 %all-to-all-start = ((bf16[16,8,8192]{2,1,0:T(8,128)(2,1)}), bf16[16,8,8192]{2,1,0:T(8,128)(2,1)S(1)}, u32[]{:S(2)}, u32[]{:S(2)}) async-start(bf16[16,8,8192]{2,1,0:T(8,128)(2,1)} %copy-done), calls=%async_computation | async-start | bytes 4194304 | tf_op jit(solution)/shard_map/all_to_all | solution.py:245
  26.9 6.3 %collective-permute-start.11 = (bf16[64,512]{1,0:T(8,128)(2,1)S(1)}, bf16[64,512]{1,0:T(8,128)(2,1)S(1)}, u32[]{:S(2)}, u32[]{:S(2)}) collective-permute-start(bf16[64,512]{1,0:T(8,128)(2,1)S(1)} %get-tuple-element.47), channel_id=1, source_target_pairs={{0,2},{1,3},{2,4},{3,5},{4,6},{5,7},{6,0},{7,1},{8,10},{9,11},{10,... | collective-permute-start | bytes 196616 | tf_op jit(solution)/shard_map/ppermute | solution.py:66
  28.4 7.2 %collective-permute-start.12 = (bf16[64,512]{1,0:T(8,128)(2,1)S(1)}, bf16[64,512]{1,0:T(8,128)(2,1)S(1)}, u32[]{:S(2)}, u32[]{:S(2)}) collective-permute-start(bf16[64,512]{1,0:T(8,128)(2,1)S(1)} %get-tuple-element.48), channel_id=1, source_target_pairs={{0,6},{1,7},{2,0},{3,1},{4,2},{5,3},{6,4},{7,5},{8,14},{9,15},{10,... | collective-permute-start | bytes 196616 | tf_op jit(solution)/shard_map/ppermute | solution.py:66
  30.2 23.8 %collective-permute-start.13 = (bf16[64,512]{1,0:T(8,128)(2,1)S(1)}, bf16[64,512]{1,0:T(8,128)(2,1)S(1)}, u32[]{:S(2)}, u32[]{:S(2)}) collective-permute-start(bf16[64,512]{1,0:T(8,128)(2,1)S(1)} %get-tuple-element.49), channel_id=1, source_target_pairs={{0,3},{1,2},{2,5},{3,4},{4,7},{5,6},{6,1},{7,0},{8,11},{9,10},{10,... | collective-permute-start | bytes 196616 | tf_op jit(solution)/shard_map/ppermute | solution.py:66
  30.2 23.8 %collective-permute-start.14 = (bf16[64,512]{1,0:T(8,128)(2,1)S(1)}, bf16[64,512]{1,0:T(8,128)(2,1)S(1)}, u32[]{:S(2)}, u32[]{:S(2)}) collective-permute-start(bf16[64,512]{1,0:T(8,128)(2,1)S(1)} %get-tuple-element.50), channel_id=1, source_target_pairs={{0,7},{1,6},{2,1},{3,0},{4,3},{5,2},{6,5},{7,4},{8,15},{9,14},{10,... | collective-permute-start | bytes 196616 | tf_op jit(solution)/shard_map/ppermute | solution.py:66
  33.2 20.9 %collective-permute-start.15 = (bf16[64,512]{1,0:T(8,128)(2,1)S(1)}, bf16[64,512]{1,0:T(8,128)(2,1)S(1)}, u32[]{:S(2)}, u32[]{:S(2)}) collective-permute-start(bf16[64,512]{1,0:T(8,128)(2,1)S(1)} %get-tuple-element.51), channel_id=1, source_target_pairs={{0,4},{1,5},{2,6},{3,7},{4,0},{5,1},{6,2},{7,3},{8,12},{9,13},{10,... | collective-permute-start | bytes 196616 | tf_op jit(solution)/shard_map/ppermute | solution.py:66
  33.2 20.9 %collective-permute-start.16 = (bf16[64,512]{1,0:T(8,128)(2,1)S(1)}, bf16[64,512]{1,0:T(8,128)(2,1)S(1)}, u32[]{:S(2)}, u32[]{:S(2)}) collective-permute-start(bf16[64,512]{1,0:T(8,128)(2,1)S(1)} %get-tuple-element.52), channel_id=1, source_target_pairs={{0,5},{1,4},{2,7},{3,6},{4,1},{5,0},{6,3},{7,2},{8,13},{9,12},{10,... | collective-permute-start | bytes 196616 | tf_op jit(solution)/shard_map/ppermute | solution.py:66
  35.6 18.4 %collective-permute-start.17 = (bf16[64,512]{1,0:T(8,128)(2,1)S(1)}, bf16[64,512]{1,0:T(8,128)(2,1)S(1)}, u32[]{:S(2)}, u32[]{:S(2)}) collective-permute-start(bf16[64,512]{1,0:T(8,128)(2,1)S(1)} %get-tuple-element.53), channel_id=1, source_target_pairs={{0,1},{1,0},{2,3},{3,2},{4,5},{5,4},{6,7},{7,6},{8,9},{9,8},{10,11... | collective-permute-start | bytes 196616 | tf_op jit(solution)/shard_map/ppermute | solution.py:66
  54.7 1.0 %copy-start.1 = (bf16[16,64,512]{2,1,0:T(8,128)(2,1)}, bf16[16,64,512]{2,1,0:T(8,128)(2,1)S(1)}, u32[]{:S(2)}) copy-start(bf16[16,64,512]{2,1,0:T(8,128)(2,1)S(1)} %pick_up.1) | copy-start | bytes 3145732
  57.5 23.5 %all-to-all-start.1 = ((bf16[16,64,512]{2,1,0:T(8,128)(2,1)}), bf16[16,64,512]{2,1,0:T(8,128)(2,1)S(1)}, u32[]{:S(2)}, u32[]{:S(2)}) async-start(bf16[16,64,512]{2,1,0:T(8,128)(2,1)} %copy-done.1), calls=%async_computation.1 | async-start | bytes 2097152 | tf_op jit(solution)/shard_map/all_to_all | solution.py:250
  70.0 1.3 %collective-permute-start.7 = (f32[7,8,128]{2,1,0:T(8,128)S(1)}, f32[7,8,128]{2,1,0:T(8,128)S(1)}, u32[]{:S(2)}, u32[]{:S(2)}) collective-permute-start(f32[7,8,128]{2,1,0:T(8,128)S(1)} %shrink.1), channel_id=1, source_target_pairs={{0,1},{1,0},{2,3},{3,2},{4,5},{5,4},{6,7},{7,6},{8,9},{9,8},{10,11... | collective-permute-start | bytes 86024 | tf_op jit(solution)/shard_map/ppermute | solution.py:253
  71.2 9.7 %collective-permute-start.8 = (f32[2,7,8,128]{3,2,1,0:T(8,128)S(1)}, f32[2,7,8,128]{3,2,1,0:T(8,128)S(1)}, u32[]{:S(2)}, u32[]{:S(2)}) collective-permute-start(f32[2,7,8,128]{3,2,1,0:T(8,128)S(1)} %pad_maximum_fusion.low0), channel_id=1, source_target_pairs={{0,2},{1,3},{2,4},{3,5},{4,6},{5,7},{6,0},{7,1},{8,10},{9,11},{10,... | collective-permute-start | bytes 172040 | tf_op jit(solution)/shard_map/ppermute | solution.py:255
  71.6 9.3 %collective-permute-start.9 = (f32[2,7,8,128]{3,2,1,0:T(8,128)S(1)}, f32[2,7,8,128]{3,2,1,0:T(8,128)S(1)}, u32[]{:S(2)}, u32[]{:S(2)}) collective-permute-start(f32[2,7,8,128]{3,2,1,0:T(8,128)S(1)} %pad_maximum_fusion.low0), channel_id=1, source_target_pairs={{0,4},{1,5},{2,6},{3,7},{4,0},{5,1},{6,2},{7,3},{8,12},{9,13},{10,... | collective-permute-start | bytes 172040 | tf_op jit(solution)/shard_map/ppermute | solution.py:255
  74.6 6.3 %collective-permute-start.10 = (f32[2,7,8,128]{3,2,1,0:T(8,128)S(1)}, f32[2,7,8,128]{3,2,1,0:T(8,128)S(1)}, u32[]{:S(2)}, u32[]{:S(2)}) collective-permute-start(f32[2,7,8,128]{3,2,1,0:T(8,128)S(1)} %pad_maximum_fusion.low0), channel_id=1, source_target_pairs={{0,6},{1,7},{2,0},{3,1},{4,2},{5,3},{6,4},{7,5},{8,14},{9,15},{10,... | collective-permute-start | bytes 172040 | tf_op jit(solution)/shard_map/ppermute | solution.py:255
  81.0 1.5 %copy-start.2 = (f32[896,512]{1,0:T(8,128)S(1)}, f32[896,512]{1,0:T(8,128)}, u32[]{:S(2)}) copy-start(f32[896,512]{1,0:T(8,128)} %get-tuple-element.64.base_ref) | copy-start | bytes 5505028

commit v4 on v3

--- a/solution.py
+++ b/solution.py
@@ -181,37 +181,66 @@
     )(owner_rows, down_got, normed)
 
 
-def expand_kernel(row_ref, lane_ref, low0, low1, low2, low3, up_ref, base_ref, out_ref, full):
+def gather_kernel(lane_ref, low0, low1, low2, low3, base_hbm, low_ref, base_ref, full, sem):
+    copy = pltpu.make_async_copy(base_hbm, base_ref, sem)
+    copy.start()
     lows = (low0, low1, low2, low3)
     lane = lane_ref[0]
-    blocks, part, block = low0.shape[1:]
+    blocks, part, _ = low0.shape[1:]
     for dx in range(X):
         for dc in range(CORES):
             src = (lane // CORES - dx) % X * CORES + (lane % CORES - dc) % CORES
             rows = pl.ds(pl.multiple_of(src * part, part), part)
             for j in range(blocks):
                 full[j, rows, :] = lows[dx][dc, j]
-
     for j in range(blocks):
-        low = full[j].astype(jnp.bfloat16)
-        term = lax.dot_general(
-            low, up_ref[row_ref[j]], (((0,), (0,)), ((), ())), preferred_element_type=jnp.float32
-        )
-        rows = slice(j * block, (j + 1) * block)
+        low_ref[j] = full[j].T.astype(low_ref.dtype)
+    copy.wait()
+
+
+def gather_low(lane, lows, base):
+    blocks, part, block = lows[0].shape[1:]
+    shape = (blocks, part * LANES, block)
+    return pl.pallas_call(
+        gather_kernel,
+        in_specs=[SMEM] + [VMEM] * len(lows) + [ANY],
+        out_specs=[VMEM, VMEM],
+        out_shape=[
+            jax.ShapeDtypeStruct((blocks, block, part * LANES), jnp.bfloat16),
+            jax.ShapeDtypeStruct(base.shape, base.dtype),
+        ],
+        scratch_shapes=[pltpu.VMEM(shape, jnp.float32), pltpu.SemaphoreType.DMA],
+        compiler_params=pltpu.CompilerParams(vmem_limit_bytes=16 * 2**20),
+        name="gather_low",
+    )(lane, *lows, base)
+
+
+def expand_kernel(row_ref, low_ref, base_ref, up_ref, out_hbm, out_ref, sems):
+    blocks, block, _ = low_ref.shape
+    copies = []
+    for j in range(blocks):
+        rows = pl.ds(j * block, block)
+        term = jnp.dot(low_ref[j], up_ref[row_ref[j]], preferred_element_type=jnp.float32)
         out_ref[rows, :] = (base_ref[rows, :] + ADAPTER_SCALE * term).astype(out_ref.dtype)
-
-
-def expand(owner_rows, lane, lows, up_got, base):
-    blocks, part, block = lows[0].shape[1:]
+        copies.append(pltpu.make_async_copy(out_ref.at[rows], out_hbm.at[rows], sems.at[j]))
+        copies[j].start()
+    for copy in copies:
+        copy.wait()
+
+
+def expand(owner_rows, low, base, up_got):
     return pl.pallas_call(
         expand_kernel,
-        in_specs=[SMEM, SMEM] + [VMEM] * (len(lows) + 2),
-        out_specs=VMEM,
+        in_specs=[SMEM, VMEM, VMEM, VMEM],
+        out_specs=ANY,
         out_shape=jax.ShapeDtypeStruct(base.shape, jnp.bfloat16),
-        scratch_shapes=[pltpu.VMEM((blocks, part * LANES, block), jnp.float32)],
+        scratch_shapes=[
+            pltpu.VMEM(base.shape, jnp.bfloat16),
+            pltpu.SemaphoreType.DMA((low.shape[0],)),
+        ],
         compiler_params=pltpu.CompilerParams(vmem_limit_bytes=16 * 2**20),
         name="expand",
-    )(owner_rows, lane, *lows, up_got, base)
+    )(owner_rows, low, base, up_got)
 
 
 def shards(
@@ -253,7 +282,8 @@
     other = lax.ppermute(low, BOTH, lane_shift(groups, 0, 1))
     chip = jnp.stack([low, other])
     lows = [chip] + [lax.ppermute(chip, BOTH, lane_shift(groups, dx, 0)) for dx in range(1, X)]
-    return expand(owner_rows, lane_arr, lows, up_got, base)
+    low, base = gather_low(lane_arr, lows, base)
+    return expand(owner_rows, low, base, up_got)
 
 
 def solution(mesh):

time: 84.8 us -> 83.1 us (0.980)
  local copies, waits for them, and re-layouts: 5.2 us -> 2.73 us
  Pallas kernels: 27.5 us -> 28.6 us
    all_to_all x1, waiting for transfers between devices: 6.31 us -> 1.75 us  [shards(): lax.all_to_all(pick(wanted, up_row, 'pick_up'), 'req', 0, 0, tiled=True)]
    ppermute x3, waiting for transfers between devices: 0.01 us -> 4.17 us  [shards(): lax.ppermute(chip, BOTH, lane_shift(groups, dx, 0))]
    unnamed x10 -> x8, local copies, waits for them, and re-layouts: 5.01 us -> 2.54 us
    pallas_call x2, Pallas kernels: 1.4 us -> 2.39 us  [pick(): pl.pallas_call(pick_kernel, in_specs=[SMEM] + [VMEM] * LANES, out_specs=V...]
    pallas_call x1 -> x2, Pallas kernels: 1.93 us -> 2 us  [the longest x1 1.69 us: expand(): pl.pallas_call(expand_kernel, in_specs=[SMEM, VMEM, VMEM, VMEM], out_spec...]
  transfers between devices with their start and end apart: 20 -> 20, of which waited for: 5 -> 8; matrix products, arithmetic and copies ran while one was open for 1% -> 1% of each run, Pallas kernels for 29% -> 32%
where the time goes in v4:
time: 83.1 us; the launch traced here: 82.7 us
  starting transfers between devices  37 us (45%)
  Pallas kernels  28.6 us (34%)
  waiting for transfers between devices  13.2 us (16%)
  local copies, waits for them, and re-layouts  2.73 us (3%)
  other arithmetic  1.05 us (1%)
    ppermute x14, starting transfers between devices, spread(): lax.ppermute(pieces[k], BOTH, lane_shift(groups, k // CORES, k % CORES))  19.9 us
    pallas_call x1, Pallas kernels, norm_base(): pl.pallas_call(norm_base_kernel, grid=(rows // NORM_ROWS,), in_specs=[pl....  17.3 us
    all_to_all x1, starting transfers between devices, shards(): down_got = lax.all_to_all(down_send, 'req', 0, 0, tiled=True)  8.17 us
    pallas_call x1, Pallas kernels, shrink(): pl.pallas_call(shrink_kernel, in_specs=[SMEM, VMEM, ANY], out_specs=VMEM,...  6.83 us
    all_to_all x1, starting transfers between devices, shards(): lax.all_to_all(pick(wanted, up_row, 'pick_up'), 'req', 0, 0, tiled=True)  5.54 us
    ppermute x14, waiting for transfers between devices, spread(): lax.ppermute(pieces[k], BOTH, lane_shift(groups, k // CORES, k % CORES))  4.37 us
    ppermute x3, waiting for transfers between devices, shards(): lax.ppermute(chip, BOTH, lane_shift(groups, dx, 0))  4.17 us
    ppermute x3, starting transfers between devices, shards(): lax.ppermute(chip, BOTH, lane_shift(groups, dx, 0))  3.34 us
  transfers between devices with their start and end apart: 20, of which 8 were waited for; matrix products, arithmetic and copies ran while one was open for 1% of the time, Pallas kernels for 32%

profile of v4, /device:TPU:0, one launch (start us, length us, event | category | flops | bytes accessed | tf_op | source)
XLA Modules:
  0.0 82.7 jit_solution(14145882318931144280)
XLA Ops:
  0.0 1.2 %copy-done.2 = bf16[1,64,8192]{2,1,0:T(8,128)(2,1)S(1)} copy-done((bf16[1,64,8192]{2,1,0:T(8,128)(2,1)S(1)}, bf16[1,64,8192]{2,1,0:T(8,128)(2,1)}, u32[]{:S(2)}) %copy-start.2) | copy-done | bytes 1048600
  1.2 0.1 split_down.1
  1.3 1.6 %collective-permute-start = (bf16[8,8192]{1,0:T(8,128)(2,1)S(1)}, bf16[8,8192]{1,0:T(8,128)(2,1)S(1)}, u32[]{:S(2)}, u32[]{:S(2)}) collective-permute-start(bf16[8,8192]{1,0:T(8,128)(2,1)S(1)} %get-tuple-element.37), channel_id=1, source_target_pairs={{0,2},{1,3},{2,4},{3,5},{4,6},{5,7},{6,0},{7,1},{8,10},{9,11},{10,... | collective-permute-start | bytes 393224 | tf_op jit(solution)/shard_map/ppermute | solution.py:66
  2.9 1.7 %collective-permute-start.1 = (bf16[8,8192]{1,0:T(8,128)(2,1)S(1)}, bf16[8,8192]{1,0:T(8,128)(2,1)S(1)}, u32[]{:S(2)}, u32[]{:S(2)}) collective-permute-start(bf16[8,8192]{1,0:T(8,128)(2,1)S(1)} %get-tuple-element.38), channel_id=1, source_target_pairs={{0,6},{1,7},{2,0},{3,1},{4,2},{5,3},{6,4},{7,5},{8,14},{9,15},{10,... | collective-permute-start | bytes 393224 | tf_op jit(solution)/shard_map/ppermute | solution.py:66
  4.6 0.0 collective-permute-start.2
  4.6 3.0 %collective-permute-start.3 = (bf16[8,8192]{1,0:T(8,128)(2,1)S(1)}, bf16[8,8192]{1,0:T(8,128)(2,1)S(1)}, u32[]{:S(2)}, u32[]{:S(2)}) collective-permute-start(bf16[8,8192]{1,0:T(8,128)(2,1)S(1)} %get-tuple-element.40), channel_id=1, source_target_pairs={{0,7},{1,6},{2,1},{3,0},{4,3},{5,2},{6,5},{7,4},{8,15},{9,14},{10,... | collective-permute-start | bytes 393224 | tf_op jit(solution)/shard_map/ppermute | solution.py:66
  7.6 0.7 collective-permute-start.4
  8.2 1.0 %select_reduce_fusion = s32[16,7]{0,1:T(8,128)S(1)} fusion(s32[128]{0:T(128)} %param.13, s32[16,7]{0,1:T(8,128)} %param.12), kind=kLoop, calls=%fused_computation.1 | loop fusion | flops 42896 | bytes 1408 | tf_op jit(solution)/shard_map/reduce_sum | solution.py:266
  9.3 0.0 collective-permute-done.rest_0_
  9.3 1.5 %collective-permute-start.5 = (bf16[8,8192]{1,0:T(8,128)(2,1)S(1)}, bf16[8,8192]{1,0:T(8,128)(2,1)S(1)}, u32[]{:S(2)}, u32[]{:S(2)}) collective-permute-start(bf16[8,8192]{1,0:T(8,128)(2,1)S(1)} %get-tuple-element.42), channel_id=1, source_target_pairs={{0,5},{1,4},{2,7},{3,6},{4,1},{5,0},{6,3},{7,2},{8,13},{9,12},{10,... | collective-permute-start | bytes 393224 | tf_op jit(solution)/shard_map/ppermute | solution.py:66
  10.8 0.0 collective-permute-done.1.rest_1_
  10.8 1.5 %collective-permute-start.6 = (bf16[8,8192]{1,0:T(8,128)(2,1)S(1)}, bf16[8,8192]{1,0:T(8,128)(2,1)S(1)}, u32[]{:S(2)}, u32[]{:S(2)}) collective-permute-start(bf16[8,8192]{1,0:T(8,128)(2,1)S(1)} %get-tuple-element.43), channel_id=1, source_target_pairs={{0,1},{1,0},{2,3},{3,2},{4,5},{5,4},{6,7},{7,6},{8,9},{9,8},{10,11... | collective-permute-start | bytes 393224 | tf_op jit(solution)/shard_map/ppermute | solution.py:66
  12.4 0.0 collective-permute-done.2.rest_2_
  12.4 3.3 %collective-permute-done.3.rest_3_ = bf16[8,8192]{1,0:T(8,128)(2,1)S(1)} collective-permute-done((bf16[8,8192]{1,0:T(8,128)(2,1)S(1)}, bf16[8,8192]{1,0:T(8,128)(2,1)S(1)}, u32[]{:S(2)}, u32[]{:S(2)}) %collective-permute-start.3) | collective-permute-done | bytes 131104 | tf_op jit(solution)/shard_map/ppermute | solution.py:66
  15.7 0.0 collective-permute-done.4.rest_4_
  15.7 1.0 %collective-permute-done.5.rest_5_ = bf16[8,8192]{1,0:T(8,128)(2,1)S(1)} collective-permute-done((bf16[8,8192]{1,0:T(8,128)(2,1)S(1)}, bf16[8,8192]{1,0:T(8,128)(2,1)S(1)}, u32[]{:S(2)}, u32[]{:S(2)}) %collective-permute-start.5) | collective-permute-done | bytes 131104 | tf_op jit(solution)/shard_map/ppermute | solution.py:66
  16.7 0.7 pick_down.1
  17.5 1.3 %copy-done = bf16[16,8,8192]{2,1,0:T(8,128)(2,1)} copy-done((bf16[16,8,8192]{2,1,0:T(8,128)(2,1)}, bf16[16,8,8192]{2,1,0:T(8,128)(2,1)S(1)}, u32[]{:S(2)}) %copy-start) | copy-done | bytes 2097176
  18.8 8.2 %all-to-all-start = ((bf16[16,8,8192]{2,1,0:T(8,128)(2,1)}), bf16[16,8,8192]{2,1,0:T(8,128)(2,1)S(1)}, u32[]{:S(2)}, u32[]{:S(2)}) async-start(bf16[16,8,8192]{2,1,0:T(8,128)(2,1)} %copy-done), calls=%async_computation | async-start | bytes 4194304 | tf_op jit(solution)/shard_map/all_to_all | solution.py:274
  27.0 0.1 split_up.1
  27.0 1.5 %collective-permute-start.11 = (bf16[64,512]{1,0:T(8,128)(2,1)S(1)}, bf16[64,512]{1,0:T(8,128)(2,1)S(1)}, u32[]{:S(2)}, u32[]{:S(2)}) collective-permute-start(bf16[64,512]{1,0:T(8,128)(2,1)S(1)} %get-tuple-element.49), channel_id=1, source_target_pairs={{0,2},{1,3},{2,4},{3,5},{4,6},{5,7},{6,0},{7,1},{8,10},{9,11},{10,... | collective-permute-start | bytes 196616 | tf_op jit(solution)/shard_map/ppermute | solution.py:66
  28.5 1.8 %collective-permute-start.12 = (bf16[64,512]{1,0:T(8,128)(2,1)S(1)}, bf16[64,512]{1,0:T(8,128)(2,1)S(1)}, u32[]{:S(2)}, u32[]{:S(2)}) collective-permute-start(bf16[64,512]{1,0:T(8,128)(2,1)S(1)} %get-tuple-element.50), channel_id=1, source_target_pairs={{0,6},{1,7},{2,0},{3,1},{4,2},{5,3},{6,4},{7,5},{8,14},{9,15},{10,... | collective-permute-start | bytes 196616 | tf_op jit(solution)/shard_map/ppermute | solution.py:66
  30.3 0.0 collective-permute-start.13
  30.3 3.0 %collective-permute-start.14 = (bf16[64,512]{1,0:T(8,128)(2,1)S(1)}, bf16[64,512]{1,0:T(8,128)(2,1)S(1)}, u32[]{:S(2)}, u32[]{:S(2)}) collective-permute-start(bf16[64,512]{1,0:T(8,128)(2,1)S(1)} %get-tuple-element.52), channel_id=1, source_target_pairs={{0,7},{1,6},{2,1},{3,0},{4,3},{5,2},{6,5},{7,4},{8,15},{9,14},{10,... | collective-permute-start | bytes 196616 | tf_op jit(solution)/shard_map/ppermute | solution.py:66
  33.3 0.0 collective-permute-start.15
  33.3 0.0 collective-permute-done.11.rest_0_
  33.3 2.5 %collective-permute-start.16 = (bf16[64,512]{1,0:T(8,128)(2,1)S(1)}, bf16[64,512]{1,0:T(8,128)(2,1)S(1)}, u32[]{:S(2)}, u32[]{:S(2)}) collective-permute-start(bf16[64,512]{1,0:T(8,128)(2,1)S(1)} %get-tuple-element.54), channel_id=1, source_target_pairs={{0,5},{1,4},{2,7},{3,6},{4,1},{5,0},{6,3},{7,2},{8,13},{9,12},{10,... | collective-permute-start | bytes 196616 | tf_op jit(solution)/shard_map/ppermute | solution.py:66
  35.8 0.0 collective-permute-done.12.rest_1_
  35.8 1.2 %collective-permute-start.17 = (bf16[64,512]{1,0:T(8,128)(2,1)S(1)}, bf16[64,512]{1,0:T(8,128)(2,1)S(1)}, u32[]{:S(2)}, u32[]{:S(2)}) collective-permute-start(bf16[64,512]{1,0:T(8,128)(2,1)S(1)} %get-tuple-element.55), channel_id=1, source_target_pairs={{0,1},{1,0},{2,3},{3,2},{4,5},{5,4},{6,7},{7,6},{8,9},{9,8},{10,11... | collective-permute-start | bytes 196616 | tf_op jit(solution)/shard_map/ppermute | solution.py:66
  37.0 17.3 %norm_base.1 = (bf16[896,8192]{1,0:T(8,128)(2,1)}, f32[896,512]{1,0:T(8,128)}) custom-call(bf16[896,8192]{1,0:T(8,128)(2,1)} %x_ref, f32[1,8192]{1,0:T(1,128)} %bitcast.8, bf16[8192,512]{1,0:T(8,128)(2,1)} %weight_ref.1), custom_call_target="tpu_custom_call" | custom-call | flops 15032385536 | bytes 37748736 | tf_op jit(solution)/shard_map/norm_base/pallas_call | solution.py:117
  54.2 0.0 collective-permute-done.15.rest_4_
  54.2 0.0 collective-permute-done.16.rest_5_
  54.3 1.6 %pick_up.1 = bf16[16,64,512]{2,1,0:T(8,128)(2,1)} custom-call(s32[16]{0:T(128)S(1)} %fusion.5.pick_ref, bf16[64,512]{1,0:T(8,128)(2,1)S(1)} %collective-permute-done.11.rest_0_, bf16[64,512]{1,0:T(8,128)(2,1)S(1)} %collective-permute-done.12.rest_1_, bf16[64,512]{1,0:T(8,128)(2,1)S(1)} %collective-permute-done.13.rest_2_, ...), custom_call_target="tpu_custom_call" | custom-call | tf_op jit(solution)/shard_map/pick_up/pallas_call | solution.py:81
  55.9 1.7 %all-to-all-done.down_ref = bf16[16,8,8192]{2,1,0:T(8,128)(2,1)S(1)} async-done(((bf16[16,8,8192]{2,1,0:T(8,128)(2,1)}), bf16[16,8,8192]{2,1,0:T(8,128)(2,1)S(1)}, u32[]{:S(2)}, u32[]{:S(2)}) %all-to-all-start) | async-done | bytes 2097184 | tf_op jit(solution)/shard_map/all_to_all | solution.py:274
  57.6 5.5 %all-to-all-start.1 = ((bf16[16,64,512]{2,1,0:T(8,128)(2,1)}), bf16[16,64,512]{2,1,0:T(8,128)(2,1)S(1)}, u32[]{:S(2)}, u32[]{:S(2)}) async-start(bf16[16,64,512]{2,1,0:T(8,128)(2,1)} %pick_up.1), calls=%async_computation.1 | async-start | bytes 2097152 | tf_op jit(solution)/shard_map/all_to_all | solution.py:279
  63.1 0.2 dynamic-slice_reduce_fusion
  63.3 6.8 %shrink.1 = f32[7,8,128]{2,1,0:T(8,128)S(1)} custom-call(s32[7]{0:T(128)S(1)} %and_select_fusion.4.row_ref, bf16[16,8,8192]{2,1,0:T(8,128)(2,1)S(1)} %all-to-all-done.down_ref, bf16[896,8192]{1,0:T(8,128)(2,1)} %get-tuple-element.47.normed_hbm), custom_call_target="tpu_custom_call" | custom-call | flops 3758096384 | bytes 14680064 | tf_op jit(solution)/shard_map/shrink/pallas_call | solution.py:170
  70.2 0.1 collective-permute-start.7
  70.3 1.2 %collective-permute-done.7 = f32[7,8,128]{2,1,0:T(8,128)S(1)} collective-permute-done((f32[7,8,128]{2,1,0:T(8,128)S(1)}, f32[7,8,128]{2,1,0:T(8,128)S(1)}, u32[]{:S(2)}, u32[]{:S(2)}) %collective-permute-start.7) | collective-permute-done | bytes 28704 | tf_op jit(solution)/shard_map/ppermute | solution.py:282
  71.5 0.3 collective-permute-start.8
  71.8 3.0 %collective-permute-start.9 = (f32[2,7,8,128]{3,2,1,0:T(8,128)S(1)}, f32[2,7,8,128]{3,2,1,0:T(8,128)S(1)}, u32[]{:S(2)}, u32[]{:S(2)}) collective-permute-start(f32[2,7,8,128]{3,2,1,0:T(8,128)S(1)} %pad_maximum_fusion.low0), channel_id=1, source_target_pairs={{0,4},{1,5},{2,6},{3,7},{4,0},{5,1},{6,2},{7,3},{8,12},{9,13},{10,... | collective-permute-start | bytes 172040 | tf_op jit(solution)/shard_map/ppermute | solution.py:284
  74.8 0.0 collective-permute-start.10
  74.8 2.6 %collective-permute-done.8.low1 = f32[2,7,8,128]{3,2,1,0:T(8,128)S(1)} collective-permute-done((f32[2,7,8,128]{3,2,1,0:T(8,128)S(1)}, f32[2,7,8,128]{3,2,1,0:T(8,128)S(1)}, u32[]{:S(2)}, u32[]{:S(2)}) %collective-permute-start.8) | collective-permute-done | bytes 57376 | tf_op jit(solution)/shard_map/ppermute | solution.py:284
  77.4 0.6 collective-permute-done.9.low2
  78.0 1.0 %collective-permute-done.10.low3 = f32[2,7,8,128]{3,2,1,0:T(8,128)S(1)} collective-permute-done((f32[2,7,8,128]{3,2,1,0:T(8,128)S(1)}, f32[2,7,8,128]{3,2,1,0:T(8,128)S(1)}, u32[]{:S(2)}, u32[]{:S(2)}) %collective-permute-start.10) | collective-permute-done | bytes 57376 | tf_op jit(solution)/shard_map/ppermute | solution.py:284
  79.0 0.3 gather_low.1
  79.3 1.7 %all-to-all-done.1.up_ref = bf16[16,64,512]{2,1,0:T(8,128)(2,1)S(1)} async-done(((bf16[16,64,512]{2,1,0:T(8,128)(2,1)}), bf16[16,64,512]{2,1,0:T(8,128)(2,1)S(1)}, u32[]{:S(2)}, u32[]{:S(2)}) %all-to-all-start.1) | async-done | bytes 1048608 | tf_op jit(solution)/shard_map/all_to_all | solution.py:279
  81.1 1.7 %expand.1 = bf16[896,512]{1,0:T(8,128)(2,1)} custom-call(s32[7]{0:T(128)S(1)} %and_select_fusion.4.row_ref, bf16[7,128,64]{2,1,0:T(8,128)(2,1)S(1)} %get-tuple-element.59.low_ref, f32[896,512]{1,0:T(8,128)S(1)} %get-tuple-element.60.base_ref, bf16[16,64,512]{2,1,0:T(8,128)(2,1)S(1)} %all-to-all-done.1.up_ref), custom_call_target="tpu_custom_call" | custom-call | tf_op jit(solution)/shard_map/expand/pallas_call | solution.py:232
  (14 shorter events, 0.1 us)
Async XLA Ops:
  0.0 1.2 %copy-start.2 = (bf16[1,64,8192]{2,1,0:T(8,128)(2,1)S(1)}, bf16[1,64,8192]{2,1,0:T(8,128)(2,1)}, u32[]{:S(2)}) copy-start(bf16[1,64,8192]{2,1,0:T(8,128)(2,1)} %param.10) | copy-start | bytes 3145732
  1.3 8.0 %collective-permute-start = (bf16[8,8192]{1,0:T(8,128)(2,1)S(1)}, bf16[8,8192]{1,0:T(8,128)(2,1)S(1)}, u32[]{:S(2)}, u32[]{:S(2)}) collective-permute-start(bf16[8,8192]{1,0:T(8,128)(2,1)S(1)} %get-tuple-element.37), channel_id=1, source_target_pairs={{0,2},{1,3},{2,4},{3,5},{4,6},{5,7},{6,0},{7,1},{8,10},{9,11},{10,... | collective-permute-start | bytes 393224 | tf_op jit(solution)/shard_map/ppermute | solution.py:66
  2.9 7.8 %collective-permute-start.1 = (bf16[8,8192]{1,0:T(8,128)(2,1)S(1)}, bf16[8,8192]{1,0:T(8,128)(2,1)S(1)}, u32[]{:S(2)}, u32[]{:S(2)}) collective-permute-start(bf16[8,8192]{1,0:T(8,128)(2,1)S(1)} %get-tuple-element.38), channel_id=1, source_target_pairs={{0,6},{1,7},{2,0},{3,1},{4,2},{5,3},{6,4},{7,5},{8,14},{9,15},{10,... | collective-permute-start | bytes 393224 | tf_op jit(solution)/shard_map/ppermute | solution.py:66
  4.6 7.8 %collective-permute-start.2 = (bf16[8,8192]{1,0:T(8,128)(2,1)S(1)}, bf16[8,8192]{1,0:T(8,128)(2,1)S(1)}, u32[]{:S(2)}, u32[]{:S(2)}) collective-permute-start(bf16[8,8192]{1,0:T(8,128)(2,1)S(1)} %get-tuple-element.39), channel_id=1, source_target_pairs={{0,3},{1,2},{2,5},{3,4},{4,7},{5,6},{6,1},{7,0},{8,11},{9,10},{10,... | collective-permute-start | bytes 393224 | tf_op jit(solution)/shard_map/ppermute | solution.py:66
  4.6 11.1 %collective-permute-start.3 = (bf16[8,8192]{1,0:T(8,128)(2,1)S(1)}, bf16[8,8192]{1,0:T(8,128)(2,1)S(1)}, u32[]{:S(2)}, u32[]{:S(2)}) collective-permute-start(bf16[8,8192]{1,0:T(8,128)(2,1)S(1)} %get-tuple-element.40), channel_id=1, source_target_pairs={{0,7},{1,6},{2,1},{3,0},{4,3},{5,2},{6,5},{7,4},{8,15},{9,14},{10,... | collective-permute-start | bytes 393224 | tf_op jit(solution)/shard_map/ppermute | solution.py:66
  7.6 8.1 %collective-permute-start.4 = (bf16[8,8192]{1,0:T(8,128)(2,1)S(1)}, bf16[8,8192]{1,0:T(8,128)(2,1)S(1)}, u32[]{:S(2)}, u32[]{:S(2)}) collective-permute-start(bf16[8,8192]{1,0:T(8,128)(2,1)S(1)} %get-tuple-element.41), channel_id=1, source_target_pairs={{0,4},{1,5},{2,6},{3,7},{4,0},{5,1},{6,2},{7,3},{8,12},{9,13},{10,... | collective-permute-start | bytes 393224 | tf_op jit(solution)/shard_map/ppermute | solution.py:66
  9.3 7.4 %collective-permute-start.5 = (bf16[8,8192]{1,0:T(8,128)(2,1)S(1)}, bf16[8,8192]{1,0:T(8,128)(2,1)S(1)}, u32[]{:S(2)}, u32[]{:S(2)}) collective-permute-start(bf16[8,8192]{1,0:T(8,128)(2,1)S(1)} %get-tuple-element.42), channel_id=1, source_target_pairs={{0,5},{1,4},{2,7},{3,6},{4,1},{5,0},{6,3},{7,2},{8,13},{9,12},{10,... | collective-permute-start | bytes 393224 | tf_op jit(solution)/shard_map/ppermute | solution.py:66
  10.8 5.9 %collective-permute-start.6 = (bf16[8,8192]{1,0:T(8,128)(2,1)S(1)}, bf16[8,8192]{1,0:T(8,128)(2,1)S(1)}, u32[]{:S(2)}, u32[]{:S(2)}) collective-permute-start(bf16[8,8192]{1,0:T(8,128)(2,1)S(1)} %get-tuple-element.43), channel_id=1, source_target_pairs={{0,1},{1,0},{2,3},{3,2},{4,5},{5,4},{6,7},{7,6},{8,9},{9,8},{10,11... | collective-permute-start | bytes 393224 | tf_op jit(solution)/shard_map/ppermute | solution.py:66
  17.5 1.3 %copy-start = (bf16[16,8,8192]{2,1,0:T(8,128)(2,1)}, bf16[16,8,8192]{2,1,0:T(8,128)(2,1)S(1)}, u32[]{:S(2)}) copy-start(bf16[16,8,8192]{2,1,0:T(8,128)(2,1)S(1)} %pick_down.1) | copy-start | bytes 6291460
  18.8 8.2 %copy-start.3 = (bf16[1,64,4096]{2,1,0:T(8,128)(2,1)S(1)}, bf16[1,64,4096]{2,1,0:T(8,128)(2,1)}, u32[]{:S(2)}) copy-start(bf16[1,64,4096]{2,1,0:T(8,128)(2,1)} %up_ref) | copy-start | bytes 1572868
  18.8 38.8 %all-to-all-start = ((bf16[16,8,8192]{2,1,0:T(8,128)(2,1)}), bf16[16,8,8192]{2,1,0:T(8,128)(2,1)S(1)}, u32[]{:S(2)}, u32[]{:S(2)}) async-start(bf16[16,8,8192]{2,1,0:T(8,128)(2,1)} %copy-done), calls=%async_computation | async-start | bytes 4194304 | tf_op jit(solution)/shard_map/all_to_all | solution.py:274
  27.0 6.3 %collective-permute-start.11 = (bf16[64,512]{1,0:T(8,128)(2,1)S(1)}, bf16[64,512]{1,0:T(8,128)(2,1)S(1)}, u32[]{:S(2)}, u32[]{:S(2)}) collective-permute-start(bf16[64,512]{1,0:T(8,128)(2,1)S(1)} %get-tuple-element.49), channel_id=1, source_target_pairs={{0,2},{1,3},{2,4},{3,5},{4,6},{5,7},{6,0},{7,1},{8,10},{9,11},{10,... | collective-permute-start | bytes 196616 | tf_op jit(solution)/shard_map/ppermute | solution.py:66
  28.5 7.2 %collective-permute-start.12 = (bf16[64,512]{1,0:T(8,128)(2,1)S(1)}, bf16[64,512]{1,0:T(8,128)(2,1)S(1)}, u32[]{:S(2)}, u32[]{:S(2)}) collective-permute-start(bf16[64,512]{1,0:T(8,128)(2,1)S(1)} %get-tuple-element.50), channel_id=1, source_target_pairs={{0,6},{1,7},{2,0},{3,1},{4,2},{5,3},{6,4},{7,5},{8,14},{9,15},{10,... | collective-permute-start | bytes 196616 | tf_op jit(solution)/shard_map/ppermute | solution.py:66
  30.3 23.9 %collective-permute-start.13 = (bf16[64,512]{1,0:T(8,128)(2,1)S(1)}, bf16[64,512]{1,0:T(8,128)(2,1)S(1)}, u32[]{:S(2)}, u32[]{:S(2)}) collective-permute-start(bf16[64,512]{1,0:T(8,128)(2,1)S(1)} %get-tuple-element.51), channel_id=1, source_target_pairs={{0,3},{1,2},{2,5},{3,4},{4,7},{5,6},{6,1},{7,0},{8,11},{9,10},{10,... | collective-permute-start | bytes 196616 | tf_op jit(solution)/shard_map/ppermute | solution.py:66
  30.3 23.9 %collective-permute-start.14 = (bf16[64,512]{1,0:T(8,128)(2,1)S(1)}, bf16[64,512]{1,0:T(8,128)(2,1)S(1)}, u32[]{:S(2)}, u32[]{:S(2)}) collective-permute-start(bf16[64,512]{1,0:T(8,128)(2,1)S(1)} %get-tuple-element.52), channel_id=1, source_target_pairs={{0,7},{1,6},{2,1},{3,0},{4,3},{5,2},{6,5},{7,4},{8,15},{9,14},{10,... | collective-permute-start | bytes 196616 | tf_op jit(solution)/shard_map/ppermute | solution.py:66
  33.3 20.9 %collective-permute-start.15 = (bf16[64,512]{1,0:T(8,128)(2,1)S(1)}, bf16[64,512]{1,0:T(8,128)(2,1)S(1)}, u32[]{:S(2)}, u32[]{:S(2)}) collective-permute-start(bf16[64,512]{1,0:T(8,128)(2,1)S(1)} %get-tuple-element.53), channel_id=1, source_target_pairs={{0,4},{1,5},{2,6},{3,7},{4,0},{5,1},{6,2},{7,3},{8,12},{9,13},{10,... | collective-permute-start | bytes 196616 | tf_op jit(solution)/shard_map/ppermute | solution.py:66
  33.3 20.9 %collective-permute-start.16 = (bf16[64,512]{1,0:T(8,128)(2,1)S(1)}, bf16[64,512]{1,0:T(8,128)(2,1)S(1)}, u32[]{:S(2)}, u32[]{:S(2)}) collective-permute-start(bf16[64,512]{1,0:T(8,128)(2,1)S(1)} %get-tuple-element.54), channel_id=1, source_target_pairs={{0,5},{1,4},{2,7},{3,6},{4,1},{5,0},{6,3},{7,2},{8,13},{9,12},{10,... | collective-permute-start | bytes 196616 | tf_op jit(solution)/shard_map/ppermute | solution.py:66
  35.8 18.5 %collective-permute-start.17 = (bf16[64,512]{1,0:T(8,128)(2,1)S(1)}, bf16[64,512]{1,0:T(8,128)(2,1)S(1)}, u32[]{:S(2)}, u32[]{:S(2)}) collective-permute-start(bf16[64,512]{1,0:T(8,128)(2,1)S(1)} %get-tuple-element.55), channel_id=1, source_target_pairs={{0,1},{1,0},{2,3},{3,2},{4,5},{5,4},{6,7},{7,6},{8,9},{9,8},{10,11... | collective-permute-start | bytes 196616 | tf_op jit(solution)/shard_map/ppermute | solution.py:66
  57.6 23.5 %all-to-all-start.1 = ((bf16[16,64,512]{2,1,0:T(8,128)(2,1)}), bf16[16,64,512]{2,1,0:T(8,128)(2,1)S(1)}, u32[]{:S(2)}, u32[]{:S(2)}) async-start(bf16[16,64,512]{2,1,0:T(8,128)(2,1)} %pick_up.1), calls=%async_computation.1 | async-start | bytes 2097152 | tf_op jit(solution)/shard_map/all_to_all | solution.py:279
  63.3 15.7 %copy-start.1 = (f32[896,512]{1,0:T(8,128)S(1)}, f32[896,512]{1,0:T(8,128)}, u32[]{:S(2)}) copy-start(f32[896,512]{1,0:T(8,128)} %get-tuple-element.58.base_hbm) | copy-start | bytes 5505028
  70.2 1.3 %collective-permute-start.7 = (f32[7,8,128]{2,1,0:T(8,128)S(1)}, f32[7,8,128]{2,1,0:T(8,128)S(1)}, u32[]{:S(2)}, u32[]{:S(2)}) collective-permute-start(f32[7,8,128]{2,1,0:T(8,128)S(1)} %shrink.1), channel_id=1, source_target_pairs={{0,1},{1,0},{2,3},{3,2},{4,5},{5,4},{6,7},{7,6},{8,9},{9,8},{10,11... | collective-permute-start | bytes 86024 | tf_op jit(solution)/shard_map/ppermute | solution.py:282
  71.5 5.9 %collective-permute-start.8 = (f32[2,7,8,128]{3,2,1,0:T(8,128)S(1)}, f32[2,7,8,128]{3,2,1,0:T(8,128)S(1)}, u32[]{:S(2)}, u32[]{:S(2)}) collective-permute-start(f32[2,7,8,128]{3,2,1,0:T(8,128)S(1)} %pad_maximum_fusion.low0), channel_id=1, source_target_pairs={{0,2},{1,3},{2,4},{3,5},{4,6},{5,7},{6,0},{7,1},{8,10},{9,11},{10,... | collective-permute-start | bytes 172040 | tf_op jit(solution)/shard_map/ppermute | solution.py:284
  71.8 6.2 %collective-permute-start.9 = (f32[2,7,8,128]{3,2,1,0:T(8,128)S(1)}, f32[2,7,8,128]{3,2,1,0:T(8,128)S(1)}, u32[]{:S(2)}, u32[]{:S(2)}) collective-permute-start(f32[2,7,8,128]{3,2,1,0:T(8,128)S(1)} %pad_maximum_fusion.low0), channel_id=1, source_target_pairs={{0,4},{1,5},{2,6},{3,7},{4,0},{5,1},{6,2},{7,3},{8,12},{9,13},{10,... | collective-permute-start | bytes 172040 | tf_op jit(solution)/shard_map/ppermute | solution.py:284
  74.8 4.2 %collective-permute-start.10 = (f32[2,7,8,128]{3,2,1,0:T(8,128)S(1)}, f32[2,7,8,128]{3,2,1,0:T(8,128)S(1)}, u32[]{:S(2)}, u32[]{:S(2)}) collective-permute-start(f32[2,7,8,128]{3,2,1,0:T(8,128)S(1)} %pad_maximum_fusion.low0), channel_id=1, source_target_pairs={{0,6},{1,7},{2,0},{3,1},{4,2},{5,3},{6,4},{7,5},{8,14},{9,15},{10,... | collective-permute-start | bytes 172040 | tf_op jit(solution)/shard_map/ppermute | solution.py:284

commit v5 on v4

--- a/solution.py
+++ b/solution.py
@@ -43,11 +43,65 @@
         outs[k][...] = down_ref[reached(lane_ref[0], k)]
 
 
-def split_up_kernel(lane_ref, up_ref, *outs):
-    width = outs[0].shape[1]
-    for k in range(LANES):
-        col = pl.multiple_of(reached(lane_ref[0], k) * width, width)
-        outs[k][...] = up_ref[0, :, pl.ds(col, width)]
+def split_up_kernel(lane_ref, up_ref, same_ref, cross_ref):
+    width = same_ref.shape[2]
+    for dx in range(X):
+        for dc, out_ref in enumerate((same_ref, cross_ref)):
+            col = pl.multiple_of(reached(lane_ref[0], dx * CORES + dc) * width, width)
+            out_ref[dx] = up_ref[0, :, pl.ds(col, width)]
+
+
+def split_up(lane, up):
+    rank, cols = up.shape[1:]
+    return pl.pallas_call(
+        split_up_kernel,
+        in_specs=[SMEM, VMEM],
+        out_specs=[VMEM, VMEM],
+        out_shape=[jax.ShapeDtypeStruct((X, rank, cols // LANES), up.dtype)] * CORES,
+        compiler_params=pltpu.CompilerParams(vmem_limit_bytes=16 * 2**20),
+        name="split_up",
+    )(lane, up)
+
+
+def pair_kernel(same_ref, cross_ref, *outs):
+    for dx in range(X):
+        outs[dx][0] = same_ref[dx]
+        outs[dx][1] = cross_ref[dx]
+
+
+def pair_up(same, cross):
+    shape = (CORES,) + same.shape[1:]
+    return pl.pallas_call(
+        pair_kernel,
+        in_specs=[VMEM, VMEM],
+        out_specs=[VMEM] * X,
+        out_shape=[jax.ShapeDtypeStruct(shape, same.dtype)] * X,
+        compiler_params=pltpu.CompilerParams(vmem_limit_bytes=16 * 2**20),
+        name="pair_up",
+    )(same, cross)
+
+
+def pick_up_kernel(pick_ref, *rest):
+    srcs, out_ref, staged = rest[:X], rest[X], rest[X + 1]
+    for dx in range(X):
+        for dc in range(CORES):
+            staged[dx * CORES + dc] = srcs[dx][dc]
+    for g in range(out_ref.shape[0]):
+        out_ref[g] = staged[pick_ref[g]]
+
+
+def pick_up(shifts, pairs):
+    groups = shifts.shape[0]
+    shape, dtype = pairs[0].shape[1:], pairs[0].dtype
+    return pl.pallas_call(
+        pick_up_kernel,
+        in_specs=[SMEM] + [VMEM] * X,
+        out_specs=VMEM,
+        out_shape=jax.ShapeDtypeStruct((groups,) + shape, dtype),
+        scratch_shapes=[pltpu.VMEM((LANES,) + shape, dtype)],
+        compiler_params=pltpu.CompilerParams(vmem_limit_bytes=16 * 2**20),
+        name="pick_up",
+    )(shifts, *pairs)
 
 
 def split(kernel, lane, whole, piece, name):
@@ -272,11 +326,13 @@
         (pick(wanted, down_row, "pick_down"), hidden, adapter_up_weight)
     )
     down_got = lax.all_to_all(down_send, "req", 0, 0, tiled=True)
-    piece = (rank, adapter_up_weight.shape[2] // LANES)
-    up_row = spread(split(split_up_kernel, lane_arr, adapter_up_weight, piece, "split_up"), groups)
+    same, cross = split_up(lane_arr, adapter_up_weight)
+    cross = lax.ppermute(cross, BOTH, lane_shift(groups, 0, 1))
+    pairs = pair_up(same, cross)
+    pairs = [pairs[0]] + [lax.ppermute(pairs[dx], BOTH, lane_shift(groups, dx, 0)) for dx in range(1, X)]
     normed, base = norm_base(hidden, norm_gain_vector, query_weight)
-    up_row, base = lax.optimization_barrier((up_row, base))
-    up_got = lax.all_to_all(pick(wanted, up_row, "pick_up"), "req", 0, 0, tiled=True)
+    pairs, base = lax.optimization_barrier((pairs, base))
+    up_got = lax.all_to_all(pick_up(wanted, pairs), "req", 0, 0, tiled=True)
 
     low = shrink(owner_rows, down_got, normed)
     other = lax.ppermute(low, BOTH, lane_shift(groups, 0, 1))

time: 83.1 us -> 81.7 us (0.983)
  starting transfers between devices: 37 us -> 32.1 us
  waiting for transfers between devices: 13.2 us -> 16.6 us
    ppermute x14 -> x7, starting transfers between devices: 19.9 us -> 9.99 us  [spread(): lax.ppermute(pieces[k], BOTH, lane_shift(groups, k // CORES, k % CORES))]
    ppermute x0 -> x4, starting transfers between devices: none -> 5.02 us  [the longest x3 4.78 us: shards(): lax.ppermute(pairs[dx], BOTH, lane_shift(groups, dx, 0))]
    all_to_all x1, waiting for transfers between devices: 1.7 us -> 5.18 us  [shards(): down_got = lax.all_to_all(down_send, 'req', 0, 0, tiled=True)]
    pallas_call x0 -> x3, Pallas kernels: none -> 1.74 us  [the longest x1 1.65 us: pick_up(): pl.pallas_call(pick_up_kernel, in_specs=[SMEM] + [VMEM] * X, out_specs=VM...]
    pallas_call x2 -> x1, Pallas kernels: 2.39 us -> 0.75 us  [pick(): pl.pallas_call(pick_kernel, in_specs=[SMEM] + [VMEM] * LANES, out_specs=V...]
    all_to_all x1, waiting for transfers between devices: 1.75 us -> 0.36 us  [shards(): up_got = lax.all_to_all(pick_up(wanted, pairs), 'req', 0, 0, tiled=True)]
    ppermute x0 -> x4, waiting for transfers between devices: none -> 1.38 us  [the longest x1 1.37 us: shards(): cross = lax.ppermute(cross, BOTH, lane_shift(groups, 0, 1))]
    ppermute x14 -> x7, waiting for transfers between devices: 4.37 us -> 4.35 us  [spread(): lax.ppermute(pieces[k], BOTH, lane_shift(groups, k // CORES, k % CORES))]
  transfers between devices with their start and end apart: 20 -> 17, of which waited for: 8 -> 9; matrix products, arithmetic and copies ran while one was open for 1% -> 2% of each run, Pallas kernels for 32% -> 32%
where the time goes in v5:
time: 81.7 us; the launch traced here: 81.3 us
  starting transfers between devices  32.1 us (39%)
  Pallas kernels  28.6 us (35%)
  waiting for transfers between devices  16.6 us (20%)
  local copies, waits for them, and re-layouts  2.71 us (3%)
  other arithmetic  1.05 us (1%)
    pallas_call x1, Pallas kernels, norm_base(): pl.pallas_call(norm_base_kernel, grid=(rows // NORM_ROWS,), in_specs=[pl....  17.3 us
    ppermute x7, starting transfers between devices, spread(): lax.ppermute(pieces[k], BOTH, lane_shift(groups, k // CORES, k % CORES))  9.99 us
    all_to_all x1, starting transfers between devices, shards(): down_got = lax.all_to_all(down_send, 'req', 0, 0, tiled=True)  8.17 us
    pallas_call x1, Pallas kernels, shrink(): pl.pallas_call(shrink_kernel, in_specs=[SMEM, VMEM, ANY], out_specs=VMEM,...  6.83 us
    all_to_all x1, starting transfers between devices, shards(): up_got = lax.all_to_all(pick_up(wanted, pairs), 'req', 0, 0, tiled=True)  5.21 us
    all_to_all x1, waiting for transfers between devices, shards(): down_got = lax.all_to_all(down_send, 'req', 0, 0, tiled=True)  5.18 us
    ppermute x3, starting transfers between devices, shards(): lax.ppermute(pairs[dx], BOTH, lane_shift(groups, dx, 0))  4.78 us
    ppermute x7, waiting for transfers between devices, spread(): lax.ppermute(pieces[k], BOTH, lane_shift(groups, k // CORES, k % CORES))  4.35 us
  transfers between devices with their start and end apart: 17, of which 9 were waited for; matrix products, arithmetic and copies ran while one was open for 2% of the time, Pallas kernels for 32%

profile of v5, /device:TPU:0, one launch (start us, length us, event | category | flops | bytes accessed | tf_op | source)
XLA Modules:
  0.0 81.3 jit_solution(14771620366925214240)
XLA Ops:
  0.0 1.2 %copy-done.2 = bf16[1,64,8192]{2,1,0:T(8,128)(2,1)S(1)} copy-done((bf16[1,64,8192]{2,1,0:T(8,128)(2,1)S(1)}, bf16[1,64,8192]{2,1,0:T(8,128)(2,1)}, u32[]{:S(2)}) %copy-start.2) | copy-done | bytes 1048600
  1.2 0.1 split_down.1
  1.3 1.6 %collective-permute-start = (bf16[8,8192]{1,0:T(8,128)(2,1)S(1)}, bf16[8,8192]{1,0:T(8,128)(2,1)S(1)}, u32[]{:S(2)}, u32[]{:S(2)}) collective-permute-start(bf16[8,8192]{1,0:T(8,128)(2,1)S(1)} %get-tuple-element.31), channel_id=1, source_target_pairs={{0,2},{1,3},{2,4},{3,5},{4,6},{5,7},{6,0},{7,1},{8,10},{9,11},{10,... | collective-permute-start | bytes 393224 | tf_op jit(solution)/shard_map/ppermute | solution.py:120
  2.9 1.7 %collective-permute-start.1 = (bf16[8,8192]{1,0:T(8,128)(2,1)S(1)}, bf16[8,8192]{1,0:T(8,128)(2,1)S(1)}, u32[]{:S(2)}, u32[]{:S(2)}) collective-permute-start(bf16[8,8192]{1,0:T(8,128)(2,1)S(1)} %get-tuple-element.32), channel_id=1, source_target_pairs={{0,6},{1,7},{2,0},{3,1},{4,2},{5,3},{6,4},{7,5},{8,14},{9,15},{10,... | collective-permute-start | bytes 393224 | tf_op jit(solution)/shard_map/ppermute | solution.py:120
  4.6 0.0 collective-permute-start.2
  4.6 3.0 %collective-permute-start.3 = (bf16[8,8192]{1,0:T(8,128)(2,1)S(1)}, bf16[8,8192]{1,0:T(8,128)(2,1)S(1)}, u32[]{:S(2)}, u32[]{:S(2)}) collective-permute-start(bf16[8,8192]{1,0:T(8,128)(2,1)S(1)} %get-tuple-element.34), channel_id=1, source_target_pairs={{0,7},{1,6},{2,1},{3,0},{4,3},{5,2},{6,5},{7,4},{8,15},{9,14},{10,... | collective-permute-start | bytes 393224 | tf_op jit(solution)/shard_map/ppermute | solution.py:120
  7.6 0.7 collective-permute-start.4
  8.2 1.0 %select_reduce_fusion = s32[16,7]{0,1:T(8,128)S(1)} fusion(s32[128]{0:T(128)} %param.13, s32[16,7]{0,1:T(8,128)} %param.12), kind=kLoop, calls=%fused_computation.1 | loop fusion | flops 42896 | bytes 1408 | tf_op jit(solution)/shard_map/reduce_sum | solution.py:320
  9.3 0.0 collective-permute-done.rest_0_
  9.3 1.5 %collective-permute-start.5 = (bf16[8,8192]{1,0:T(8,128)(2,1)S(1)}, bf16[8,8192]{1,0:T(8,128)(2,1)S(1)}, u32[]{:S(2)}, u32[]{:S(2)}) collective-permute-start(bf16[8,8192]{1,0:T(8,128)(2,1)S(1)} %get-tuple-element.36), channel_id=1, source_target_pairs={{0,5},{1,4},{2,7},{3,6},{4,1},{5,0},{6,3},{7,2},{8,13},{9,12},{10,... | collective-permute-start | bytes 393224 | tf_op jit(solution)/shard_map/ppermute | solution.py:120
  10.8 0.0 collective-permute-done.1.rest_1_
  10.8 1.5 %collective-permute-start.6 = (bf16[8,8192]{1,0:T(8,128)(2,1)S(1)}, bf16[8,8192]{1,0:T(8,128)(2,1)S(1)}, u32[]{:S(2)}, u32[]{:S(2)}) collective-permute-start(bf16[8,8192]{1,0:T(8,128)(2,1)S(1)} %get-tuple-element.37), channel_id=1, source_target_pairs={{0,1},{1,0},{2,3},{3,2},{4,5},{5,4},{6,7},{7,6},{8,9},{9,8},{10,11... | collective-permute-start | bytes 393224 | tf_op jit(solution)/shard_map/ppermute | solution.py:120
  12.4 0.0 collective-permute-done.2.rest_2_
  12.4 3.3 %collective-permute-done.3.rest_3_ = bf16[8,8192]{1,0:T(8,128)(2,1)S(1)} collective-permute-done((bf16[8,8192]{1,0:T(8,128)(2,1)S(1)}, bf16[8,8192]{1,0:T(8,128)(2,1)S(1)}, u32[]{:S(2)}, u32[]{:S(2)}) %collective-permute-start.3) | collective-permute-done | bytes 131104 | tf_op jit(solution)/shard_map/ppermute | solution.py:120
  15.7 0.0 collective-permute-done.4.rest_4_
  15.7 1.0 %collective-permute-done.5.rest_5_ = bf16[8,8192]{1,0:T(8,128)(2,1)S(1)} collective-permute-done((bf16[8,8192]{1,0:T(8,128)(2,1)S(1)}, bf16[8,8192]{1,0:T(8,128)(2,1)S(1)}, u32[]{:S(2)}, u32[]{:S(2)}) %collective-permute-start.5) | collective-permute-done | bytes 131104 | tf_op jit(solution)/shard_map/ppermute | solution.py:120
  16.7 0.0 collective-permute-done.6.rest_6_
  16.7 0.7 pick_down.1
  17.5 1.3 %copy-done = bf16[16,8,8192]{2,1,0:T(8,128)(2,1)} copy-done((bf16[16,8,8192]{2,1,0:T(8,128)(2,1)}, bf16[16,8,8192]{2,1,0:T(8,128)(2,1)S(1)}, u32[]{:S(2)}) %copy-start) | copy-done | bytes 2097176
  18.8 8.2 %all-to-all-start = ((bf16[16,8,8192]{2,1,0:T(8,128)(2,1)}), bf16[16,8,8192]{2,1,0:T(8,128)(2,1)S(1)}, u32[]{:S(2)}, u32[]{:S(2)}) async-start(bf16[16,8,8192]{2,1,0:T(8,128)(2,1)} %copy-done), calls=%async_computation | async-start | bytes 4194304 | tf_op jit(solution)/shard_map/all_to_all | solution.py:328
  26.9 0.0 copy-done.3
  27.0 0.1 split_up.1
  27.0 0.2 collective-permute-start.11
  27.3 1.4 %collective-permute-done.11.cross_ref = bf16[4,64,512]{2,1,0:T(8,128)(2,1)S(1)} collective-permute-done((bf16[4,64,512]{2,1,0:T(8,128)(2,1)S(1)}, bf16[4,64,512]{2,1,0:T(8,128)(2,1)S(1)}, u32[]{:S(2)}, u32[]{:S(2)}) %collective-permute-start.11) | collective-permute-done | bytes 262176 | tf_op jit(solution)/shard_map/ppermute | solution.py:330
  28.7 1.5 %collective-permute-start.12 = (bf16[2,64,512]{2,1,0:T(8,128)(2,1)S(1)}, bf16[2,64,512]{2,1,0:T(8,128)(2,1)S(1)}, u32[]{:S(2)}, u32[]{:S(2)}) collective-permute-start(bf16[2,64,512]{2,1,0:T(8,128)(2,1)S(1)} %get-tuple-element.46), channel_id=1, source_target_pairs={{0,2},{1,3},{2,4},{3,5},{4,6},{5,7},{6,0},{7,1},{8,10},{9,11},{10,... | collective-permute-start | bytes 393224 | tf_op jit(solution)/shard_map/ppermute | solution.py:332
  30.2 2.1 %collective-permute-start.13 = (bf16[2,64,512]{2,1,0:T(8,128)(2,1)S(1)}, bf16[2,64,512]{2,1,0:T(8,128)(2,1)S(1)}, u32[]{:S(2)}, u32[]{:S(2)}) collective-permute-start(bf16[2,64,512]{2,1,0:T(8,128)(2,1)S(1)} %get-tuple-element.47), channel_id=1, source_target_pairs={{0,4},{1,5},{2,6},{3,7},{4,0},{5,1},{6,2},{7,3},{8,12},{9,13},{10,... | collective-permute-start | bytes 393224 | tf_op jit(solution)/shard_map/ppermute | solution.py:332
  32.3 1.2 %collective-permute-start.14 = (bf16[2,64,512]{2,1,0:T(8,128)(2,1)S(1)}, bf16[2,64,512]{2,1,0:T(8,128)(2,1)S(1)}, u32[]{:S(2)}, u32[]{:S(2)}) collective-permute-start(bf16[2,64,512]{2,1,0:T(8,128)(2,1)S(1)} %get-tuple-element.48), channel_id=1, source_target_pairs={{0,6},{1,7},{2,0},{3,1},{4,2},{5,3},{6,4},{7,5},{8,14},{9,15},{10,... | collective-permute-start | bytes 393224 | tf_op jit(solution)/shard_map/ppermute | solution.py:332
  33.5 17.3 %norm_base.1 = (bf16[896,8192]{1,0:T(8,128)(2,1)}, f32[896,512]{1,0:T(8,128)}) custom-call(bf16[896,8192]{1,0:T(8,128)(2,1)} %x_ref, f32[1,8192]{1,0:T(1,128)} %bitcast.8, bf16[8192,512]{1,0:T(8,128)(2,1)} %weight_ref.1), custom_call_target="tpu_custom_call" | custom-call | flops 15032385536 | bytes 37748736 | tf_op jit(solution)/shard_map/norm_base/pallas_call | solution.py:171
  50.7 0.0 collective-permute-done.12.rest_1_
  50.7 0.0 collective-permute-done.13.rest_2_
  50.7 0.0 collective-permute-done.14.rest_3_
  50.7 1.6 %pick_up.1 = bf16[16,64,512]{2,1,0:T(8,128)(2,1)} custom-call(s32[16]{0:T(128)S(1)} %fusion.5.pick_ref, bf16[2,64,512]{2,1,0:T(8,128)(2,1)S(1)} %get-tuple-element.53.rest_0_, bf16[2,64,512]{2,1,0:T(8,128)(2,1)S(1)} %collective-permute-done.12.rest_1_, bf16[2,64,512]{2,1,0:T(8,128)(2,1)S(1)} %collective-permute-done.13.rest_2_, ...), custom_call_target="tpu_custom_call" | custom-call | tf_op jit(solution)/shard_map/pick_up/pallas_call | solution.py:96
  52.4 5.2 %all-to-all-done.down_ref = bf16[16,8,8192]{2,1,0:T(8,128)(2,1)S(1)} async-done(((bf16[16,8,8192]{2,1,0:T(8,128)(2,1)}), bf16[16,8,8192]{2,1,0:T(8,128)(2,1)S(1)}, u32[]{:S(2)}, u32[]{:S(2)}) %all-to-all-start) | async-done | bytes 2097184 | tf_op jit(solution)/shard_map/all_to_all | solution.py:328
  57.6 5.2 %all-to-all-start.1 = ((bf16[16,64,512]{2,1,0:T(8,128)(2,1)}), bf16[16,64,512]{2,1,0:T(8,128)(2,1)S(1)}, u32[]{:S(2)}, u32[]{:S(2)}) async-start(bf16[16,64,512]{2,1,0:T(8,128)(2,1)} %pick_up.1), calls=%async_computation.1 | async-start | bytes 2097152 | tf_op jit(solution)/shard_map/all_to_all | solution.py:335
  62.8 0.2 dynamic-slice_reduce_fusion
  63.0 6.8 %shrink.1 = f32[7,8,128]{2,1,0:T(8,128)S(1)} custom-call(s32[7]{0:T(128)S(1)} %and_select_fusion.4.row_ref, bf16[16,8,8192]{2,1,0:T(8,128)(2,1)S(1)} %all-to-all-done.down_ref, bf16[896,8192]{1,0:T(8,128)(2,1)} %get-tuple-element.41.normed_hbm), custom_call_target="tpu_custom_call" | custom-call | flops 3758096384 | bytes 14680064 | tf_op jit(solution)/shard_map/shrink/pallas_call | solution.py:224
  69.8 0.1 collective-permute-start.7
  69.9 1.2 %collective-permute-done.7 = f32[7,8,128]{2,1,0:T(8,128)S(1)} collective-permute-done((f32[7,8,128]{2,1,0:T(8,128)S(1)}, f32[7,8,128]{2,1,0:T(8,128)S(1)}, u32[]{:S(2)}, u32[]{:S(2)}) %collective-permute-start.7) | collective-permute-done | bytes 28704 | tf_op jit(solution)/shard_map/ppermute | solution.py:338
  71.1 0.7 collective-permute-start.8
  71.8 3.0 %collective-permute-start.9 = (f32[2,7,8,128]{3,2,1,0:T(8,128)S(1)}, f32[2,7,8,128]{3,2,1,0:T(8,128)S(1)}, u32[]{:S(2)}, u32[]{:S(2)}) collective-permute-start(f32[2,7,8,128]{3,2,1,0:T(8,128)S(1)} %pad_maximum_fusion.low0), channel_id=1, source_target_pairs={{0,4},{1,5},{2,6},{3,7},{4,0},{5,1},{6,2},{7,3},{8,12},{9,13},{10,... | collective-permute-start | bytes 172040 | tf_op jit(solution)/shard_map/ppermute | solution.py:340
  74.8 0.0 collective-permute-start.10
  74.8 2.2 %collective-permute-done.8.low1 = f32[2,7,8,128]{3,2,1,0:T(8,128)S(1)} collective-permute-done((f32[2,7,8,128]{3,2,1,0:T(8,128)S(1)}, f32[2,7,8,128]{3,2,1,0:T(8,128)S(1)}, u32[]{:S(2)}, u32[]{:S(2)}) %collective-permute-start.8) | collective-permute-done | bytes 57376 | tf_op jit(solution)/shard_map/ppermute | solution.py:340
  77.0 0.9 %collective-permute-done.9.low2 = f32[2,7,8,128]{3,2,1,0:T(8,128)S(1)} collective-permute-done((f32[2,7,8,128]{3,2,1,0:T(8,128)S(1)}, f32[2,7,8,128]{3,2,1,0:T(8,128)S(1)}, u32[]{:S(2)}, u32[]{:S(2)}) %collective-permute-start.9) | collective-permute-done | bytes 57376 | tf_op jit(solution)/shard_map/ppermute | solution.py:340
  78.0 1.0 %collective-permute-done.10.low3 = f32[2,7,8,128]{3,2,1,0:T(8,128)S(1)} collective-permute-done((f32[2,7,8,128]{3,2,1,0:T(8,128)S(1)}, f32[2,7,8,128]{3,2,1,0:T(8,128)S(1)}, u32[]{:S(2)}, u32[]{:S(2)}) %collective-permute-start.10) | collective-permute-done | bytes 57376 | tf_op jit(solution)/shard_map/ppermute | solution.py:340
  79.0 0.0 copy-done.1
  79.0 0.3 gather_low.1
  79.3 0.4 all-to-all-done.1.up_ref
  79.6 1.7 %expand.1 = bf16[896,512]{1,0:T(8,128)(2,1)} custom-call(s32[7]{0:T(128)S(1)} %and_select_fusion.4.row_ref, bf16[7,128,64]{2,1,0:T(8,128)(2,1)S(1)} %get-tuple-element.51.low_ref, f32[896,512]{1,0:T(8,128)S(1)} %get-tuple-element.52.base_ref, bf16[16,64,512]{2,1,0:T(8,128)(2,1)S(1)} %all-to-all-done.1.up_ref), custom_call_target="tpu_custom_call" | custom-call | tf_op jit(solution)/shard_map/expand/pallas_call | solution.py:286
  (9 shorter events, 0.1 us)
Async XLA Ops:
  0.0 1.2 %copy-start.2 = (bf16[1,64,8192]{2,1,0:T(8,128)(2,1)S(1)}, bf16[1,64,8192]{2,1,0:T(8,128)(2,1)}, u32[]{:S(2)}) copy-start(bf16[1,64,8192]{2,1,0:T(8,128)(2,1)} %param.10) | copy-start | bytes 3145732
  1.3 8.0 %collective-permute-start = (bf16[8,8192]{1,0:T(8,128)(2,1)S(1)}, bf16[8,8192]{1,0:T(8,128)(2,1)S(1)}, u32[]{:S(2)}, u32[]{:S(2)}) collective-permute-start(bf16[8,8192]{1,0:T(8,128)(2,1)S(1)} %get-tuple-element.31), channel_id=1, source_target_pairs={{0,2},{1,3},{2,4},{3,5},{4,6},{5,7},{6,0},{7,1},{8,10},{9,11},{10,... | collective-permute-start | bytes 393224 | tf_op jit(solution)/shard_map/ppermute | solution.py:120
  2.9 7.8 %collective-permute-start.1 = (bf16[8,8192]{1,0:T(8,128)(2,1)S(1)}, bf16[8,8192]{1,0:T(8,128)(2,1)S(1)}, u32[]{:S(2)}, u32[]{:S(2)}) collective-permute-start(bf16[8,8192]{1,0:T(8,128)(2,1)S(1)} %get-tuple-element.32), channel_id=1, source_target_pairs={{0,6},{1,7},{2,0},{3,1},{4,2},{5,3},{6,4},{7,5},{8,14},{9,15},{10,... | collective-permute-start | bytes 393224 | tf_op jit(solution)/shard_map/ppermute | solution.py:120
  4.6 7.8 %collective-permute-start.2 = (bf16[8,8192]{1,0:T(8,128)(2,1)S(1)}, bf16[8,8192]{1,0:T(8,128)(2,1)S(1)}, u32[]{:S(2)}, u32[]{:S(2)}) collective-permute-start(bf16[8,8192]{1,0:T(8,128)(2,1)S(1)} %get-tuple-element.33), channel_id=1, source_target_pairs={{0,3},{1,2},{2,5},{3,4},{4,7},{5,6},{6,1},{7,0},{8,11},{9,10},{10,... | collective-permute-start | bytes 393224 | tf_op jit(solution)/shard_map/ppermute | solution.py:120
  4.6 11.1 %collective-permute-start.3 = (bf16[8,8192]{1,0:T(8,128)(2,1)S(1)}, bf16[8,8192]{1,0:T(8,128)(2,1)S(1)}, u32[]{:S(2)}, u32[]{:S(2)}) collective-permute-start(bf16[8,8192]{1,0:T(8,128)(2,1)S(1)} %get-tuple-element.34), channel_id=1, source_target_pairs={{0,7},{1,6},{2,1},{3,0},{4,3},{5,2},{6,5},{7,4},{8,15},{9,14},{10,... | collective-permute-start | bytes 393224 | tf_op jit(solution)/shard_map/ppermute | solution.py:120
  7.6 8.1 %collective-permute-start.4 = (bf16[8,8192]{1,0:T(8,128)(2,1)S(1)}, bf16[8,8192]{1,0:T(8,128)(2,1)S(1)}, u32[]{:S(2)}, u32[]{:S(2)}) collective-permute-start(bf16[8,8192]{1,0:T(8,128)(2,1)S(1)} %get-tuple-element.35), channel_id=1, source_target_pairs={{0,4},{1,5},{2,6},{3,7},{4,0},{5,1},{6,2},{7,3},{8,12},{9,13},{10,... | collective-permute-start | bytes 393224 | tf_op jit(solution)/shard_map/ppermute | solution.py:120
  9.3 7.4 %collective-permute-start.5 = (bf16[8,8192]{1,0:T(8,128)(2,1)S(1)}, bf16[8,8192]{1,0:T(8,128)(2,1)S(1)}, u32[]{:S(2)}, u32[]{:S(2)}) collective-permute-start(bf16[8,8192]{1,0:T(8,128)(2,1)S(1)} %get-tuple-element.36), channel_id=1, source_target_pairs={{0,5},{1,4},{2,7},{3,6},{4,1},{5,0},{6,3},{7,2},{8,13},{9,12},{10,... | collective-permute-start | bytes 393224 | tf_op jit(solution)/shard_map/ppermute | solution.py:120
  10.8 5.9 %collective-permute-start.6 = (bf16[8,8192]{1,0:T(8,128)(2,1)S(1)}, bf16[8,8192]{1,0:T(8,128)(2,1)S(1)}, u32[]{:S(2)}, u32[]{:S(2)}) collective-permute-start(bf16[8,8192]{1,0:T(8,128)(2,1)S(1)} %get-tuple-element.37), channel_id=1, source_target_pairs={{0,1},{1,0},{2,3},{3,2},{4,5},{5,4},{6,7},{7,6},{8,9},{9,8},{10,11... | collective-permute-start | bytes 393224 | tf_op jit(solution)/shard_map/ppermute | solution.py:120
  17.5 1.3 %copy-start = (bf16[16,8,8192]{2,1,0:T(8,128)(2,1)}, bf16[16,8,8192]{2,1,0:T(8,128)(2,1)S(1)}, u32[]{:S(2)}) copy-start(bf16[16,8,8192]{2,1,0:T(8,128)(2,1)S(1)} %pick_down.1) | copy-start | bytes 6291460
  18.8 8.2 %copy-start.3 = (bf16[1,64,4096]{2,1,0:T(8,128)(2,1)S(1)}, bf16[1,64,4096]{2,1,0:T(8,128)(2,1)}, u32[]{:S(2)}) copy-start(bf16[1,64,4096]{2,1,0:T(8,128)(2,1)} %up_ref) | copy-start | bytes 1572868
  18.8 38.8 %all-to-all-start = ((bf16[16,8,8192]{2,1,0:T(8,128)(2,1)}), bf16[16,8,8192]{2,1,0:T(8,128)(2,1)S(1)}, u32[]{:S(2)}, u32[]{:S(2)}) async-start(bf16[16,8,8192]{2,1,0:T(8,128)(2,1)} %copy-done), calls=%async_computation | async-start | bytes 4194304 | tf_op jit(solution)/shard_map/all_to_all | solution.py:328
  27.0 1.6 %collective-permute-start.11 = (bf16[4,64,512]{2,1,0:T(8,128)(2,1)S(1)}, bf16[4,64,512]{2,1,0:T(8,128)(2,1)S(1)}, u32[]{:S(2)}, u32[]{:S(2)}) collective-permute-start(bf16[4,64,512]{2,1,0:T(8,128)(2,1)S(1)} %get-tuple-element.44), channel_id=1, source_target_pairs={{0,1},{1,0},{2,3},{3,2},{4,5},{5,4},{6,7},{7,6},{8,9},{9,8},{10,11... | collective-permute-start | bytes 786440 | tf_op jit(solution)/shard_map/ppermute | solution.py:330
  28.7 22.1 %collective-permute-start.12 = (bf16[2,64,512]{2,1,0:T(8,128)(2,1)S(1)}, bf16[2,64,512]{2,1,0:T(8,128)(2,1)S(1)}, u32[]{:S(2)}, u32[]{:S(2)}) collective-permute-start(bf16[2,64,512]{2,1,0:T(8,128)(2,1)S(1)} %get-tuple-element.46), channel_id=1, source_target_pairs={{0,2},{1,3},{2,4},{3,5},{4,6},{5,7},{6,0},{7,1},{8,10},{9,11},{10,... | collective-permute-start | bytes 393224 | tf_op jit(solution)/shard_map/ppermute | solution.py:332
  30.2 20.6 %collective-permute-start.13 = (bf16[2,64,512]{2,1,0:T(8,128)(2,1)S(1)}, bf16[2,64,512]{2,1,0:T(8,128)(2,1)S(1)}, u32[]{:S(2)}, u32[]{:S(2)}) collective-permute-start(bf16[2,64,512]{2,1,0:T(8,128)(2,1)S(1)} %get-tuple-element.47), channel_id=1, source_target_pairs={{0,4},{1,5},{2,6},{3,7},{4,0},{5,1},{6,2},{7,3},{8,12},{9,13},{10,... | collective-permute-start | bytes 393224 | tf_op jit(solution)/shard_map/ppermute | solution.py:332
  32.3 18.5 %collective-permute-start.14 = (bf16[2,64,512]{2,1,0:T(8,128)(2,1)S(1)}, bf16[2,64,512]{2,1,0:T(8,128)(2,1)S(1)}, u32[]{:S(2)}, u32[]{:S(2)}) collective-permute-start(bf16[2,64,512]{2,1,0:T(8,128)(2,1)S(1)} %get-tuple-element.48), channel_id=1, source_target_pairs={{0,6},{1,7},{2,0},{3,1},{4,2},{5,3},{6,4},{7,5},{8,14},{9,15},{10,... | collective-permute-start | bytes 393224 | tf_op jit(solution)/shard_map/ppermute | solution.py:332
  57.6 22.1 %all-to-all-start.1 = ((bf16[16,64,512]{2,1,0:T(8,128)(2,1)}), bf16[16,64,512]{2,1,0:T(8,128)(2,1)S(1)}, u32[]{:S(2)}, u32[]{:S(2)}) async-start(bf16[16,64,512]{2,1,0:T(8,128)(2,1)} %pick_up.1), calls=%async_computation.1 | async-start | bytes 2097152 | tf_op jit(solution)/shard_map/all_to_all | solution.py:335
  63.0 16.0 %copy-start.1 = (f32[896,512]{1,0:T(8,128)S(1)}, f32[896,512]{1,0:T(8,128)}, u32[]{:S(2)}) copy-start(f32[896,512]{1,0:T(8,128)} %get-tuple-element.50.base_hbm) | copy-start | bytes 5505028
  69.8 1.3 %collective-permute-start.7 = (f32[7,8,128]{2,1,0:T(8,128)S(1)}, f32[7,8,128]{2,1,0:T(8,128)S(1)}, u32[]{:S(2)}, u32[]{:S(2)}) collective-permute-start(f32[7,8,128]{2,1,0:T(8,128)S(1)} %shrink.1), channel_id=1, source_target_pairs={{0,1},{1,0},{2,3},{3,2},{4,5},{5,4},{6,7},{7,6},{8,9},{9,8},{10,11... | collective-permute-start | bytes 86024 | tf_op jit(solution)/shard_map/ppermute | solution.py:338
  71.1 5.9 %collective-permute-start.8 = (f32[2,7,8,128]{3,2,1,0:T(8,128)S(1)}, f32[2,7,8,128]{3,2,1,0:T(8,128)S(1)}, u32[]{:S(2)}, u32[]{:S(2)}) collective-permute-start(f32[2,7,8,128]{3,2,1,0:T(8,128)S(1)} %pad_maximum_fusion.low0), channel_id=1, source_target_pairs={{0,2},{1,3},{2,4},{3,5},{4,6},{5,7},{6,0},{7,1},{8,10},{9,11},{10,... | collective-permute-start | bytes 172040 | tf_op jit(solution)/shard_map/ppermute | solution.py:340
  71.8 6.2 %collective-permute-start.9 = (f32[2,7,8,128]{3,2,1,0:T(8,128)S(1)}, f32[2,7,8,128]{3,2,1,0:T(8,128)S(1)}, u32[]{:S(2)}, u32[]{:S(2)}) collective-permute-start(f32[2,7,8,128]{3,2,1,0:T(8,128)S(1)} %pad_maximum_fusion.low0), channel_id=1, source_target_pairs={{0,4},{1,5},{2,6},{3,7},{4,0},{5,1},{6,2},{7,3},{8,12},{9,13},{10,... | collective-permute-start | bytes 172040 | tf_op jit(solution)/shard_map/ppermute | solution.py:340
  74.8 4.2 %collective-permute-start.10 = (f32[2,7,8,128]{3,2,1,0:T(8,128)S(1)}, f32[2,7,8,128]{3,2,1,0:T(8,128)S(1)}, u32[]{:S(2)}, u32[]{:S(2)}) collective-permute-start(f32[2,7,8,128]{3,2,1,0:T(8,128)S(1)} %pad_maximum_fusion.low0), channel_id=1, source_target_pairs={{0,6},{1,7},{2,0},{3,1},{4,2},{5,3},{6,4},{7,5},{8,14},{9,15},{10,... | collective-permute-start | bytes 172040 | tf_op jit(solution)/shard_map/ppermute | solution.py:340

commit v6 on v5

--- a/solution.py
+++ b/solution.py
@@ -10,7 +10,7 @@
 ADAPTER_SCALE = 0.5
 X, CORES = 4, 2
 LANES = X * CORES
-ORDER = (2, 6, 3, 7, 4, 5, 1)
+ORDER = (4, 5, 2, 6, 3, 7, 1)
 BOTH = ("req", "tp")
 
 

time: 81.7 us -> 80.8 us (0.989)
  waiting for transfers between devices: 16.6 us -> 15.7 us
    all_to_all x1, starting transfers between devices: 5.21 us -> 3.65 us  [shards(): up_got = lax.all_to_all(pick_up(wanted, pairs), 'req', 0, 0, tiled=True)]
    ppermute x3, starting transfers between devices: 3.67 us -> 5.15 us  [shards(): lax.ppermute(chip, BOTH, lane_shift(groups, dx, 0))]
    ppermute x3, waiting for transfers between devices: 4.17 us -> 2.7 us  [shards(): lax.ppermute(chip, BOTH, lane_shift(groups, dx, 0))]
  transfers between devices with their start and end apart: 17 -> 17, of which waited for: 9 -> 9; matrix products, arithmetic and copies ran while one was open for 2% -> 2% of each run, Pallas kernels for 32% -> 33%
where the time goes in v6:
time: 80.8 us; the launch traced here: 80.3 us
  starting transfers between devices  32 us (40%)
  Pallas kernels  28.6 us (35%)
  waiting for transfers between devices  15.7 us (19%)
  local copies, waits for them, and re-layouts  2.71 us (3%)
  other arithmetic  1.05 us (1%)
    pallas_call x1, Pallas kernels, norm_base(): pl.pallas_call(norm_base_kernel, grid=(rows // NORM_ROWS,), in_specs=[pl....  17.3 us
    ppermute x7, starting transfers between devices, spread(): lax.ppermute(pieces[k], BOTH, lane_shift(groups, k // CORES, k % CORES))  9.58 us
    all_to_all x1, starting transfers between devices, shards(): down_got = lax.all_to_all(down_send, 'req', 0, 0, tiled=True)  8.19 us
    pallas_call x1, Pallas kernels, shrink(): pl.pallas_call(shrink_kernel, in_specs=[SMEM, VMEM, ANY], out_specs=VMEM,...  6.83 us
    ppermute x3, starting transfers between devices, shards(): lax.ppermute(pairs[dx], BOTH, lane_shift(groups, dx, 0))  5.25 us
    all_to_all x1, waiting for transfers between devices, shards(): down_got = lax.all_to_all(down_send, 'req', 0, 0, tiled=True)  5.17 us
    ppermute x7, waiting for transfers between devices, spread(): lax.ppermute(pieces[k], BOTH, lane_shift(groups, k // CORES, k % CORES))  5.15 us
    ppermute x3, starting transfers between devices, shards(): lax.ppermute(chip, BOTH, lane_shift(groups, dx, 0))  5.15 us
  transfers between devices with their start and end apart: 17, of which 9 were waited for; matrix products, arithmetic and copies ran while one was open for 2% of the time, Pallas kernels for 33%

profile of v6, /device:TPU:0, one launch (start us, length us, event | category | flops | bytes accessed | tf_op | source)
XLA Modules:
  0.0 80.3 jit_solution(3455827140996748620)
XLA Ops:
  0.0 1.2 %copy-done.2 = bf16[1,64,8192]{2,1,0:T(8,128)(2,1)S(1)} copy-done((bf16[1,64,8192]{2,1,0:T(8,128)(2,1)S(1)}, bf16[1,64,8192]{2,1,0:T(8,128)(2,1)}, u32[]{:S(2)}) %copy-start.2) | copy-done | bytes 1048600
  1.2 0.1 split_down.1
  1.3 3.2 %collective-permute-start = (bf16[8,8192]{1,0:T(8,128)(2,1)S(1)}, bf16[8,8192]{1,0:T(8,128)(2,1)S(1)}, u32[]{:S(2)}, u32[]{:S(2)}) collective-permute-start(bf16[8,8192]{1,0:T(8,128)(2,1)S(1)} %get-tuple-element.31), channel_id=1, source_target_pairs={{0,4},{1,5},{2,6},{3,7},{4,0},{5,1},{6,2},{7,3},{8,12},{9,13},{10,... | collective-permute-start | bytes 393224 | tf_op jit(solution)/shard_map/ppermute | solution.py:120
  4.5 0.0 collective-permute-start.1
  4.5 1.2 %collective-permute-start.2 = (bf16[8,8192]{1,0:T(8,128)(2,1)S(1)}, bf16[8,8192]{1,0:T(8,128)(2,1)S(1)}, u32[]{:S(2)}, u32[]{:S(2)}) collective-permute-start(bf16[8,8192]{1,0:T(8,128)(2,1)S(1)} %get-tuple-element.33), channel_id=1, source_target_pairs={{0,2},{1,3},{2,4},{3,5},{4,6},{5,7},{6,0},{7,1},{8,10},{9,11},{10,... | collective-permute-start | bytes 393224 | tf_op jit(solution)/shard_map/ppermute | solution.py:120
  5.6 2.1 %collective-permute-start.3 = (bf16[8,8192]{1,0:T(8,128)(2,1)S(1)}, bf16[8,8192]{1,0:T(8,128)(2,1)S(1)}, u32[]{:S(2)}, u32[]{:S(2)}) collective-permute-start(bf16[8,8192]{1,0:T(8,128)(2,1)S(1)} %get-tuple-element.34), channel_id=1, source_target_pairs={{0,6},{1,7},{2,0},{3,1},{4,2},{5,3},{6,4},{7,5},{8,14},{9,15},{10,... | collective-permute-start | bytes 393224 | tf_op jit(solution)/shard_map/ppermute | solution.py:120
  7.7 0.0 collective-permute-start.4
  7.7 1.0 %select_reduce_fusion = s32[16,7]{0,1:T(8,128)S(1)} fusion(s32[128]{0:T(128)} %param.13, s32[16,7]{0,1:T(8,128)} %param.12), kind=kLoop, calls=%fused_computation.1 | loop fusion | flops 42896 | bytes 1408 | tf_op jit(solution)/shard_map/reduce_sum | solution.py:320
  8.8 0.0 collective-permute-done.rest_0_
  8.8 3.0 %collective-permute-start.5 = (bf16[8,8192]{1,0:T(8,128)(2,1)S(1)}, bf16[8,8192]{1,0:T(8,128)(2,1)S(1)}, u32[]{:S(2)}, u32[]{:S(2)}) collective-permute-start(bf16[8,8192]{1,0:T(8,128)(2,1)S(1)} %get-tuple-element.36), channel_id=1, source_target_pairs={{0,7},{1,6},{2,1},{3,0},{4,3},{5,2},{6,5},{7,4},{8,15},{9,14},{10,... | collective-permute-start | bytes 393224 | tf_op jit(solution)/shard_map/ppermute | solution.py:120
  11.8 0.0 collective-permute-done.1.rest_1_
  11.8 0.1 collective-permute-start.6
  12.0 2.4 %collective-permute-done.2.rest_2_ = bf16[8,8192]{1,0:T(8,128)(2,1)S(1)} collective-permute-done((bf16[8,8192]{1,0:T(8,128)(2,1)S(1)}, bf16[8,8192]{1,0:T(8,128)(2,1)S(1)}, u32[]{:S(2)}, u32[]{:S(2)}) %collective-permute-start.2) | collective-permute-done | bytes 131104 | tf_op jit(solution)/shard_map/ppermute | solution.py:120
  14.4 0.4 collective-permute-done.3.rest_3_
  14.8 2.3 %collective-permute-done.4.rest_4_ = bf16[8,8192]{1,0:T(8,128)(2,1)S(1)} collective-permute-done((bf16[8,8192]{1,0:T(8,128)(2,1)S(1)}, bf16[8,8192]{1,0:T(8,128)(2,1)S(1)}, u32[]{:S(2)}, u32[]{:S(2)}) %collective-permute-start.4) | collective-permute-done | bytes 131104 | tf_op jit(solution)/shard_map/ppermute | solution.py:120
  17.1 0.0 collective-permute-done.5.rest_5_
  17.1 0.0 collective-permute-done.6.rest_6_
  17.1 0.7 pick_down.1
  17.9 0.0 copy-start
  17.9 1.3 %copy-done = bf16[16,8,8192]{2,1,0:T(8,128)(2,1)} copy-done((bf16[16,8,8192]{2,1,0:T(8,128)(2,1)}, bf16[16,8,8192]{2,1,0:T(8,128)(2,1)S(1)}, u32[]{:S(2)}) %copy-start) | copy-done | bytes 2097176
  19.2 8.2 %all-to-all-start = ((bf16[16,8,8192]{2,1,0:T(8,128)(2,1)}), bf16[16,8,8192]{2,1,0:T(8,128)(2,1)S(1)}, u32[]{:S(2)}, u32[]{:S(2)}) async-start(bf16[16,8,8192]{2,1,0:T(8,128)(2,1)} %copy-done), calls=%async_computation | async-start | bytes 4194304 | tf_op jit(solution)/shard_map/all_to_all | solution.py:328
  27.4 0.0 copy-done.3
  27.4 0.1 split_up.1
  27.4 0.1 collective-permute-start.11
  27.5 1.5 %collective-permute-done.11.cross_ref = bf16[4,64,512]{2,1,0:T(8,128)(2,1)S(1)} collective-permute-done((bf16[4,64,512]{2,1,0:T(8,128)(2,1)S(1)}, bf16[4,64,512]{2,1,0:T(8,128)(2,1)S(1)}, u32[]{:S(2)}, u32[]{:S(2)}) %collective-permute-start.11) | collective-permute-done | bytes 262176 | tf_op jit(solution)/shard_map/ppermute | solution.py:330
  29.1 1.1 %collective-permute-start.12 = (bf16[2,64,512]{2,1,0:T(8,128)(2,1)S(1)}, bf16[2,64,512]{2,1,0:T(8,128)(2,1)S(1)}, u32[]{:S(2)}, u32[]{:S(2)}) collective-permute-start(bf16[2,64,512]{2,1,0:T(8,128)(2,1)S(1)} %get-tuple-element.46), channel_id=1, source_target_pairs={{0,2},{1,3},{2,4},{3,5},{4,6},{5,7},{6,0},{7,1},{8,10},{9,11},{10,... | collective-permute-start | bytes 393224 | tf_op jit(solution)/shard_map/ppermute | solution.py:332
  30.1 2.7 %collective-permute-start.13 = (bf16[2,64,512]{2,1,0:T(8,128)(2,1)S(1)}, bf16[2,64,512]{2,1,0:T(8,128)(2,1)S(1)}, u32[]{:S(2)}, u32[]{:S(2)}) collective-permute-start(bf16[2,64,512]{2,1,0:T(8,128)(2,1)S(1)} %get-tuple-element.47), channel_id=1, source_target_pairs={{0,4},{1,5},{2,6},{3,7},{4,0},{5,1},{6,2},{7,3},{8,12},{9,13},{10,... | collective-permute-start | bytes 393224 | tf_op jit(solution)/shard_map/ppermute | solution.py:332
  32.8 1.5 %collective-permute-start.14 = (bf16[2,64,512]{2,1,0:T(8,128)(2,1)S(1)}, bf16[2,64,512]{2,1,0:T(8,128)(2,1)S(1)}, u32[]{:S(2)}, u32[]{:S(2)}) collective-permute-start(bf16[2,64,512]{2,1,0:T(8,128)(2,1)S(1)} %get-tuple-element.48), channel_id=1, source_target_pairs={{0,6},{1,7},{2,0},{3,1},{4,2},{5,3},{6,4},{7,5},{8,14},{9,15},{10,... | collective-permute-start | bytes 393224 | tf_op jit(solution)/shard_map/ppermute | solution.py:332
  34.3 17.3 %norm_base.1 = (bf16[896,8192]{1,0:T(8,128)(2,1)}, f32[896,512]{1,0:T(8,128)}) custom-call(bf16[896,8192]{1,0:T(8,128)(2,1)} %x_ref, f32[1,8192]{1,0:T(1,128)} %bitcast.8, bf16[8192,512]{1,0:T(8,128)(2,1)} %weight_ref.1), custom_call_target="tpu_custom_call" | custom-call | flops 15032385536 | bytes 37748736 | tf_op jit(solution)/shard_map/norm_base/pallas_call | solution.py:171
  51.6 0.0 collective-permute-done.12.rest_1_
  51.6 0.0 collective-permute-done.13.rest_2_
  51.6 0.0 collective-permute-done.14.rest_3_
  51.6 1.6 %pick_up.1 = bf16[16,64,512]{2,1,0:T(8,128)(2,1)} custom-call(s32[16]{0:T(128)S(1)} %fusion.5.pick_ref, bf16[2,64,512]{2,1,0:T(8,128)(2,1)S(1)} %get-tuple-element.53.rest_0_, bf16[2,64,512]{2,1,0:T(8,128)(2,1)S(1)} %collective-permute-done.12.rest_1_, bf16[2,64,512]{2,1,0:T(8,128)(2,1)S(1)} %collective-permute-done.13.rest_2_, ...), custom_call_target="tpu_custom_call" | custom-call | tf_op jit(solution)/shard_map/pick_up/pallas_call | solution.py:96
  53.3 5.2 %all-to-all-done.down_ref = bf16[16,8,8192]{2,1,0:T(8,128)(2,1)S(1)} async-done(((bf16[16,8,8192]{2,1,0:T(8,128)(2,1)}), bf16[16,8,8192]{2,1,0:T(8,128)(2,1)S(1)}, u32[]{:S(2)}, u32[]{:S(2)}) %all-to-all-start) | async-done | bytes 2097184 | tf_op jit(solution)/shard_map/all_to_all | solution.py:328
  58.4 3.7 %all-to-all-start.1 = ((bf16[16,64,512]{2,1,0:T(8,128)(2,1)}), bf16[16,64,512]{2,1,0:T(8,128)(2,1)S(1)}, u32[]{:S(2)}, u32[]{:S(2)}) async-start(bf16[16,64,512]{2,1,0:T(8,128)(2,1)} %pick_up.1), calls=%async_computation.1 | async-start | bytes 2097152 | tf_op jit(solution)/shard_map/all_to_all | solution.py:335
  62.1 0.2 dynamic-slice_reduce_fusion
  62.3 6.8 %shrink.1 = f32[7,8,128]{2,1,0:T(8,128)S(1)} custom-call(s32[7]{0:T(128)S(1)} %and_select_fusion.4.row_ref, bf16[16,8,8192]{2,1,0:T(8,128)(2,1)S(1)} %all-to-all-done.down_ref, bf16[896,8192]{1,0:T(8,128)(2,1)} %get-tuple-element.41.normed_hbm), custom_call_target="tpu_custom_call" | custom-call | flops 3758096384 | bytes 14680064 | tf_op jit(solution)/shard_map/shrink/pallas_call | solution.py:224
  69.1 0.1 collective-permute-start.7
  69.2 1.2 %collective-permute-done.7 = f32[7,8,128]{2,1,0:T(8,128)S(1)} collective-permute-done((f32[7,8,128]{2,1,0:T(8,128)S(1)}, f32[7,8,128]{2,1,0:T(8,128)S(1)}, u32[]{:S(2)}, u32[]{:S(2)}) %collective-permute-start.7) | collective-permute-done | bytes 28704 | tf_op jit(solution)/shard_map/ppermute | solution.py:338
  70.4 1.0 %collective-permute-start.8 = (f32[2,7,8,128]{3,2,1,0:T(8,128)S(1)}, f32[2,7,8,128]{3,2,1,0:T(8,128)S(1)}, u32[]{:S(2)}, u32[]{:S(2)}) collective-permute-start(f32[2,7,8,128]{3,2,1,0:T(8,128)S(1)} %pad_maximum_fusion.low0), channel_id=1, source_target_pairs={{0,2},{1,3},{2,4},{3,5},{4,6},{5,7},{6,0},{7,1},{8,10},{9,11},{10,... | collective-permute-start | bytes 172040 | tf_op jit(solution)/shard_map/ppermute | solution.py:340
  71.4 2.7 %collective-permute-start.9 = (f32[2,7,8,128]{3,2,1,0:T(8,128)S(1)}, f32[2,7,8,128]{3,2,1,0:T(8,128)S(1)}, u32[]{:S(2)}, u32[]{:S(2)}) collective-permute-start(f32[2,7,8,128]{3,2,1,0:T(8,128)S(1)} %pad_maximum_fusion.low0), channel_id=1, source_target_pairs={{0,4},{1,5},{2,6},{3,7},{4,0},{5,1},{6,2},{7,3},{8,12},{9,13},{10,... | collective-permute-start | bytes 172040 | tf_op jit(solution)/shard_map/ppermute | solution.py:340
  74.1 1.5 %collective-permute-start.10 = (f32[2,7,8,128]{3,2,1,0:T(8,128)S(1)}, f32[2,7,8,128]{3,2,1,0:T(8,128)S(1)}, u32[]{:S(2)}, u32[]{:S(2)}) collective-permute-start(f32[2,7,8,128]{3,2,1,0:T(8,128)S(1)} %pad_maximum_fusion.low0), channel_id=1, source_target_pairs={{0,6},{1,7},{2,0},{3,1},{4,2},{5,3},{6,4},{7,5},{8,14},{9,15},{10,... | collective-permute-start | bytes 172040 | tf_op jit(solution)/shard_map/ppermute | solution.py:340
  75.6 0.8 collective-permute-done.8.low1
  76.3 1.0 %collective-permute-done.9.low2 = f32[2,7,8,128]{3,2,1,0:T(8,128)S(1)} collective-permute-done((f32[2,7,8,128]{3,2,1,0:T(8,128)S(1)}, f32[2,7,8,128]{3,2,1,0:T(8,128)S(1)}, u32[]{:S(2)}, u32[]{:S(2)}) %collective-permute-start.9) | collective-permute-done | bytes 57376 | tf_op jit(solution)/shard_map/ppermute | solution.py:340
  77.3 1.0 %collective-permute-done.10.low3 = f32[2,7,8,128]{3,2,1,0:T(8,128)S(1)} collective-permute-done((f32[2,7,8,128]{3,2,1,0:T(8,128)S(1)}, f32[2,7,8,128]{3,2,1,0:T(8,128)S(1)}, u32[]{:S(2)}, u32[]{:S(2)}) %collective-permute-start.10) | collective-permute-done | bytes 57376 | tf_op jit(solution)/shard_map/ppermute | solution.py:340
  78.3 0.3 gather_low.1
  78.6 0.0 all-to-all-done.1.up_ref
  78.6 1.7 %expand.1 = bf16[896,512]{1,0:T(8,128)(2,1)} custom-call(s32[7]{0:T(128)S(1)} %and_select_fusion.4.row_ref, bf16[7,128,64]{2,1,0:T(8,128)(2,1)S(1)} %get-tuple-element.51.low_ref, f32[896,512]{1,0:T(8,128)S(1)} %get-tuple-element.52.base_ref, bf16[16,64,512]{2,1,0:T(8,128)(2,1)S(1)} %all-to-all-done.1.up_ref), custom_call_target="tpu_custom_call" | custom-call | tf_op jit(solution)/shard_map/expand/pallas_call | solution.py:286
  (9 shorter events, 0.1 us)
Async XLA Ops:
  0.0 1.2 %copy-start.2 = (bf16[1,64,8192]{2,1,0:T(8,128)(2,1)S(1)}, bf16[1,64,8192]{2,1,0:T(8,128)(2,1)}, u32[]{:S(2)}) copy-start(bf16[1,64,8192]{2,1,0:T(8,128)(2,1)} %param.10) | copy-start | bytes 3145732
  1.3 7.5 %collective-permute-start = (bf16[8,8192]{1,0:T(8,128)(2,1)S(1)}, bf16[8,8192]{1,0:T(8,128)(2,1)S(1)}, u32[]{:S(2)}, u32[]{:S(2)}) collective-permute-start(bf16[8,8192]{1,0:T(8,128)(2,1)S(1)} %get-tuple-element.31), channel_id=1, source_target_pairs={{0,4},{1,5},{2,6},{3,7},{4,0},{5,1},{6,2},{7,3},{8,12},{9,13},{10,... | collective-permute-start | bytes 393224 | tf_op jit(solution)/shard_map/ppermute | solution.py:120
  4.5 7.3 %collective-permute-start.1 = (bf16[8,8192]{1,0:T(8,128)(2,1)S(1)}, bf16[8,8192]{1,0:T(8,128)(2,1)S(1)}, u32[]{:S(2)}, u32[]{:S(2)}) collective-permute-start(bf16[8,8192]{1,0:T(8,128)(2,1)S(1)} %get-tuple-element.32), channel_id=1, source_target_pairs={{0,5},{1,4},{2,7},{3,6},{4,1},{5,0},{6,3},{7,2},{8,13},{9,12},{10,... | collective-permute-start | bytes 393224 | tf_op jit(solution)/shard_map/ppermute | solution.py:120
  4.5 9.9 %collective-permute-start.2 = (bf16[8,8192]{1,0:T(8,128)(2,1)S(1)}, bf16[8,8192]{1,0:T(8,128)(2,1)S(1)}, u32[]{:S(2)}, u32[]{:S(2)}) collective-permute-start(bf16[8,8192]{1,0:T(8,128)(2,1)S(1)} %get-tuple-element.33), channel_id=1, source_target_pairs={{0,2},{1,3},{2,4},{3,5},{4,6},{5,7},{6,0},{7,1},{8,10},{9,11},{10,... | collective-permute-start | bytes 393224 | tf_op jit(solution)/shard_map/ppermute | solution.py:120
  5.6 9.1 %collective-permute-start.3 = (bf16[8,8192]{1,0:T(8,128)(2,1)S(1)}, bf16[8,8192]{1,0:T(8,128)(2,1)S(1)}, u32[]{:S(2)}, u32[]{:S(2)}) collective-permute-start(bf16[8,8192]{1,0:T(8,128)(2,1)S(1)} %get-tuple-element.34), channel_id=1, source_target_pairs={{0,6},{1,7},{2,0},{3,1},{4,2},{5,3},{6,4},{7,5},{8,14},{9,15},{10,... | collective-permute-start | bytes 393224 | tf_op jit(solution)/shard_map/ppermute | solution.py:120
  7.7 9.4 %collective-permute-start.4 = (bf16[8,8192]{1,0:T(8,128)(2,1)S(1)}, bf16[8,8192]{1,0:T(8,128)(2,1)S(1)}, u32[]{:S(2)}, u32[]{:S(2)}) collective-permute-start(bf16[8,8192]{1,0:T(8,128)(2,1)S(1)} %get-tuple-element.35), channel_id=1, source_target_pairs={{0,3},{1,2},{2,5},{3,4},{4,7},{5,6},{6,1},{7,0},{8,11},{9,10},{10,... | collective-permute-start | bytes 393224 | tf_op jit(solution)/shard_map/ppermute | solution.py:120
  8.8 8.3 %collective-permute-start.5 = (bf16[8,8192]{1,0:T(8,128)(2,1)S(1)}, bf16[8,8192]{1,0:T(8,128)(2,1)S(1)}, u32[]{:S(2)}, u32[]{:S(2)}) collective-permute-start(bf16[8,8192]{1,0:T(8,128)(2,1)S(1)} %get-tuple-element.36), channel_id=1, source_target_pairs={{0,7},{1,6},{2,1},{3,0},{4,3},{5,2},{6,5},{7,4},{8,15},{9,14},{10,... | collective-permute-start | bytes 393224 | tf_op jit(solution)/shard_map/ppermute | solution.py:120
  11.8 5.3 %collective-permute-start.6 = (bf16[8,8192]{1,0:T(8,128)(2,1)S(1)}, bf16[8,8192]{1,0:T(8,128)(2,1)S(1)}, u32[]{:S(2)}, u32[]{:S(2)}) collective-permute-start(bf16[8,8192]{1,0:T(8,128)(2,1)S(1)} %get-tuple-element.37), channel_id=1, source_target_pairs={{0,1},{1,0},{2,3},{3,2},{4,5},{5,4},{6,7},{7,6},{8,9},{9,8},{10,11... | collective-permute-start | bytes 393224 | tf_op jit(solution)/shard_map/ppermute | solution.py:120
  17.9 1.3 %copy-start = (bf16[16,8,8192]{2,1,0:T(8,128)(2,1)}, bf16[16,8,8192]{2,1,0:T(8,128)(2,1)S(1)}, u32[]{:S(2)}) copy-start(bf16[16,8,8192]{2,1,0:T(8,128)(2,1)S(1)} %pick_down.1) | copy-start | bytes 6291460
  19.2 8.2 %copy-start.3 = (bf16[1,64,4096]{2,1,0:T(8,128)(2,1)S(1)}, bf16[1,64,4096]{2,1,0:T(8,128)(2,1)}, u32[]{:S(2)}) copy-start(bf16[1,64,4096]{2,1,0:T(8,128)(2,1)} %up_ref) | copy-start | bytes 1572868
  19.2 39.3 %all-to-all-start = ((bf16[16,8,8192]{2,1,0:T(8,128)(2,1)}), bf16[16,8,8192]{2,1,0:T(8,128)(2,1)S(1)}, u32[]{:S(2)}, u32[]{:S(2)}) async-start(bf16[16,8,8192]{2,1,0:T(8,128)(2,1)} %copy-done), calls=%async_computation | async-start | bytes 4194304 | tf_op jit(solution)/shard_map/all_to_all | solution.py:328
  27.4 1.6 %collective-permute-start.11 = (bf16[4,64,512]{2,1,0:T(8,128)(2,1)S(1)}, bf16[4,64,512]{2,1,0:T(8,128)(2,1)S(1)}, u32[]{:S(2)}, u32[]{:S(2)}) collective-permute-start(bf16[4,64,512]{2,1,0:T(8,128)(2,1)S(1)} %get-tuple-element.44), channel_id=1, source_target_pairs={{0,1},{1,0},{2,3},{3,2},{4,5},{5,4},{6,7},{7,6},{8,9},{9,8},{10,11... | collective-permute-start | bytes 786440 | tf_op jit(solution)/shard_map/ppermute | solution.py:330
  29.1 22.5 %collective-permute-start.12 = (bf16[2,64,512]{2,1,0:T(8,128)(2,1)S(1)}, bf16[2,64,512]{2,1,0:T(8,128)(2,1)S(1)}, u32[]{:S(2)}, u32[]{:S(2)}) collective-permute-start(bf16[2,64,512]{2,1,0:T(8,128)(2,1)S(1)} %get-tuple-element.46), channel_id=1, source_target_pairs={{0,2},{1,3},{2,4},{3,5},{4,6},{5,7},{6,0},{7,1},{8,10},{9,11},{10,... | collective-permute-start | bytes 393224 | tf_op jit(solution)/shard_map/ppermute | solution.py:332
  30.1 21.5 %collective-permute-start.13 = (bf16[2,64,512]{2,1,0:T(8,128)(2,1)S(1)}, bf16[2,64,512]{2,1,0:T(8,128)(2,1)S(1)}, u32[]{:S(2)}, u32[]{:S(2)}) collective-permute-start(bf16[2,64,512]{2,1,0:T(8,128)(2,1)S(1)} %get-tuple-element.47), channel_id=1, source_target_pairs={{0,4},{1,5},{2,6},{3,7},{4,0},{5,1},{6,2},{7,3},{8,12},{9,13},{10,... | collective-permute-start | bytes 393224 | tf_op jit(solution)/shard_map/ppermute | solution.py:332
  32.8 18.8 %collective-permute-start.14 = (bf16[2,64,512]{2,1,0:T(8,128)(2,1)S(1)}, bf16[2,64,512]{2,1,0:T(8,128)(2,1)S(1)}, u32[]{:S(2)}, u32[]{:S(2)}) collective-permute-start(bf16[2,64,512]{2,1,0:T(8,128)(2,1)S(1)} %get-tuple-element.48), channel_id=1, source_target_pairs={{0,6},{1,7},{2,0},{3,1},{4,2},{5,3},{6,4},{7,5},{8,14},{9,15},{10,... | collective-permute-start | bytes 393224 | tf_op jit(solution)/shard_map/ppermute | solution.py:332
  58.4 20.2 %all-to-all-start.1 = ((bf16[16,64,512]{2,1,0:T(8,128)(2,1)}), bf16[16,64,512]{2,1,0:T(8,128)(2,1)S(1)}, u32[]{:S(2)}, u32[]{:S(2)}) async-start(bf16[16,64,512]{2,1,0:T(8,128)(2,1)} %pick_up.1), calls=%async_computation.1 | async-start | bytes 2097152 | tf_op jit(solution)/shard_map/all_to_all | solution.py:335
  62.3 16.0 %copy-start.1 = (f32[896,512]{1,0:T(8,128)S(1)}, f32[896,512]{1,0:T(8,128)}, u32[]{:S(2)}) copy-start(f32[896,512]{1,0:T(8,128)} %get-tuple-element.50.base_hbm) | copy-start | bytes 5505028
  69.1 1.3 %collective-permute-start.7 = (f32[7,8,128]{2,1,0:T(8,128)S(1)}, f32[7,8,128]{2,1,0:T(8,128)S(1)}, u32[]{:S(2)}, u32[]{:S(2)}) collective-permute-start(f32[7,8,128]{2,1,0:T(8,128)S(1)} %shrink.1), channel_id=1, source_target_pairs={{0,1},{1,0},{2,3},{3,2},{4,5},{5,4},{6,7},{7,6},{8,9},{9,8},{10,11... | collective-permute-start | bytes 86024 | tf_op jit(solution)/shard_map/ppermute | solution.py:338
  70.4 5.9 %collective-permute-start.8 = (f32[2,7,8,128]{3,2,1,0:T(8,128)S(1)}, f32[2,7,8,128]{3,2,1,0:T(8,128)S(1)}, u32[]{:S(2)}, u32[]{:S(2)}) collective-permute-start(f32[2,7,8,128]{3,2,1,0:T(8,128)S(1)} %pad_maximum_fusion.low0), channel_id=1, source_target_pairs={{0,2},{1,3},{2,4},{3,5},{4,6},{5,7},{6,0},{7,1},{8,10},{9,11},{10,... | collective-permute-start | bytes 172040 | tf_op jit(solution)/shard_map/ppermute | solution.py:340
  71.4 5.9 %collective-permute-start.9 = (f32[2,7,8,128]{3,2,1,0:T(8,128)S(1)}, f32[2,7,8,128]{3,2,1,0:T(8,128)S(1)}, u32[]{:S(2)}, u32[]{:S(2)}) collective-permute-start(f32[2,7,8,128]{3,2,1,0:T(8,128)S(1)} %pad_maximum_fusion.low0), channel_id=1, source_target_pairs={{0,4},{1,5},{2,6},{3,7},{4,0},{5,1},{6,2},{7,3},{8,12},{9,13},{10,... | collective-permute-start | bytes 172040 | tf_op jit(solution)/shard_map/ppermute | solution.py:340
  74.1 4.2 %collective-permute-start.10 = (f32[2,7,8,128]{3,2,1,0:T(8,128)S(1)}, f32[2,7,8,128]{3,2,1,0:T(8,128)S(1)}, u32[]{:S(2)}, u32[]{:S(2)}) collective-permute-start(f32[2,7,8,128]{3,2,1,0:T(8,128)S(1)} %pad_maximum_fusion.low0), channel_id=1, source_target_pairs={{0,6},{1,7},{2,0},{3,1},{4,2},{5,3},{6,4},{7,5},{8,14},{9,15},{10,... | collective-permute-start | bytes 172040 | tf_op jit(solution)/shard_map/ppermute | solution.py:340

commit v7 on v6

--- a/solution.py
+++ b/solution.py
@@ -235,7 +235,7 @@
     )(owner_rows, down_got, normed)
 
 
-def gather_kernel(lane_ref, low0, low1, low2, low3, base_hbm, low_ref, base_ref, full, sem):
+def gather_kernel(lane_ref, low2, low1, low3, low0, base_hbm, low_ref, base_ref, full, sem):
     copy = pltpu.make_async_copy(base_hbm, base_ref, sem)
     copy.start()
     lows = (low0, low1, low2, low3)
@@ -266,7 +266,7 @@
         scratch_shapes=[pltpu.VMEM(shape, jnp.float32), pltpu.SemaphoreType.DMA],
         compiler_params=pltpu.CompilerParams(vmem_limit_bytes=16 * 2**20),
         name="gather_low",
-    )(lane, *lows, base)
+    )(lane, lows[2], lows[1], lows[3], lows[0], base)
 
 
 def expand_kernel(row_ref, low_ref, base_ref, up_ref, out_hbm, out_ref, sems):
@@ -337,7 +337,8 @@
     low = shrink(owner_rows, down_got, normed)
     other = lax.ppermute(low, BOTH, lane_shift(groups, 0, 1))
     chip = jnp.stack([low, other])
-    lows = [chip] + [lax.ppermute(chip, BOTH, lane_shift(groups, dx, 0)) for dx in range(1, X)]
+    far, right, left = [lax.ppermute(chip, BOTH, lane_shift(groups, dx, 0)) for dx in (2, 1, 3)]
+    lows = [chip, right, far, left]
     low, base = gather_low(lane_arr, lows, base)
     return expand(owner_rows, low, base, up_got)
 

time: 80.8 us -> 81.4 us (level)
  transfers between devices with their start and end apart: 17 -> 17, of which waited for: 9 -> 8; matrix products, arithmetic and copies ran while one was open for 2% -> 2% of each run, Pallas kernels for 33% -> 33%
where the time goes in v7:
time: 81.4 us; the launch traced here: 80.4 us
  starting transfers between devices  32.6 us (40%)
  Pallas kernels  28.6 us (35%)
  waiting for transfers between devices  15.2 us (19%)
  local copies, waits for them, and re-layouts  2.71 us (3%)
  other arithmetic  1.05 us (1%)
    pallas_call x1, Pallas kernels, norm_base(): pl.pallas_call(norm_base_kernel, grid=(rows // NORM_ROWS,), in_specs=[pl....  17.3 us
    ppermute x7, starting transfers between devices, spread(): lax.ppermute(pieces[k], BOTH, lane_shift(groups, k // CORES, k % CORES))  9.58 us
    all_to_all x1, starting transfers between devices, shards(): down_got = lax.all_to_all(down_send, 'req', 0, 0, tiled=True)  8.19 us
    pallas_call x1, Pallas kernels, shrink(): pl.pallas_call(shrink_kernel, in_specs=[SMEM, VMEM, ANY], out_specs=VMEM,...  6.83 us
    ppermute x3, starting transfers between devices, shards(): lax.ppermute(chip, BOTH, lane_shift(groups, dx, 0))  5.76 us
    ppermute x3, starting transfers between devices, shards(): lax.ppermute(pairs[dx], BOTH, lane_shift(groups, dx, 0))  5.25 us
    all_to_all x1, waiting for transfers between devices, shards(): down_got = lax.all_to_all(down_send, 'req', 0, 0, tiled=True)  5.17 us
    ppermute x7, waiting for transfers between devices, spread(): lax.ppermute(pieces[k], BOTH, lane_shift(groups, k // CORES, k % CORES))  5.15 us
  transfers between devices with their start and end apart: 17, of which 8 were waited for; matrix products, arithmetic and copies ran while one was open for 2% of the time, Pallas kernels for 33%

profile of v7, /device:TPU:0, one launch (start us, length us, event | category | flops | bytes accessed | tf_op | source)
XLA Modules:
  0.0 80.4 jit_solution(8452503330996066495)
XLA Ops:
  0.0 1.2 %copy-done.2 = bf16[1,64,8192]{2,1,0:T(8,128)(2,1)S(1)} copy-done((bf16[1,64,8192]{2,1,0:T(8,128)(2,1)S(1)}, bf16[1,64,8192]{2,1,0:T(8,128)(2,1)}, u32[]{:S(2)}) %copy-start.2) | copy-done | bytes 1048600
  1.2 0.1 split_down.1
  1.3 3.2 %collective-permute-start = (bf16[8,8192]{1,0:T(8,128)(2,1)S(1)}, bf16[8,8192]{1,0:T(8,128)(2,1)S(1)}, u32[]{:S(2)}, u32[]{:S(2)}) collective-permute-start(bf16[8,8192]{1,0:T(8,128)(2,1)S(1)} %get-tuple-element.31), channel_id=1, source_target_pairs={{0,4},{1,5},{2,6},{3,7},{4,0},{5,1},{6,2},{7,3},{8,12},{9,13},{10,... | collective-permute-start | bytes 393224 | tf_op jit(solution)/shard_map/ppermute | solution.py:120
  4.5 0.0 collective-permute-start.1
  4.5 1.2 %collective-permute-start.2 = (bf16[8,8192]{1,0:T(8,128)(2,1)S(1)}, bf16[8,8192]{1,0:T(8,128)(2,1)S(1)}, u32[]{:S(2)}, u32[]{:S(2)}) collective-permute-start(bf16[8,8192]{1,0:T(8,128)(2,1)S(1)} %get-tuple-element.33), channel_id=1, source_target_pairs={{0,2},{1,3},{2,4},{3,5},{4,6},{5,7},{6,0},{7,1},{8,10},{9,11},{10,... | collective-permute-start | bytes 393224 | tf_op jit(solution)/shard_map/ppermute | solution.py:120
  5.6 2.1 %collective-permute-start.3 = (bf16[8,8192]{1,0:T(8,128)(2,1)S(1)}, bf16[8,8192]{1,0:T(8,128)(2,1)S(1)}, u32[]{:S(2)}, u32[]{:S(2)}) collective-permute-start(bf16[8,8192]{1,0:T(8,128)(2,1)S(1)} %get-tuple-element.34), channel_id=1, source_target_pairs={{0,6},{1,7},{2,0},{3,1},{4,2},{5,3},{6,4},{7,5},{8,14},{9,15},{10,... | collective-permute-start | bytes 393224 | tf_op jit(solution)/shard_map/ppermute | solution.py:120
  7.7 0.0 collective-permute-start.4
  7.7 1.0 %select_reduce_fusion = s32[16,7]{0,1:T(8,128)S(1)} fusion(s32[128]{0:T(128)} %param.13, s32[16,7]{0,1:T(8,128)} %param.12), kind=kLoop, calls=%fused_computation.1 | loop fusion | flops 42896 | bytes 1408 | tf_op jit(solution)/shard_map/reduce_sum | solution.py:320
  8.8 0.0 collective-permute-done.rest_0_
  8.8 3.0 %collective-permute-start.5 = (bf16[8,8192]{1,0:T(8,128)(2,1)S(1)}, bf16[8,8192]{1,0:T(8,128)(2,1)S(1)}, u32[]{:S(2)}, u32[]{:S(2)}) collective-permute-start(bf16[8,8192]{1,0:T(8,128)(2,1)S(1)} %get-tuple-element.36), channel_id=1, source_target_pairs={{0,7},{1,6},{2,1},{3,0},{4,3},{5,2},{6,5},{7,4},{8,15},{9,14},{10,... | collective-permute-start | bytes 393224 | tf_op jit(solution)/shard_map/ppermute | solution.py:120
  11.8 0.0 collective-permute-done.1.rest_1_
  11.8 0.1 collective-permute-start.6
  12.0 2.4 %collective-permute-done.2.rest_2_ = bf16[8,8192]{1,0:T(8,128)(2,1)S(1)} collective-permute-done((bf16[8,8192]{1,0:T(8,128)(2,1)S(1)}, bf16[8,8192]{1,0:T(8,128)(2,1)S(1)}, u32[]{:S(2)}, u32[]{:S(2)}) %collective-permute-start.2) | collective-permute-done | bytes 131104 | tf_op jit(solution)/shard_map/ppermute | solution.py:120
  14.4 0.4 collective-permute-done.3.rest_3_
  14.8 2.3 %collective-permute-done.4.rest_4_ = bf16[8,8192]{1,0:T(8,128)(2,1)S(1)} collective-permute-done((bf16[8,8192]{1,0:T(8,128)(2,1)S(1)}, bf16[8,8192]{1,0:T(8,128)(2,1)S(1)}, u32[]{:S(2)}, u32[]{:S(2)}) %collective-permute-start.4) | collective-permute-done | bytes 131104 | tf_op jit(solution)/shard_map/ppermute | solution.py:120
  17.1 0.0 collective-permute-done.5.rest_5_
  17.1 0.0 collective-permute-done.6.rest_6_
  17.1 0.7 pick_down.1
  17.9 0.0 copy-start
  17.9 1.3 %copy-done = bf16[16,8,8192]{2,1,0:T(8,128)(2,1)} copy-done((bf16[16,8,8192]{2,1,0:T(8,128)(2,1)}, bf16[16,8,8192]{2,1,0:T(8,128)(2,1)S(1)}, u32[]{:S(2)}) %copy-start) | copy-done | bytes 2097176
  19.2 8.2 %all-to-all-start = ((bf16[16,8,8192]{2,1,0:T(8,128)(2,1)}), bf16[16,8,8192]{2,1,0:T(8,128)(2,1)S(1)}, u32[]{:S(2)}, u32[]{:S(2)}) async-start(bf16[16,8,8192]{2,1,0:T(8,128)(2,1)} %copy-done), calls=%async_computation | async-start | bytes 4194304 | tf_op jit(solution)/shard_map/all_to_all | solution.py:328
  27.4 0.0 copy-done.3
  27.4 0.1 split_up.1
  27.4 0.1 collective-permute-start.11
  27.5 1.5 %collective-permute-done.11.cross_ref = bf16[4,64,512]{2,1,0:T(8,128)(2,1)S(1)} collective-permute-done((bf16[4,64,512]{2,1,0:T(8,128)(2,1)S(1)}, bf16[4,64,512]{2,1,0:T(8,128)(2,1)S(1)}, u32[]{:S(2)}, u32[]{:S(2)}) %collective-permute-start.11) | collective-permute-done | bytes 262176 | tf_op jit(solution)/shard_map/ppermute | solution.py:330
  29.1 1.1 %collective-permute-start.12 = (bf16[2,64,512]{2,1,0:T(8,128)(2,1)S(1)}, bf16[2,64,512]{2,1,0:T(8,128)(2,1)S(1)}, u32[]{:S(2)}, u32[]{:S(2)}) collective-permute-start(bf16[2,64,512]{2,1,0:T(8,128)(2,1)S(1)} %get-tuple-element.46), channel_id=1, source_target_pairs={{0,2},{1,3},{2,4},{3,5},{4,6},{5,7},{6,0},{7,1},{8,10},{9,11},{10,... | collective-permute-start | bytes 393224 | tf_op jit(solution)/shard_map/ppermute | solution.py:332
  30.1 2.7 %collective-permute-start.13 = (bf16[2,64,512]{2,1,0:T(8,128)(2,1)S(1)}, bf16[2,64,512]{2,1,0:T(8,128)(2,1)S(1)}, u32[]{:S(2)}, u32[]{:S(2)}) collective-permute-start(bf16[2,64,512]{2,1,0:T(8,128)(2,1)S(1)} %get-tuple-element.47), channel_id=1, source_target_pairs={{0,4},{1,5},{2,6},{3,7},{4,0},{5,1},{6,2},{7,3},{8,12},{9,13},{10,... | collective-permute-start | bytes 393224 | tf_op jit(solution)/shard_map/ppermute | solution.py:332
  32.8 1.5 %collective-permute-start.14 = (bf16[2,64,512]{2,1,0:T(8,128)(2,1)S(1)}, bf16[2,64,512]{2,1,0:T(8,128)(2,1)S(1)}, u32[]{:S(2)}, u32[]{:S(2)}) collective-permute-start(bf16[2,64,512]{2,1,0:T(8,128)(2,1)S(1)} %get-tuple-element.48), channel_id=1, source_target_pairs={{0,6},{1,7},{2,0},{3,1},{4,2},{5,3},{6,4},{7,5},{8,14},{9,15},{10,... | collective-permute-start | bytes 393224 | tf_op jit(solution)/shard_map/ppermute | solution.py:332
  34.3 17.3 %norm_base.1 = (bf16[896,8192]{1,0:T(8,128)(2,1)}, f32[896,512]{1,0:T(8,128)}) custom-call(bf16[896,8192]{1,0:T(8,128)(2,1)} %x_ref, f32[1,8192]{1,0:T(1,128)} %bitcast.8, bf16[8192,512]{1,0:T(8,128)(2,1)} %weight_ref.1), custom_call_target="tpu_custom_call" | custom-call | flops 15032385536 | bytes 37748736 | tf_op jit(solution)/shard_map/norm_base/pallas_call | solution.py:171
  51.6 0.0 collective-permute-done.12.rest_1_
  51.6 0.0 collective-permute-done.13.rest_2_
  51.6 0.0 collective-permute-done.14.rest_3_
  51.6 1.6 %pick_up.1 = bf16[16,64,512]{2,1,0:T(8,128)(2,1)} custom-call(s32[16]{0:T(128)S(1)} %fusion.5.pick_ref, bf16[2,64,512]{2,1,0:T(8,128)(2,1)S(1)} %get-tuple-element.53.rest_0_, bf16[2,64,512]{2,1,0:T(8,128)(2,1)S(1)} %collective-permute-done.12.rest_1_, bf16[2,64,512]{2,1,0:T(8,128)(2,1)S(1)} %collective-permute-done.13.rest_2_, ...), custom_call_target="tpu_custom_call" | custom-call | tf_op jit(solution)/shard_map/pick_up/pallas_call | solution.py:96
  53.3 5.2 %all-to-all-done.down_ref = bf16[16,8,8192]{2,1,0:T(8,128)(2,1)S(1)} async-done(((bf16[16,8,8192]{2,1,0:T(8,128)(2,1)}), bf16[16,8,8192]{2,1,0:T(8,128)(2,1)S(1)}, u32[]{:S(2)}, u32[]{:S(2)}) %all-to-all-start) | async-done | bytes 2097184 | tf_op jit(solution)/shard_map/all_to_all | solution.py:328
  58.4 3.7 %all-to-all-start.1 = ((bf16[16,64,512]{2,1,0:T(8,128)(2,1)}), bf16[16,64,512]{2,1,0:T(8,128)(2,1)S(1)}, u32[]{:S(2)}, u32[]{:S(2)}) async-start(bf16[16,64,512]{2,1,0:T(8,128)(2,1)} %pick_up.1), calls=%async_computation.1 | async-start | bytes 2097152 | tf_op jit(solution)/shard_map/all_to_all | solution.py:335
  62.1 0.2 dynamic-slice_reduce_fusion
  62.3 6.8 %shrink.1 = f32[7,8,128]{2,1,0:T(8,128)S(1)} custom-call(s32[7]{0:T(128)S(1)} %and_select_fusion.4.row_ref, bf16[16,8,8192]{2,1,0:T(8,128)(2,1)S(1)} %all-to-all-done.down_ref, bf16[896,8192]{1,0:T(8,128)(2,1)} %get-tuple-element.41.normed_hbm), custom_call_target="tpu_custom_call" | custom-call | flops 3758096384 | bytes 14680064 | tf_op jit(solution)/shard_map/shrink/pallas_call | solution.py:224
  69.1 0.1 collective-permute-start.7
  69.2 1.2 %collective-permute-done.7 = f32[7,8,128]{2,1,0:T(8,128)S(1)} collective-permute-done((f32[7,8,128]{2,1,0:T(8,128)S(1)}, f32[7,8,128]{2,1,0:T(8,128)S(1)}, u32[]{:S(2)}, u32[]{:S(2)}) %collective-permute-start.7) | collective-permute-done | bytes 28704 | tf_op jit(solution)/shard_map/ppermute | solution.py:338
  70.4 2.5 %collective-permute-start.8 = (f32[2,7,8,128]{3,2,1,0:T(8,128)S(1)}, f32[2,7,8,128]{3,2,1,0:T(8,128)S(1)}, u32[]{:S(2)}, u32[]{:S(2)}) collective-permute-start(f32[2,7,8,128]{3,2,1,0:T(8,128)S(1)} %pad_maximum_fusion.low0), channel_id=1, source_target_pairs={{0,4},{1,5},{2,6},{3,7},{4,0},{5,1},{6,2},{7,3},{8,12},{9,13},{10,... | collective-permute-start | bytes 172040 | tf_op jit(solution)/shard_map/ppermute | solution.py:340
  72.9 0.6 collective-permute-start.9
  73.5 2.7 %collective-permute-start.10 = (f32[2,7,8,128]{3,2,1,0:T(8,128)S(1)}, f32[2,7,8,128]{3,2,1,0:T(8,128)S(1)}, u32[]{:S(2)}, u32[]{:S(2)}) collective-permute-start(f32[2,7,8,128]{3,2,1,0:T(8,128)S(1)} %pad_maximum_fusion.low0), channel_id=1, source_target_pairs={{0,6},{1,7},{2,0},{3,1},{4,2},{5,3},{6,4},{7,5},{8,14},{9,15},{10,... | collective-permute-start | bytes 172040 | tf_op jit(solution)/shard_map/ppermute | solution.py:340
  76.2 0.1 collective-permute-done.8.low2
  76.3 2.1 %collective-permute-done.9.low1 = f32[2,7,8,128]{3,2,1,0:T(8,128)S(1)} collective-permute-done((f32[2,7,8,128]{3,2,1,0:T(8,128)S(1)}, f32[2,7,8,128]{3,2,1,0:T(8,128)S(1)}, u32[]{:S(2)}, u32[]{:S(2)}) %collective-permute-start.9) | collective-permute-done | bytes 57376 | tf_op jit(solution)/shard_map/ppermute | solution.py:340
  78.3 0.0 collective-permute-done.10.low3
  78.3 0.3 gather_low.1
  78.7 0.0 all-to-all-done.1.up_ref
  78.7 1.7 %expand.1 = bf16[896,512]{1,0:T(8,128)(2,1)} custom-call(s32[7]{0:T(128)S(1)} %and_select_fusion.4.row_ref, bf16[7,128,64]{2,1,0:T(8,128)(2,1)S(1)} %get-tuple-element.51.low_ref, f32[896,512]{1,0:T(8,128)S(1)} %get-tuple-element.52.base_ref, bf16[16,64,512]{2,1,0:T(8,128)(2,1)S(1)} %all-to-all-done.1.up_ref), custom_call_target="tpu_custom_call" | custom-call | tf_op jit(solution)/shard_map/expand/pallas_call | solution.py:286
  (9 shorter events, 0.1 us)
Async XLA Ops:
  0.0 1.2 %copy-start.2 = (bf16[1,64,8192]{2,1,0:T(8,128)(2,1)S(1)}, bf16[1,64,8192]{2,1,0:T(8,128)(2,1)}, u32[]{:S(2)}) copy-start(bf16[1,64,8192]{2,1,0:T(8,128)(2,1)} %param.10) | copy-start | bytes 3145732
  1.3 7.5 %collective-permute-start = (bf16[8,8192]{1,0:T(8,128)(2,1)S(1)}, bf16[8,8192]{1,0:T(8,128)(2,1)S(1)}, u32[]{:S(2)}, u32[]{:S(2)}) collective-permute-start(bf16[8,8192]{1,0:T(8,128)(2,1)S(1)} %get-tuple-element.31), channel_id=1, source_target_pairs={{0,4},{1,5},{2,6},{3,7},{4,0},{5,1},{6,2},{7,3},{8,12},{9,13},{10,... | collective-permute-start | bytes 393224 | tf_op jit(solution)/shard_map/ppermute | solution.py:120
  4.5 7.3 %collective-permute-start.1 = (bf16[8,8192]{1,0:T(8,128)(2,1)S(1)}, bf16[8,8192]{1,0:T(8,128)(2,1)S(1)}, u32[]{:S(2)}, u32[]{:S(2)}) collective-permute-start(bf16[8,8192]{1,0:T(8,128)(2,1)S(1)} %get-tuple-element.32), channel_id=1, source_target_pairs={{0,5},{1,4},{2,7},{3,6},{4,1},{5,0},{6,3},{7,2},{8,13},{9,12},{10,... | collective-permute-start | bytes 393224 | tf_op jit(solution)/shard_map/ppermute | solution.py:120
  4.5 9.9 %collective-permute-start.2 = (bf16[8,8192]{1,0:T(8,128)(2,1)S(1)}, bf16[8,8192]{1,0:T(8,128)(2,1)S(1)}, u32[]{:S(2)}, u32[]{:S(2)}) collective-permute-start(bf16[8,8192]{1,0:T(8,128)(2,1)S(1)} %get-tuple-element.33), channel_id=1, source_target_pairs={{0,2},{1,3},{2,4},{3,5},{4,6},{5,7},{6,0},{7,1},{8,10},{9,11},{10,... | collective-permute-start | bytes 393224 | tf_op jit(solution)/shard_map/ppermute | solution.py:120
  5.6 9.1 %collective-permute-start.3 = (bf16[8,8192]{1,0:T(8,128)(2,1)S(1)}, bf16[8,8192]{1,0:T(8,128)(2,1)S(1)}, u32[]{:S(2)}, u32[]{:S(2)}) collective-permute-start(bf16[8,8192]{1,0:T(8,128)(2,1)S(1)} %get-tuple-element.34), channel_id=1, source_target_pairs={{0,6},{1,7},{2,0},{3,1},{4,2},{5,3},{6,4},{7,5},{8,14},{9,15},{10,... | collective-permute-start | bytes 393224 | tf_op jit(solution)/shard_map/ppermute | solution.py:120
  7.7 9.4 %collective-permute-start.4 = (bf16[8,8192]{1,0:T(8,128)(2,1)S(1)}, bf16[8,8192]{1,0:T(8,128)(2,1)S(1)}, u32[]{:S(2)}, u32[]{:S(2)}) collective-permute-start(bf16[8,8192]{1,0:T(8,128)(2,1)S(1)} %get-tuple-element.35), channel_id=1, source_target_pairs={{0,3},{1,2},{2,5},{3,4},{4,7},{5,6},{6,1},{7,0},{8,11},{9,10},{10,... | collective-permute-start | bytes 393224 | tf_op jit(solution)/shard_map/ppermute | solution.py:120
  8.8 8.3 %collective-permute-start.5 = (bf16[8,8192]{1,0:T(8,128)(2,1)S(1)}, bf16[8,8192]{1,0:T(8,128)(2,1)S(1)}, u32[]{:S(2)}, u32[]{:S(2)}) collective-permute-start(bf16[8,8192]{1,0:T(8,128)(2,1)S(1)} %get-tuple-element.36), channel_id=1, source_target_pairs={{0,7},{1,6},{2,1},{3,0},{4,3},{5,2},{6,5},{7,4},{8,15},{9,14},{10,... | collective-permute-start | bytes 393224 | tf_op jit(solution)/shard_map/ppermute | solution.py:120
  11.8 5.3 %collective-permute-start.6 = (bf16[8,8192]{1,0:T(8,128)(2,1)S(1)}, bf16[8,8192]{1,0:T(8,128)(2,1)S(1)}, u32[]{:S(2)}, u32[]{:S(2)}) collective-permute-start(bf16[8,8192]{1,0:T(8,128)(2,1)S(1)} %get-tuple-element.37), channel_id=1, source_target_pairs={{0,1},{1,0},{2,3},{3,2},{4,5},{5,4},{6,7},{7,6},{8,9},{9,8},{10,11... | collective-permute-start | bytes 393224 | tf_op jit(solution)/shard_map/ppermute | solution.py:120
  17.9 1.3 %copy-start = (bf16[16,8,8192]{2,1,0:T(8,128)(2,1)}, bf16[16,8,8192]{2,1,0:T(8,128)(2,1)S(1)}, u32[]{:S(2)}) copy-start(bf16[16,8,8192]{2,1,0:T(8,128)(2,1)S(1)} %pick_down.1) | copy-start | bytes 6291460
  19.2 8.2 %copy-start.3 = (bf16[1,64,4096]{2,1,0:T(8,128)(2,1)S(1)}, bf16[1,64,4096]{2,1,0:T(8,128)(2,1)}, u32[]{:S(2)}) copy-start(bf16[1,64,4096]{2,1,0:T(8,128)(2,1)} %up_ref) | copy-start | bytes 1572868
  19.2 39.3 %all-to-all-start = ((bf16[16,8,8192]{2,1,0:T(8,128)(2,1)}), bf16[16,8,8192]{2,1,0:T(8,128)(2,1)S(1)}, u32[]{:S(2)}, u32[]{:S(2)}) async-start(bf16[16,8,8192]{2,1,0:T(8,128)(2,1)} %copy-done), calls=%async_computation | async-start | bytes 4194304 | tf_op jit(solution)/shard_map/all_to_all | solution.py:328
  27.4 1.6 %collective-permute-start.11 = (bf16[4,64,512]{2,1,0:T(8,128)(2,1)S(1)}, bf16[4,64,512]{2,1,0:T(8,128)(2,1)S(1)}, u32[]{:S(2)}, u32[]{:S(2)}) collective-permute-start(bf16[4,64,512]{2,1,0:T(8,128)(2,1)S(1)} %get-tuple-element.44), channel_id=1, source_target_pairs={{0,1},{1,0},{2,3},{3,2},{4,5},{5,4},{6,7},{7,6},{8,9},{9,8},{10,11... | collective-permute-start | bytes 786440 | tf_op jit(solution)/shard_map/ppermute | solution.py:330
  29.1 22.5 %collective-permute-start.12 = (bf16[2,64,512]{2,1,0:T(8,128)(2,1)S(1)}, bf16[2,64,512]{2,1,0:T(8,128)(2,1)S(1)}, u32[]{:S(2)}, u32[]{:S(2)}) collective-permute-start(bf16[2,64,512]{2,1,0:T(8,128)(2,1)S(1)} %get-tuple-element.46), channel_id=1, source_target_pairs={{0,2},{1,3},{2,4},{3,5},{4,6},{5,7},{6,0},{7,1},{8,10},{9,11},{10,... | collective-permute-start | bytes 393224 | tf_op jit(solution)/shard_map/ppermute | solution.py:332
  30.1 21.5 %collective-permute-start.13 = (bf16[2,64,512]{2,1,0:T(8,128)(2,1)S(1)}, bf16[2,64,512]{2,1,0:T(8,128)(2,1)S(1)}, u32[]{:S(2)}, u32[]{:S(2)}) collective-permute-start(bf16[2,64,512]{2,1,0:T(8,128)(2,1)S(1)} %get-tuple-element.47), channel_id=1, source_target_pairs={{0,4},{1,5},{2,6},{3,7},{4,0},{5,1},{6,2},{7,3},{8,12},{9,13},{10,... | collective-permute-start | bytes 393224 | tf_op jit(solution)/shard_map/ppermute | solution.py:332
  32.8 18.8 %collective-permute-start.14 = (bf16[2,64,512]{2,1,0:T(8,128)(2,1)S(1)}, bf16[2,64,512]{2,1,0:T(8,128)(2,1)S(1)}, u32[]{:S(2)}, u32[]{:S(2)}) collective-permute-start(bf16[2,64,512]{2,1,0:T(8,128)(2,1)S(1)} %get-tuple-element.48), channel_id=1, source_target_pairs={{0,6},{1,7},{2,0},{3,1},{4,2},{5,3},{6,4},{7,5},{8,14},{9,15},{10,... | collective-permute-start | bytes 393224 | tf_op jit(solution)/shard_map/ppermute | solution.py:332
  58.4 20.2 %all-to-all-start.1 = ((bf16[16,64,512]{2,1,0:T(8,128)(2,1)}), bf16[16,64,512]{2,1,0:T(8,128)(2,1)S(1)}, u32[]{:S(2)}, u32[]{:S(2)}) async-start(bf16[16,64,512]{2,1,0:T(8,128)(2,1)} %pick_up.1), calls=%async_computation.1 | async-start | bytes 2097152 | tf_op jit(solution)/shard_map/all_to_all | solution.py:335
  62.3 16.0 %copy-start.1 = (f32[896,512]{1,0:T(8,128)S(1)}, f32[896,512]{1,0:T(8,128)}, u32[]{:S(2)}) copy-start(f32[896,512]{1,0:T(8,128)} %get-tuple-element.50.base_hbm) | copy-start | bytes 5505028
  69.1 1.3 %collective-permute-start.7 = (f32[7,8,128]{2,1,0:T(8,128)S(1)}, f32[7,8,128]{2,1,0:T(8,128)S(1)}, u32[]{:S(2)}, u32[]{:S(2)}) collective-permute-start(f32[7,8,128]{2,1,0:T(8,128)S(1)} %shrink.1), channel_id=1, source_target_pairs={{0,1},{1,0},{2,3},{3,2},{4,5},{5,4},{6,7},{7,6},{8,9},{9,8},{10,11... | collective-permute-start | bytes 86024 | tf_op jit(solution)/shard_map/ppermute | solution.py:338
  70.4 5.8 %collective-permute-start.8 = (f32[2,7,8,128]{3,2,1,0:T(8,128)S(1)}, f32[2,7,8,128]{3,2,1,0:T(8,128)S(1)}, u32[]{:S(2)}, u32[]{:S(2)}) collective-permute-start(f32[2,7,8,128]{3,2,1,0:T(8,128)S(1)} %pad_maximum_fusion.low0), channel_id=1, source_target_pairs={{0,4},{1,5},{2,6},{3,7},{4,0},{5,1},{6,2},{7,3},{8,12},{9,13},{10,... | collective-permute-start | bytes 172040 | tf_op jit(solution)/shard_map/ppermute | solution.py:340
  72.9 5.4 %collective-permute-start.9 = (f32[2,7,8,128]{3,2,1,0:T(8,128)S(1)}, f32[2,7,8,128]{3,2,1,0:T(8,128)S(1)}, u32[]{:S(2)}, u32[]{:S(2)}) collective-permute-start(f32[2,7,8,128]{3,2,1,0:T(8,128)S(1)} %pad_maximum_fusion.low0), channel_id=1, source_target_pairs={{0,2},{1,3},{2,4},{3,5},{4,6},{5,7},{6,0},{7,1},{8,10},{9,11},{10,... | collective-permute-start | bytes 172040 | tf_op jit(solution)/shard_map/ppermute | solution.py:340
  73.5 4.8 %collective-permute-start.10 = (f32[2,7,8,128]{3,2,1,0:T(8,128)S(1)}, f32[2,7,8,128]{3,2,1,0:T(8,128)S(1)}, u32[]{:S(2)}, u32[]{:S(2)}) collective-permute-start(f32[2,7,8,128]{3,2,1,0:T(8,128)S(1)} %pad_maximum_fusion.low0), channel_id=1, source_target_pairs={{0,6},{1,7},{2,0},{3,1},{4,2},{5,3},{6,4},{7,5},{8,14},{9,15},{10,... | collective-permute-start | bytes 172040 | tf_op jit(solution)/shard_map/ppermute | solution.py:340
